TPU v7x, 32 devices: a whole 2x2x4 slice. The times are simulated.
32 devices in a mesh: row: 8 (over y, x, core), col: 4 (over z).
Axes of the slice: x: 2, y: 2, z: 4, core: 2. Of those that a mesh axis runs over, the one named last changes fastest.
Arguments:
- covariance: float32 [3, 8, 6, 4, 128, 128], P(None, 'row', None, 'col'), may hold values from -2 to 2, as said below
- tile_mask: int32 [24, 24], replicated, may hold values from 0 to 1, as said below
Outputs:
- updated: bfloat16 [3, 8, 6, 4, 128, 128], P(None, 'row', None, 'col')
Inputs may be any that keep to these rules, and one draw needn't show every extreme that they name: `covariance`: symmetric; the masked leading block of order 512 is positive definite. `tile_mask`: symmetric; tiles on the diagonal and next to it, and tiles whose row and column both lie among the first 4 tile rows, are all ones.
All inputs are finite; a program needn't handle non-finite values.
Results may differ from a plain program's by a relative error of at most 0.001.
Values sent between devices are 32-bit elements; how exact they have to be, the bound alone decides.
No kernel may reach another device: no remote copies, remote signals or barrier semaphores. Data moves between devices by JAX's collectives and lax.ppermute only.
A program may use at most 64 MiB of HBM per device.

v0:
```python
import jax
import jax.numpy as jnp
from jax import lax
from jax.sharding import PartitionSpec as P

TPP = 2
PANELS = 2


def spread(value, axis, source):
    kept = jnp.where(lax.axis_index(axis) == source, value, 0).astype(value.dtype)
    return lax.psum(kept, axis)


def panel_step(current, rows_idx, cols_idx, first_tile, tile_count):
    tile_rows, tile_cols, tile_size, _ = current.shape
    width = tile_count * tile_size
    row_devices = lax.axis_size("row")
    col_devices = lax.axis_size("col")
    my_col = lax.axis_index("col")
    received = []
    for offset in range(tile_count):
        received.append(spread(current[:, 0], "col", first_tile + offset))
    panel_raw = jnp.concatenate(received, axis=2)
    diag_pieces = []
    for offset in range(tile_count):
        target = first_tile + offset
        diag_pieces.append(spread(panel_raw[target // row_devices], "row", target % row_devices))
    diag_block = jnp.concatenate(diag_pieces, axis=0)
    cholesky_factor = jnp.linalg.cholesky(diag_block)
    flattened = panel_raw.reshape(tile_rows * tile_size, width)
    solved = lax.linalg.triangular_solve(
        cholesky_factor, flattened, left_side=False, lower=True, transpose_a=True
    )
    solved = solved.reshape(tile_rows, tile_size, width)
    diag_tiles = cholesky_factor.reshape(tile_count, tile_size, width)
    row_choice = jnp.clip(rows_idx - first_tile, 0, tile_count - 1)
    diag_pick = jnp.take(diag_tiles, row_choice, axis=0)
    row_key = rows_idx[:, None, None]
    factor = jnp.where(
        row_key < first_tile, 0.0, jnp.where(row_key < first_tile + tile_count, diag_pick, solved)
    )
    gathered = []
    for column in range(tile_cols):
        target = column * col_devices + my_col
        owned_rows = lax.dynamic_index_in_dim(factor, target // row_devices, 0, keepdims=False)
        gathered.append(spread(owned_rows, "row", target % row_devices))
    across = jnp.stack(gathered)
    product = jnp.einsum("kxw,myw->kmxy", factor, across, precision=lax.Precision.HIGHEST)
    trailing = jnp.logical_and(
        rows_idx[:, None] >= first_tile + tile_count, cols_idx[None, :] >= first_tile + tile_count
    )
    in_panel = jnp.logical_and(cols_idx >= first_tile, cols_idx < first_tile + tile_count)
    col_pick = jnp.clip(cols_idx - first_tile, 0, tile_count - 1)
    panel_view = factor.reshape(tile_rows, tile_size, tile_count, tile_size)
    panel_cols = jnp.transpose(jnp.take(panel_view, col_pick, axis=2), (0, 2, 1, 3))
    updated = jnp.where(trailing[:, :, None, None], current - product, current)
    return jnp.where(in_panel[None, :, None, None], panel_cols, updated)


def on_device(covariance, tile_mask):
    tile_rows = covariance.shape[0]
    tile_cols = covariance.shape[2]
    tile_size = covariance.shape[4]
    row_devices = lax.axis_size("row")
    col_devices = lax.axis_size("col")
    my_row = lax.axis_index("row")
    my_col = lax.axis_index("col")
    rows_idx = jnp.arange(tile_rows, dtype=jnp.int32) * row_devices + my_row
    cols_idx = jnp.arange(tile_cols, dtype=jnp.int32) * col_devices + my_col
    mask_grid = tile_mask.reshape(tile_rows, row_devices, tile_cols, col_devices)
    picked = lax.dynamic_index_in_dim(mask_grid, my_row, 1, keepdims=False)
    picked = lax.dynamic_index_in_dim(picked, my_col, 2, keepdims=False)
    current = (
        covariance.reshape(tile_rows, tile_cols, tile_size, tile_size)
        * picked.astype(jnp.float32)[:, :, None, None]
    )
    for panel_index in range(PANELS):
        current = panel_step(current, rows_idx, cols_idx, panel_index * TPP, TPP)
    lead_tiles = PANELS * TPP
    above_lead = jnp.logical_and(rows_idx[:, None] < lead_tiles, cols_idx[None, :] >= lead_tiles)
    result = jnp.where(above_lead[:, :, None, None], 0.0, current).astype(jnp.bfloat16)
    return result.reshape(tile_rows, 1, tile_cols, 1, tile_size, tile_size)


def solution(mesh):
    in_specs = (P(None, "row", None, "col", None, None), P())
    out_specs = P(None, "row", None, "col", None, None)
    return jax.shard_map(
        on_device, mesh=mesh, in_specs=in_specs, out_specs=out_specs, check_vma=False
    )
```

profile of v0, /device:TPU:0, one launch (start us, length us, event | category | flops | bytes accessed | tf_op | source)
XLA Modules:
  0.0 466.2 jit_solution(15366503638760042811)
XLA Ops:
  7.6 1.6 copy.32
  9.4 1.0 copy-done
  11.4 39.8 %all-reduce.24.cloned.1.call-done = (f32[3,128,128]{1,2,0:T(8,128)}, f32[3,128,128]{1,2,0:T(8,128)}) async-done(((f32[3,128,128]{1,2,0:T(8,128)}, f32[3,128,128]{1,2,0:T(8,128)}), (f32[3,128,128]{1,2,0:T(8,128)}, f32[3,128,128]{1,2,0:T(8,128)})) %all-reduce.24.cloned.1.call-update) | async-done | bytes 393232 | tf_op jit(solution)/shard_map/psum | solution.py:12
  51.2 0.9 constant_dynamic-update-slice_fusion.1
  52.2 0.9 constant_dynamic-update-slice_fusion
  54.2 53.6 %all-reduce.20.cloned.1.call-done = (f32[128,256]{0,1:T(8,128)}, f32[128,256]{0,1:T(8,128)}) async-done(((f32[128,256]{0,1:T(8,128)}, f32[128,256]{0,1:T(8,128)}), (f32[128,256]{0,1:T(8,128)}, f32[128,256]{0,1:T(8,128)})) %all-reduce.20.cloned.1.call-update) | async-done | bytes 262160 | tf_op jit(solution)/shard_map/psum | solution.py:12
  108.7 0.9 constant_dynamic-update-slice_fusion.2
  109.8 11.7 %cholesky.130 = f32[128,128]{1,0:T(8,128)S(1)} custom-call(f32[128,128]{1,0:T(8,128)S(1)} %cholesky.194), custom_call_target="Cholesky" | custom-call | tf_op jit(solution)/shard_map/jit(cholesky)/cholesky | solution.py:30
  121.6 9.8 %custom-call.13 = f32[1,128,128]{1,2,0:T(8,128)S(1)} custom-call(f32[1,128,128]{2,1,0:T(8,128)S(1)} %get-tuple-element.96), custom_call_target="InvertDiagBlocksLowerTriangular" | custom-call | tf_op jit(solution)/shard_map/jit(cholesky)/cholesky | solution.py:30
  131.9 11.7 %cholesky.147 = f32[128,128]{1,0:T(8,128)S(1)} custom-call(f32[128,128]{1,0:T(8,128)S(1)} %convolution_subtract_fusion.3), custom_call_target="Cholesky" | custom-call | tf_op jit(solution)/shard_map/jit(cholesky)/cholesky | solution.py:30
  145.8 4.1 while.4
  146.6 1.4 bitcast_dynamic-update-slice_fusion.4
  148.5 1.4 bitcast_dynamic-update-slice_fusion.4
  149.9 19.7 %custom-call.14 = f32[2,128,128]{1,2,0:T(8,128)S(1)} custom-call(f32[2,128,128]{2,1,0:T(8,128)S(1)} %get-tuple-element.23), custom_call_target="InvertDiagBlocksLowerTriangular" | custom-call | tf_op jit(solution)/shard_map/triangular_solve/custom-call.0 | solution.py:32
  173.8 55.6 %all-reduce.18.cloned.1.call-done = (f32[1,128,256]{1,2,0:T(8,128)}, f32[1,128,256]{1,2,0:T(8,128)}, f32[1,128,256]{1,2,0:T(8,128)}, f32[1,128,256]{1,2,0:T(8,12...) async-done(((f32[1,128,256]{1,2,0:T(8,128)}, f32[1,128,256]{1,2,0:T(8,128)}, f32[1,128,256]{1,2,0:T(8,128)}, f32[1,128,256]{1,2,0:T(8,128)}, f32[1,128,256]{1,2,0:T(8,128)}, ...) | async-done | bytes 786448 | tf_op jit(solution)/shard_map/psum | solution.py:12
  229.4 1.0 constant_dynamic-update-slice_fusion.9
  234.2 1.7 fusion
  236.8 36.3 %all-reduce.22.cloned.1.call-done = (f32[3,128,128]{1,2,0:T(8,128)}, f32[3,128,128]{1,2,0:T(8,128)}) async-done(((f32[3,128,128]{1,2,0:T(8,128)}, f32[3,128,128]{1,2,0:T(8,128)}), (f32[3,128,128]{1,2,0:T(8,128)}, f32[3,128,128]{1,2,0:T(8,128)})) %all-reduce.22.cloned.1.call-update) | async-done | bytes 393232 | tf_op jit(solution)/shard_map/psum | solution.py:12
  273.0 0.9 constant_dynamic-update-slice_fusion.11
  274.0 0.9 constant_dynamic-update-slice_fusion.10
  275.9 53.6 %all-reduce.16.cloned.1.call-done = (f32[128,256]{0,1:T(8,128)}, f32[128,256]{0,1:T(8,128)}) async-done(((f32[128,256]{0,1:T(8,128)}, f32[128,256]{0,1:T(8,128)}), (f32[128,256]{0,1:T(8,128)}, f32[128,256]{0,1:T(8,128)})) %all-reduce.16.cloned.1.call-update) | async-done | bytes 262160 | tf_op jit(solution)/shard_map/psum | solution.py:12
  331.5 11.7 %cholesky.164 = f32[128,128]{1,0:T(8,128)S(1)} custom-call(f32[128,128]{1,0:T(8,128)S(1)} %cholesky.197), custom_call_target="Cholesky" | custom-call | tf_op jit(solution)/shard_map/jit(cholesky)/cholesky | solution.py:30
  343.3 9.8 %custom-call.15 = f32[1,128,128]{1,2,0:T(8,128)S(1)} custom-call(f32[1,128,128]{2,1,0:T(8,128)S(1)} %get-tuple-element.92), custom_call_target="InvertDiagBlocksLowerTriangular" | custom-call | tf_op jit(solution)/shard_map/jit(cholesky)/cholesky | solution.py:30
  353.5 11.7 %cholesky.181 = f32[128,128]{1,0:T(8,128)S(1)} custom-call(f32[128,128]{1,0:T(8,128)S(1)} %convolution_subtract_fusion.2), custom_call_target="Cholesky" | custom-call | tf_op jit(solution)/shard_map/jit(cholesky)/cholesky | solution.py:30
  368.1 4.3 while.5
  368.9 1.4 bitcast_dynamic-update-slice_fusion.5
  370.9 1.4 bitcast_dynamic-update-slice_fusion.5
  372.4 19.7 %custom-call.16 = f32[2,128,128]{1,2,0:T(8,128)S(1)} custom-call(f32[2,128,128]{2,1,0:T(8,128)S(1)} %get-tuple-element.24), custom_call_target="InvertDiagBlocksLowerTriangular" | custom-call | tf_op jit(solution)/shard_map/triangular_solve/custom-call.0 | solution.py:32
  396.3 55.6 %all-reduce.14.cloned.1.call-done = (f32[1,128,256]{1,2,0:T(8,128)}, f32[1,128,256]{1,2,0:T(8,128)}, f32[1,128,256]{1,2,0:T(8,128)}, f32[1,128,256]{1,2,0:T(8,12...) async-done(((f32[1,128,256]{1,2,0:T(8,128)}, f32[1,128,256]{1,2,0:T(8,128)}, f32[1,128,256]{1,2,0:T(8,128)}, f32[1,128,256]{1,2,0:T(8,128)}, f32[1,128,256]{1,2,0:T(8,128)}, ...) | async-done | bytes 786448 | tf_op jit(solution)/shard_map/psum | solution.py:12
  451.9 0.9 constant_dynamic-update-slice_fusion.19
  456.5 1.7 fusion.4
  458.3 1.1 copy.50
  (114 shorter events, 29.3 us)
Async XLA Ops:
  6.5 44.7 %all-reduce.24.cloned.1.call-start = ((), (), s32[]{:S(2)}) async-start(), calls=%async_computation.5 | async-start | bytes 786432 | tf_op jit(solution)/shard_map/psum | solution.py:12
  9.4 1.1 copy-start
  11.3 96.5 %all-reduce.20.cloned.1.call-start = ((), (), s32[]{:S(2)}) async-start(), calls=%async_computation.3 | async-start | bytes 524288 | tf_op jit(solution)/shard_map/psum | solution.py:12
  53.9 175.6 %all-reduce.18.cloned.1.call-start = ((), (), s32[]{:S(2)}) async-start(), calls=%async_computation.2 | async-start | bytes 1572864 | tf_op jit(solution)/shard_map/psum | solution.py:12
  173.1 100.0 %all-reduce.22.cloned.1.call-start = ((), (), s32[]{:S(2)}) async-start(), calls=%async_computation.4 | async-start | bytes 786432 | tf_op jit(solution)/shard_map/psum | solution.py:12
  229.4 4.7 %copy-start.3 = (f32[1,128,256]{1,2,0:T(8,128)S(1)}, f32[1,128,256]{1,2,0:T(8,128)}, u32[]{:S(2)}) copy-start(f32[1,128,256]{1,2,0:T(8,128)} %get-tuple-element.54) | copy-start | bytes 393220
  229.4 4.7 %copy-start.1 = (f32[3,6,128,128]{2,3,0,1:T(8,128)S(1)}, f32[3,6,128,128]{2,3,0,1:T(8,128)}, u32[]{:S(2)}) copy-start(f32[3,6,128,128]{2,3,0,1:T(8,128)} %copy-done) | copy-start | bytes 3538948
  236.7 92.8 %all-reduce.16.cloned.1.call-start = ((), (), s32[]{:S(2)}) async-start(), calls=%async_computation.1 | async-start | bytes 524288 | tf_op jit(solution)/shard_map/psum | solution.py:12
  275.6 176.2 %all-reduce.14.cloned.1.call-start = ((), (), s32[]{:S(2)}) async-start(), calls=%async_computation | async-start | bytes 1572864 | tf_op jit(solution)/shard_map/psum | solution.py:12
  451.9 4.6 copy-start.2
Sparse Core Ops, SparseCore 0:
  11.4 39.7 all-reduce.23
  54.6 53.1 all-reduce.19
  173.2 56.1 all-reduce.17
  236.8 36.1 all-reduce.21
  276.3 53.1 all-reduce.15
  395.7 56.1 all-reduce.13
where the time goes:
time: 467 us; the launch traced here: 466 us
  waiting for transfers between devices  294 us (63%)
  other arithmetic  114 us (24%)
  local copies, waits for them, and re-layouts  33.5 us (7%)
  between operations  16.8 us (4%)
  matrix products  6.99 us (1%)
    psum x6, waiting for transfers between devices, spread(): return lax.psum(kept, axis)  294 us
    another operation x13, other arithmetic, panel_step(): cholesky_factor = jnp.linalg.cholesky(diag_block)  68.7 us
    another operation x7, other arithmetic, panel_step(): lax.linalg.triangular_solve(cholesky_factor, flattened, left_side=False,...  39.5 us
    unnamed x24, local copies, waits for them, and re-layouts  16.5 us
  transfers between devices with their start and end apart: 6, of which 6 were waited for; matrix products, arithmetic and copies ran while one was open for 0% of the time, Pallas kernels for 0%

commit v1 on v0

v1 whole, which is shorter than its diff:
```python
import functools

import jax
import jax.numpy as jnp
from jax import lax
from jax.experimental import pallas as pl
from jax.experimental.pallas import tpu as pltpu
from jax.sharding import PartitionSpec as P

LEAD_TILES = 4
GROUP = 16
HIGHEST = lax.Precision.HIGHEST
VMEM = pl.BlockSpec(memory_space=pltpu.VMEM)
SMEM = pl.BlockSpec(memory_space=pltpu.SMEM)


def dot(a, b):
    return lax.dot_general(a, b, (((1,), (0,)), ((), ())), precision=HIGHEST, preferred_element_type=jnp.float32)


def dot_t(a, b):
    return lax.dot_general(a, b, (((1,), (1,)), ((), ())), precision=HIGHEST, preferred_element_type=jnp.float32)


def twice(a):
    return jnp.concatenate([a, a], axis=1)


def factor_tile(tile, u_ref, w_ref):
    n = tile.shape[0]
    row = lax.broadcasted_iota(jnp.int32, (n, n), 0)
    col = lax.broadcasted_iota(jnp.int32, (n, n), 1)
    w_ref[:, :n] = tile
    w_ref[:, n:] = jnp.where(row == col, 1.0, 0.0).astype(jnp.float32)
    row_1 = lax.broadcasted_iota(jnp.int32, (GROUP, n), 0)
    row_2 = lax.broadcasted_iota(jnp.int32, (GROUP, 2 * n), 0)
    group = w_ref[:GROUP, :]
    for first in range(0, n, GROUP):
        after = first + GROUP
        column = [jnp.broadcast_to(group[:, first + k : first + k + 1], (GROUP, n)) for k in range(GROUP)]
        if after < n:
            ahead = w_ref[after : after + GROUP, :]
            ahead_column = [jnp.broadcast_to(ahead[:, first + k : first + k + 1], (GROUP, n)) for k in range(GROUP)]
        for k in range(GROUP):
            pivot = jnp.broadcast_to(column[k][k : k + 1, :], (GROUP, n))
            inverse = 1.0 / pivot
            u_ref[first + k : first + k + 1, :] = group[k : k + 1, :] * twice(lax.rsqrt(pivot[:1]))
            scaled = jnp.broadcast_to(group[k : k + 1, :], (GROUP, 2 * n)) * twice(inverse)
            group = jnp.where(row_2 == k, scaled, group - twice(column[k]) * scaled)
            for m in range(k + 1, GROUP):
                scaled = jnp.broadcast_to(column[m][k : k + 1, :], (GROUP, n)) * inverse
                column[m] = jnp.where(row_1 == k, scaled, column[m] - column[k] * scaled)
        if after < n:
            reduced = group
            group = ahead
            for k in range(GROUP):
                group = group - twice(ahead_column[k]) * jnp.broadcast_to(reduced[k : k + 1, :], (GROUP, 2 * n))
            if after + GROUP < n:
                rest = w_ref[after + GROUP :, :]
                w_ref[after + GROUP :, :] = rest - dot(rest[:, first:after], reduced)


def factor_kernel(a_ref, l_ref, k_ref, w_ref, u_ref, s_ref):
    tiles, _, n, _ = a_ref.shape
    row = lax.broadcasted_iota(jnp.int32, (n, n), 0)
    col = lax.broadcasted_iota(jnp.int32, (n, n), 1)
    zero = jnp.zeros((n, n), jnp.float32)

    def at(i):
        return slice(i * n, (i + 1) * n)

    for i in range(tiles):
        for j in range(i + 1):
            s_ref[i, j] = a_ref[i, j]
    for b in range(tiles):
        factor_tile(s_ref[b, b], u_ref.at[b], w_ref)
        inverse = u_ref[b, :, n:]
        l_ref[at(b), at(b)] = jnp.where(col >= row, u_ref[b, :, :n], 0.0).T
        k_ref[at(b), at(b)] = inverse
        for i in range(b + 1, tiles):
            l_ref[at(i), at(b)] = dot_t(s_ref[i, b], inverse)
            for j in range(b + 1, i + 1):
                s_ref[i, j] = s_ref[i, j] - dot_t(l_ref[at(i), at(b)], l_ref[at(j), at(b)])
        for j in range(b):
            total = dot(l_ref[at(b), at(j)], k_ref[at(j), at(j)])
            for m in range(j + 1, b):
                total = total + dot(l_ref[at(b), at(m)], k_ref[at(m), at(j)])
            k_ref[at(b), at(j)] = -dot(inverse, total)
        for j in range(b + 1, tiles):
            l_ref[at(b), at(j)] = zero
            k_ref[at(b), at(j)] = zero


def factor(lead):
    tiles, _, n, _ = lead.shape
    whole = jax.ShapeDtypeStruct((tiles * n, tiles * n), jnp.float32)
    return pl.pallas_call(
        factor_kernel,
        out_shape=[whole, whole],
        in_specs=[VMEM],
        out_specs=[VMEM, VMEM],
        scratch_shapes=[
            pltpu.VMEM((n, 2 * n), jnp.float32),
            pltpu.VMEM((tiles, n, 2 * n), jnp.float32),
            pltpu.VMEM(lead.shape, jnp.float32),
        ],
        compiler_params=pltpu.CompilerParams(vmem_limit_bytes=32 * 2**20),
    )(lead)


def update_kernel(rows, cols, place_ref, mask_ref, a_ref, xr_ref, xc_ref, l_ref, k_ref, out_ref, zr_ref, zc_ref, x_ref, y_ref):
    tile_rows, tile_cols, n, _ = a_ref.shape
    lead = LEAD_TILES
    my_row, my_col = place_ref[0], place_ref[1]

    def at(i):
        return slice(i * n, (i + 1) * n)

    def mask(i, j):
        return mask_ref[i, j].astype(jnp.float32)

    first = 1 if cols == lead else 0
    for k in range(lead):
        for i in range(tile_rows):
            x_ref[at(i), at(k)] = xr_ref[k, i] * mask(i * rows + my_row, k)
        for j in range(first, tile_cols):
            y_ref[at(k), at(j - first)] = xc_ref[k, j] * mask(k, j * cols + my_col)
    half = lead * n // 2
    zr_ref[:, :half] = dot_t(x_ref[:, :half], k_ref[:half, :half])
    zr_ref[:, half:] = dot_t(x_ref[...], k_ref[half:, :])
    zc_ref[:half, :] = dot(k_ref[:half, :half], y_ref[:half, :])
    zc_ref[half:, :] = dot(k_ref[half:, :], y_ref[...])
    for i in range(tile_rows):
        in_lead = jnp.logical_and(i == 0, my_row < lead)
        product = dot(zr_ref[at(i), :], zc_ref[...])
        for j in range(first, tile_cols):
            rest = a_ref[i, j] * mask(i * rows + my_row, j * cols + my_col) - product[:, at(j - first)]
            out_ref[i, j] = jnp.where(in_lead, 0.0, rest).astype(jnp.bfloat16)
        for c in range(lead):

            @pl.when(my_col == c)
            def _():
                out_ref[i, 0] = zr_ref[at(i), at(c)].astype(jnp.bfloat16)
                if i == 0:
                    for r in range(lead):

                        @pl.when(my_row == r)
                        def _():
                            out_ref[0, 0] = l_ref[at(r), at(c)].astype(jnp.bfloat16)


def update(rows, cols, place, tile_mask, mine, from_cols, from_rows, lower, inverse):
    tile_rows, tile_cols, n, _ = mine.shape
    width = LEAD_TILES * n
    used = tile_cols - 1 if cols == LEAD_TILES else tile_cols
    return pl.pallas_call(
        functools.partial(update_kernel, rows, cols),
        out_shape=jax.ShapeDtypeStruct(mine.shape, jnp.bfloat16),
        in_specs=[SMEM, SMEM, VMEM, VMEM, VMEM, VMEM, VMEM],
        out_specs=VMEM,
        scratch_shapes=[
            pltpu.VMEM((tile_rows * n, width), jnp.float32),
            pltpu.VMEM((width, used * n), jnp.float32),
            pltpu.VMEM((tile_rows * n, width), jnp.float32),
            pltpu.VMEM((width, used * n), jnp.float32),
        ],
        compiler_params=pltpu.CompilerParams(vmem_limit_bytes=40 * 2**20),
    )(place, tile_mask, mine, from_cols, from_rows, lower, inverse)


def copy_down(value, axis):
    size, index = lax.axis_size(axis), lax.axis_index(axis)
    have = LEAD_TILES
    while have < size:
        pairs = [(i, i + have) for i in range(have) if i + have < size]
        value = jnp.where(index >= have, lax.ppermute(value, axis, pairs), value)
        have *= 2
    return value


def swap(value, axis, bit):
    size, index = lax.axis_size(axis), lax.axis_index(axis)
    other = lax.ppermute(value, axis, [(i, i ^ bit) for i in range(size)])
    upper = (index & bit) != 0
    return jnp.stack([jnp.where(upper, other, value), jnp.where(upper, value, other)])


def rotate(value, axis):
    size, index = lax.axis_size(axis), lax.axis_index(axis)
    group = LEAD_TILES
    parts = [value]
    for shift in range(1, group):
        pairs = [(i, i // group * group + (i + shift) % group) for i in range(size)]
        parts.append(lax.ppermute(value, axis, pairs))
    place = index % group
    return jnp.stack([lax.select_n((place - k) % group, *parts) for k in range(group)])


def on_device(covariance, tile_mask):
    tile_rows, _, tile_cols, _, n, _ = covariance.shape
    rows, cols = lax.axis_size("row"), lax.axis_size("col")
    mine = covariance.reshape(tile_rows, tile_cols, n, n)
    lead = copy_down(mine[0, 0], "row")
    lead = rotate(copy_down(lead, "col"), "col")
    lead = swap(swap(lead, "row", 2), "row", 1)
    lead = jnp.stack([lead[r & 1, r >> 1] for r in range(LEAD_TILES)])
    from_cols = rotate(copy_down(mine[:, 0], "col"), "col")
    from_rows = swap(swap(copy_down(mine[0], "row"), "row", 2), "row", 1)
    from_rows = jnp.stack([from_rows[r & 1, r >> 1] for r in range(LEAD_TILES)])
    lower, inverse = factor(lead)
    place = jnp.stack([lax.axis_index("row"), lax.axis_index("col")]).astype(jnp.int32)
    out = update(rows, cols, place, tile_mask, mine, from_cols, from_rows, lower, inverse)
    return out.reshape(tile_rows, 1, tile_cols, 1, n, n)


def solution(mesh):
    in_specs = (P(None, "row", None, "col", None, None), P())
    out_specs = P(None, "row", None, "col", None, None)
    return jax.shard_map(on_device, mesh=mesh, in_specs=in_specs, out_specs=out_specs, check_vma=False)
```

time: 467 us -> 71.6 us (0.15)
  the two profiles are of different devices: /device:TPU:0 before, /device:TPU:19 now
where the time goes in v1:
time: 71.6 us; the launch traced here: 71.3 us
  starting transfers between devices  22.8 us (32%)
  Pallas kernels  22 us (31%)
  waiting for transfers between devices  20.6 us (29%)
  local copies, waits for them, and re-layouts  3.83 us (5%)
  other arithmetic  1.87 us (3%)
    pallas_call x1, Pallas kernels, factor(): pl.pallas_call(factor_kernel, out_shape=[whole, whole], in_specs=[VMEM],...  14.9 us
    ppermute x6, starting transfers between devices, rotate(): parts.append(lax.ppermute(value, axis, pairs))  12 us
    ppermute x4, waiting for transfers between devices, swap(): other = lax.ppermute(value, axis, [(i, i ^ bit) for i in range(size)])  9.13 us
    pallas_call x1, Pallas kernels, update(): pl.pallas_call(functools.partial(update_kernel, rows, cols), out_shape=ja...  7.1 us
    ppermute x4, starting transfers between devices, swap(): other = lax.ppermute(value, axis, [(i, i ^ bit) for i in range(size)])  6.2 us
    ppermute x2, waiting for transfers between devices, copy_down(): value = jnp.where(index >= have, lax.ppermute(value, axis, pairs), value)  5.73 us
    ppermute x6, waiting for transfers between devices, rotate(): parts.append(lax.ppermute(value, axis, pairs))  5.71 us
    ppermute x2, starting transfers between devices, copy_down(): value = jnp.where(index >= have, lax.ppermute(value, axis, pairs), value)  4.59 us
  transfers between devices with their start and end apart: 12, of which 7 were waited for; matrix products, arithmetic and copies ran while one was open for 5% of the time, Pallas kernels for 21%

profile of v1, /device:TPU:19, one launch (start us, length us, event | category | flops | bytes accessed | tf_op | source)
XLA Modules:
  0.0 71.3 jit_solution(4499137197665941027)
XLA Ops:
  0.0 1.0 %slice_bitcast_fusion.4 = f32[6,128,128]{2,1,0:T(8,128)S(1)} fusion(f32[3,1,6,1,128,128]{5,4,2,3,1,0:T(8,128)} %bitcast.76), kind=kLoop, calls=%fused_computation.14 | loop fusion | bytes 786432 | tf_op jit(solution)/shard_map/squeeze | solution.py:208
  1.0 3.3 %collective-permute-start.3 = (f32[6,128,128]{2,1,0:T(8,128)S(1)}, f32[6,128,128]{2,1,0:T(8,128)S(1)}, u32[]{:S(2)}, u32[]{:S(2)}) collective-permute-start(f32[6,128,128]{2,1,0:T(8,128)S(1)} %slice_bitcast_fusion.4), channel_id=1, source_target_pairs={{0,16},{4,20},{8,24},{12,28},{1,17},{5,21},{9,25},{13,29},{2,18},{... | collective-permute-start | bytes 1179656 | tf_op jit(solution)/shard_map/ppermute | solution.py:176
  4.3 1.3 %copy.9 = f32[3,1,6,1,128,128]{5,4,0,2,3,1:T(8,128)S(1)} copy(f32[3,1,6,1,128,128]{5,4,3,2,1,0:T(8,128)} %param.2) | data formatting | bytes 2359296 | tf_op args[0]
  5.7 1.3 %collective-permute-start.6 = (f32[128,128]{1,0:T(8,128)S(1)}, f32[128,128]{1,0:T(8,128)S(1)}, u32[]{:S(2)}, u32[]{:S(2)}) collective-permute-start(f32[128,128]{1,0:T(8,128)S(1)} %slice_bitcast_fusion.10), channel_id=1, source_target_pairs={{0,16},{4,20},{8,24},{12,28},{1,17},{5,21},{9,25},{13,29},{2,18},{... | collective-permute-start | bytes 196616 | tf_op jit(solution)/shard_map/ppermute | solution.py:176
  7.0 0.7 slice_bitcast_fusion.9
  7.8 5.7 %collective-permute-done.6 = f32[128,128]{1,0:T(8,128)S(1)} collective-permute-done((f32[128,128]{1,0:T(8,128)S(1)}, f32[128,128]{1,0:T(8,128)S(1)}, u32[]{:S(2)}, u32[]{:S(2)}) %collective-permute-start.6) | collective-permute-done | bytes 65568 | tf_op jit(solution)/shard_map/ppermute | solution.py:176
  13.5 0.2 collective-permute-start.9
  13.7 3.2 %collective-permute-start.8 = (f32[128,128]{1,0:T(8,128)S(1)}, f32[128,128]{1,0:T(8,128)S(1)}, u32[]{:S(2)}, u32[]{:S(2)}) collective-permute-start(f32[128,128]{1,0:T(8,128)S(1)} %broadcast_select_fusion.1), channel_id=1, source_target_pairs={{0,2},{1,3},{2,0},{3,1},{4,6},{5,7},{6,4},{7,5},{8,10},{9,11},{10,... | collective-permute-start | bytes 196616 | tf_op jit(solution)/shard_map/ppermute | solution.py:194
  17.0 0.8 %collective-permute-done.9 = f32[128,128]{1,0:T(8,128)S(1)} collective-permute-done((f32[128,128]{1,0:T(8,128)S(1)}, f32[128,128]{1,0:T(8,128)S(1)}, u32[]{:S(2)}, u32[]{:S(2)}) %collective-permute-start.9) | collective-permute-done | bytes 65568 | tf_op jit(solution)/shard_map/ppermute | solution.py:194
  17.9 1.9 %collective-permute-start.2 = (f32[3,128,128]{2,1,0:T(8,128)}, f32[3,128,128]{2,1,0:T(8,128)S(1)}, u32[]{:S(2)}, u32[]{:S(2)}) collective-permute-start(f32[3,128,128]{2,1,0:T(8,128)} %slice_bitcast_fusion.9), channel_id=1, source_target_pairs={{0,3},{1,0},{2,1},{3,2},{4,7},{5,4},{6,5},{7,6},{8,11},{9,8},{10,9... | collective-permute-start | bytes 589832 | tf_op jit(solution)/shard_map/ppermute | solution.py:194
  19.8 0.9 %collective-permute-done.8 = f32[128,128]{1,0:T(8,128)S(1)} collective-permute-done((f32[128,128]{1,0:T(8,128)S(1)}, f32[128,128]{1,0:T(8,128)S(1)}, u32[]{:S(2)}, u32[]{:S(2)}) %collective-permute-start.8) | collective-permute-done | bytes 65568 | tf_op jit(solution)/shard_map/ppermute | solution.py:194
  20.7 6.7 %collective-permute-start = (f32[3,128,128]{2,1,0:T(8,128)}, f32[3,128,128]{2,1,0:T(8,128)S(1)}, u32[]{:S(2)}, u32[]{:S(2)}) collective-permute-start(f32[3,128,128]{2,1,0:T(8,128)} %slice_bitcast_fusion.9), channel_id=1, source_target_pairs={{0,1},{1,2},{2,3},{3,0},{4,5},{5,6},{6,7},{7,4},{8,9},{9,10},{10,1... | collective-permute-start | bytes 589832 | tf_op jit(solution)/shard_map/ppermute | solution.py:194
  27.4 2.3 %collective-permute-done.7 = f32[128,128]{1,0:T(8,128)} collective-permute-done((f32[128,128]{1,0:T(8,128)S(1)}, f32[128,128]{1,0:T(8,128)}, u32[]{:S(2)}, u32[]{:S(2)}) %collective-permute-start.7) | collective-permute-done | bytes 65568 | tf_op jit(solution)/shard_map/ppermute | solution.py:194
  29.6 0.9 %select_bitcast_fusion.15 = (f32[1,128,128]{2,1,0:T(8,128)S(1)}, f32[1,128,128]{2,1,0:T(8,128)S(1)}, f32[1,128,128]{2,1,0:T(8,128)S(1)}, f32[1,128,128]{2,1,0:T(8,128)S(1)}) fusion(f32[128,128]{1,0:T(8,128)S(1)} %collective-permute-done.8, f32[128,128]{1,0:T(8,128)S(1)} %collective-permute-done.9, f32[128,128]{1,0:T(8,128)S(1)} %broadcast_select_fusion.1, ...), kind=kLoop, calls=%fused_computation.34 | loop fusion | flops 196608 | bytes 524300 | tf_op jit(solution)/shard_map/stack | solution.py:196
  30.5 0.3 collective-permute-start.10
  30.9 1.3 %collective-permute-start.4 = (f32[6,128,128]{2,1,0:T(8,128)S(1)}, f32[6,128,128]{2,1,0:T(8,128)S(1)}, u32[]{:S(2)}, u32[]{:S(2)}) collective-permute-start(f32[6,128,128]{2,1,0:T(8,128)S(1)} %broadcast_select_fusion), channel_id=1, source_target_pairs={{0,8},{4,12},{8,0},{12,4},{16,24},{20,28},{24,16},{28,20},{1,9},{5... | collective-permute-start | bytes 1179656 | tf_op jit(solution)/shard_map/ppermute | solution.py:183
  32.2 1.7 %collective-permute-done = f32[3,128,128]{2,1,0:T(8,128)S(1)} collective-permute-done((f32[3,128,128]{2,1,0:T(8,128)}, f32[3,128,128]{2,1,0:T(8,128)S(1)}, u32[]{:S(2)}, u32[]{:S(2)}) %collective-permute-start) | collective-permute-done | bytes 196640 | tf_op jit(solution)/shard_map/ppermute | solution.py:194
  33.9 0.1 select_bitcast_fusion.11
  34.0 3.7 %collective-permute-done.10 = f32[4,128,128]{2,1,0:T(8,128)S(1)} collective-permute-done((f32[4,128,128]{2,1,0:T(8,128)S(1)}, f32[4,128,128]{2,1,0:T(8,128)S(1)}, u32[]{:S(2)}, u32[]{:S(2)}) %collective-permute-start.10) | collective-permute-done | bytes 262176 | tf_op jit(solution)/shard_map/ppermute | solution.py:183
  37.8 2.9 %collective-permute-start.11 = (f32[2,4,128,128]{3,2,1,0:T(8,128)S(1)}, f32[2,4,128,128]{3,2,1,0:T(8,128)S(1)}, u32[]{:S(2)}, u32[]{:S(2)}) collective-permute-start(f32[2,4,128,128]{3,2,1,0:T(8,128)S(1)} %pad_maximum_fusion.4), channel_id=1, source_target_pairs={{0,4},{4,0},{8,12},{12,8},{16,20},{20,16},{24,28},{28,24},{1,5},{5... | collective-permute-start | bytes 1572872 | tf_op jit(solution)/shard_map/ppermute | solution.py:183
  40.7 5.4 %collective-permute-done.4 = f32[6,128,128]{2,1,0:T(8,128)S(1)} collective-permute-done((f32[6,128,128]{2,1,0:T(8,128)S(1)}, f32[6,128,128]{2,1,0:T(8,128)S(1)}, u32[]{:S(2)}, u32[]{:S(2)}) %collective-permute-start.4) | collective-permute-done | bytes 393248 | tf_op jit(solution)/shard_map/ppermute | solution.py:183
  46.1 0.1 select_bitcast_fusion.5
  46.3 1.7 %collective-permute-start.5 = (f32[2,6,128,128]{3,2,1,0:T(8,128)S(1)}, f32[2,6,128,128]{3,2,1,0:T(8,128)S(1)}, u32[]{:S(2)}, u32[]{:S(2)}) collective-permute-start(f32[2,6,128,128]{3,2,1,0:T(8,128)S(1)} %pad_maximum_fusion.3), channel_id=1, source_target_pairs={{0,4},{4,0},{8,12},{12,8},{16,20},{20,16},{24,28},{28,24},{1,5},{5... | collective-permute-start | bytes 2359304 | tf_op jit(solution)/shard_map/ppermute | solution.py:183
  48.0 0.1 select_bitcast_fusion.3
  48.1 0.1 slice_bitcast_fusion.7
  48.2 0.1 pad_maximum_fusion.1.a_ref
  48.3 14.9 %shard_map.28 = (f32[512,512]{1,0:T(8,128)S(1)}, f32[512,512]{1,0:T(8,128)S(1)}) custom-call(f32[4,4,128,128]{3,2,1,0:T(8,128)S(1)} %pad_maximum_fusion.1.a_ref), custom_call_target="tpu_custom_call" | custom-call | tf_op jit(solution)/shard_map/pallas_call | solution.py:97
  63.2 0.2 select_bitcast_fusion.1
  63.4 0.1 slice_bitcast_fusion.2
  63.5 0.1 pad_maximum_fusion.xc_ref
  63.7 0.5 copy-done.1
  64.2 7.1 %shard_map.29 = bf16[3,6,128,128]{3,2,1,0:T(8,128)(2,1)} custom-call(s32[2]{0:T(128)S(1)} %pad_add_fusion.place_ref, s32[24,24]{1,0:T(8,128)S(1)} %copy-done.1, f32[3,6,128,128]{3,2,1,0:T(8,128)S(1)} %bitcast.78, f32[4,3,128,128]{3,2,1,0:T(8,128)S(1)} %pad_maximum_fusion.2.xr_ref, f32[4,6,128,128]{3,2,1,0:T(8,128)S(1)} %pad_maximum_fusion.xc_ref, ...), custom_call_target="tpu_custom_call" | custom-call | tf_op jit(solution)/shard_map/pallas_call | solution.py:156
  (19 shorter events, 0.4 us)
Async XLA Ops:
  1.0 29.8 %copy-start = (f32[3,1,6,1,128,128]{5,4,3,2,1,0:T(8,128)S(1)}, f32[3,1,6,1,128,128]{5,4,3,2,1,0:T(8,128)}, u32[]{:S(2)}) copy-start(f32[3,1,6,1,128,128]{5,4,3,2,1,0:T(8,128)} %param.2) | copy-start | bytes 3538948
  1.0 29.8 %collective-permute-start.3 = (f32[6,128,128]{2,1,0:T(8,128)S(1)}, f32[6,128,128]{2,1,0:T(8,128)S(1)}, u32[]{:S(2)}, u32[]{:S(2)}) collective-permute-start(f32[6,128,128]{2,1,0:T(8,128)S(1)} %slice_bitcast_fusion.4), channel_id=1, source_target_pairs={{0,16},{4,20},{8,24},{12,28},{1,17},{5,21},{9,25},{13,29},{2,18},{... | collective-permute-start | bytes 1179656 | tf_op jit(solution)/shard_map/ppermute | solution.py:176
  5.7 7.8 %collective-permute-start.6 = (f32[128,128]{1,0:T(8,128)S(1)}, f32[128,128]{1,0:T(8,128)S(1)}, u32[]{:S(2)}, u32[]{:S(2)}) collective-permute-start(f32[128,128]{1,0:T(8,128)S(1)} %slice_bitcast_fusion.10), channel_id=1, source_target_pairs={{0,16},{4,20},{8,24},{12,28},{1,17},{5,21},{9,25},{13,29},{2,18},{... | collective-permute-start | bytes 196616 | tf_op jit(solution)/shard_map/ppermute | solution.py:176
  7.7 24.5 %collective-permute-start.1 = (f32[3,128,128]{2,1,0:T(8,128)}, f32[3,128,128]{2,1,0:T(8,128)S(1)}, u32[]{:S(2)}, u32[]{:S(2)}) collective-permute-start(f32[3,128,128]{2,1,0:T(8,128)} %slice_bitcast_fusion.9), channel_id=1, source_target_pairs={{0,2},{1,3},{2,0},{3,1},{4,6},{5,7},{6,4},{7,5},{8,10},{9,11},{10,... | collective-permute-start | bytes 589832 | tf_op jit(solution)/shard_map/ppermute | solution.py:194
  13.5 4.4 %collective-permute-start.9 = (f32[128,128]{1,0:T(8,128)S(1)}, f32[128,128]{1,0:T(8,128)S(1)}, u32[]{:S(2)}, u32[]{:S(2)}) collective-permute-start(f32[128,128]{1,0:T(8,128)S(1)} %broadcast_select_fusion.1), channel_id=1, source_target_pairs={{0,3},{1,0},{2,1},{3,2},{4,7},{5,4},{6,5},{7,6},{8,11},{9,8},{10,9... | collective-permute-start | bytes 196616 | tf_op jit(solution)/shard_map/ppermute | solution.py:194
  13.7 7.0 %collective-permute-start.8 = (f32[128,128]{1,0:T(8,128)S(1)}, f32[128,128]{1,0:T(8,128)S(1)}, u32[]{:S(2)}, u32[]{:S(2)}) collective-permute-start(f32[128,128]{1,0:T(8,128)S(1)} %broadcast_select_fusion.1), channel_id=1, source_target_pairs={{0,2},{1,3},{2,0},{3,1},{4,6},{5,7},{6,4},{7,5},{8,10},{9,11},{10,... | collective-permute-start | bytes 196616 | tf_op jit(solution)/shard_map/ppermute | solution.py:194
  16.9 12.7 %collective-permute-start.7 = (f32[128,128]{1,0:T(8,128)S(1)}, f32[128,128]{1,0:T(8,128)}, u32[]{:S(2)}, u32[]{:S(2)}) collective-permute-start(f32[128,128]{1,0:T(8,128)S(1)} %broadcast_select_fusion.1), channel_id=1, source_target_pairs={{0,1},{1,2},{2,3},{3,0},{4,5},{5,6},{6,7},{7,4},{8,9},{9,10},{10,1... | collective-permute-start | bytes 196616 | tf_op jit(solution)/shard_map/ppermute | solution.py:194
  17.9 14.3 %collective-permute-start.2 = (f32[3,128,128]{2,1,0:T(8,128)}, f32[3,128,128]{2,1,0:T(8,128)S(1)}, u32[]{:S(2)}, u32[]{:S(2)}) collective-permute-start(f32[3,128,128]{2,1,0:T(8,128)} %slice_bitcast_fusion.9), channel_id=1, source_target_pairs={{0,3},{1,0},{2,1},{3,2},{4,7},{5,4},{6,5},{7,6},{8,11},{9,8},{10,9... | collective-permute-start | bytes 589832 | tf_op jit(solution)/shard_map/ppermute | solution.py:194
  20.7 13.2 %collective-permute-start = (f32[3,128,128]{2,1,0:T(8,128)}, f32[3,128,128]{2,1,0:T(8,128)S(1)}, u32[]{:S(2)}, u32[]{:S(2)}) collective-permute-start(f32[3,128,128]{2,1,0:T(8,128)} %slice_bitcast_fusion.9), channel_id=1, source_target_pairs={{0,1},{1,2},{2,3},{3,0},{4,5},{5,6},{6,7},{7,4},{8,9},{9,10},{10,1... | collective-permute-start | bytes 589832 | tf_op jit(solution)/shard_map/ppermute | solution.py:194
  30.5 7.2 %collective-permute-start.10 = (f32[4,128,128]{2,1,0:T(8,128)S(1)}, f32[4,128,128]{2,1,0:T(8,128)S(1)}, u32[]{:S(2)}, u32[]{:S(2)}) collective-permute-start(f32[4,128,128]{2,1,0:T(8,128)S(1)} %pad_maximum_fusion.5), channel_id=1, source_target_pairs={{0,8},{4,12},{8,0},{12,4},{16,24},{20,28},{24,16},{28,20},{1,9},{5... | collective-permute-start | bytes 786440 | tf_op jit(solution)/shard_map/ppermute | solution.py:183
  30.9 15.2 %collective-permute-start.4 = (f32[6,128,128]{2,1,0:T(8,128)S(1)}, f32[6,128,128]{2,1,0:T(8,128)S(1)}, u32[]{:S(2)}, u32[]{:S(2)}) collective-permute-start(f32[6,128,128]{2,1,0:T(8,128)S(1)} %broadcast_select_fusion), channel_id=1, source_target_pairs={{0,8},{4,12},{8,0},{12,4},{16,24},{20,28},{24,16},{28,20},{1,9},{5... | collective-permute-start | bytes 1179656 | tf_op jit(solution)/shard_map/ppermute | solution.py:183
  37.8 10.2 %collective-permute-start.11 = (f32[2,4,128,128]{3,2,1,0:T(8,128)S(1)}, f32[2,4,128,128]{3,2,1,0:T(8,128)S(1)}, u32[]{:S(2)}, u32[]{:S(2)}) collective-permute-start(f32[2,4,128,128]{3,2,1,0:T(8,128)S(1)} %pad_maximum_fusion.4), channel_id=1, source_target_pairs={{0,4},{4,0},{8,12},{12,8},{16,20},{20,16},{24,28},{28,24},{1,5},{5... | collective-permute-start | bytes 1572872 | tf_op jit(solution)/shard_map/ppermute | solution.py:183
  46.3 16.9 %collective-permute-start.5 = (f32[2,6,128,128]{3,2,1,0:T(8,128)S(1)}, f32[2,6,128,128]{3,2,1,0:T(8,128)S(1)}, u32[]{:S(2)}, u32[]{:S(2)}) collective-permute-start(f32[2,6,128,128]{3,2,1,0:T(8,128)S(1)} %pad_maximum_fusion.3), channel_id=1, source_target_pairs={{0,4},{4,0},{8,12},{12,8},{16,20},{20,16},{24,28},{28,24},{1,5},{5... | collective-permute-start | bytes 2359304 | tf_op jit(solution)/shard_map/ppermute | solution.py:183
  63.5 0.7 copy-start.1

commit v2 on v1

v2 whole, which is shorter than its diff:
```python
import functools

import jax
import jax.numpy as jnp
from jax import lax
from jax.experimental import pallas as pl
from jax.experimental.pallas import tpu as pltpu
from jax.sharding import PartitionSpec as P

LEAD = 4
HALF = 2
SENT = 3
GROUP = 16
HIGHEST = lax.Precision.HIGHEST
VMEM = pl.BlockSpec(memory_space=pltpu.VMEM)
SMEM = pl.BlockSpec(memory_space=pltpu.SMEM)
ROW_BY_COL = (((1,), (0,)), ((), ()))
ROW_BY_ROW = (((1,), (1,)), ((), ()))


def dot(a, b, dims=ROW_BY_COL):
    return lax.dot_general(a, b, dims, precision=HIGHEST, preferred_element_type=jnp.float32)


def dot_t(a, b):
    return dot(a, b, ROW_BY_ROW)


def split(a):
    high = a.astype(jnp.bfloat16)
    return high, (a - high.astype(jnp.float32)).astype(jnp.bfloat16)


def dot_3(a, b, dims=ROW_BY_COL):
    def part(x, y):
        return lax.dot_general(x, y, dims, preferred_element_type=jnp.float32)

    return part(a[0], b[0]) + (part(a[0], b[1]) + part(a[1], b[0]))


def twice(a):
    return jnp.concatenate([a, a], axis=1)


def factor_tile(tile, u_ref, w_ref):
    n = tile.shape[0]
    row = lax.broadcasted_iota(jnp.int32, (n, n), 0)
    col = lax.broadcasted_iota(jnp.int32, (n, n), 1)
    w_ref[:, :n] = tile
    w_ref[:, n:] = jnp.where(row == col, 1.0, 0.0).astype(jnp.float32)
    group_row = lax.broadcasted_iota(jnp.int32, (GROUP, n), 0)
    group = w_ref[:GROUP, :]
    for first in range(0, n, GROUP):
        after = first + GROUP
        column = [jnp.broadcast_to(group[:, first + k : first + k + 1], (GROUP, n)) for k in range(GROUP)]
        if after < n:
            ahead = w_ref[after : after + GROUP, :]
            ahead_column = [jnp.broadcast_to(ahead[:, first + k : first + k + 1], (GROUP, n)) for k in range(GROUP)]
        pivots = inverses = jnp.ones((GROUP, n), jnp.float32)
        for k in range(GROUP):
            here = group_row == k
            pivot = jnp.broadcast_to(column[k][k : k + 1, :], (GROUP, n))
            inverse = 1.0 / pivot
            factors = jnp.where(here, 0.0, column[k] * inverse)
            pivots = jnp.where(here, pivot, pivots)
            inverses = jnp.where(here, inverse, inverses)
            u_ref[first + k : first + k + 1, :] = group[k : k + 1, :]
            for m in range(k + 1, GROUP):
                column[m] = column[m] - factors * jnp.broadcast_to(column[m][k : k + 1, :], (GROUP, n))
            group = group - twice(factors) * jnp.broadcast_to(group[k : k + 1, :], (GROUP, 2 * n))
        u_ref[first:after, :] = u_ref[first:after, :] * twice(lax.rsqrt(pivots))
        if after < n:
            reduced = group * twice(inverses)
            terms = [
                twice(ahead_column[k]) * jnp.broadcast_to(reduced[k : k + 1, :], (GROUP, 2 * n)) for k in range(GROUP)
            ]
            group = (ahead - sum(terms[2::2], terms[0])) - sum(terms[3::2], terms[1])
            if after + GROUP < n:
                rest = w_ref[after + GROUP :, :]
                w_ref[after + GROUP :, :] = rest - dot(rest[:, first:after], reduced)


def finish_tile(u):
    n = u.shape[0]
    row = lax.broadcasted_iota(jnp.int32, (n, n), 0)
    col = lax.broadcasted_iota(jnp.int32, (n, n), 1)
    return jnp.where(col >= row, u[:, :n], 0.0).T, u[:, n:]


def at(i, n):
    return slice(i * n, (i + 1) * n)


def factor_first(place_ref, a_ref, l_ref, k_ref, s_out_ref, w_ref, u_ref, s_ref):
    n = a_ref.shape[-1]
    my_row = place_ref[0]

    def raw(i, j):
        if (i - j) % LEAD < SENT:
            apart = (my_row ^ i) & (LEAD - 1)
            return a_ref[apart & 1, apart >> 1, (i - j) % LEAD]
        return raw(j, i).T

    for i in range(LEAD):
        for j in range(i + 1):
            s_ref[i, j] = raw(i, j)
    for b in range(HALF):
        factor_tile(s_ref[b, b], u_ref, w_ref)
        lower, inverse = finish_tile(u_ref[...])
        l_ref[at(b, n), at(b, n)] = lower
        k_ref[at(b, n), at(b, n)] = inverse
        for i in range(b + 1, LEAD):
            l_ref[at(i, n), at(b, n)] = dot_t(s_ref[i, b], inverse)
            for j in range(b + 1, i + 1):
                s_ref[i, j] = s_ref[i, j] - dot_t(l_ref[at(i, n), at(b, n)], l_ref[at(j, n), at(b, n)])
        for j in range(b):
            k_ref[at(b, n), at(j, n)] = -dot(inverse, dot(l_ref[at(b, n), at(j, n)], k_ref[at(j, n), at(j, n)]))
        for j in range(b + 1, HALF):
            l_ref[at(b, n), at(j, n)] = jnp.zeros((n, n), jnp.float32)
            k_ref[at(b, n), at(j, n)] = jnp.zeros((n, n), jnp.float32)
    for i in range(HALF, LEAD):
        for j in range(HALF, i + 1):
            s_out_ref[i - HALF, j - HALF] = s_ref[i, j]


def factor_second(s_in_ref, l_in_ref, k_in_ref, l_ref, k_ref, w_ref, u_ref, s_ref):
    n = s_in_ref.shape[-1]
    rest = LEAD - HALF
    start = HALF * n
    for i in range(rest):
        for j in range(i + 1):
            s_ref[i, j] = s_in_ref[i, j]
    for b in range(rest):
        factor_tile(s_ref[b, b], u_ref, w_ref)
        lower, inverse = finish_tile(u_ref[...])
        l_ref[at(b, n), at(b, n)] = lower
        k_ref[at(b, n), at(b + HALF, n)] = inverse
        for i in range(b + 1, rest):
            l_ref[at(i, n), at(b, n)] = dot_t(s_ref[i, b], inverse)
            for j in range(b + 1, i + 1):
                s_ref[i, j] = s_ref[i, j] - dot_t(l_ref[at(i, n), at(b, n)], l_ref[at(j, n), at(b, n)])
        total = dot(l_in_ref[at(b + HALF, n), :], k_in_ref[...])
        for m in range(b):
            total = total + dot(l_ref[at(b, n), at(m, n)], k_ref[at(m, n), :start])
        k_ref[at(b, n), :start] = -dot(inverse, total)
        for j in range(b):
            k_ref[at(b, n), at(j + HALF, n)] = -dot(inverse, dot(l_ref[at(b, n), at(j, n)], k_ref[at(j, n), at(j + HALF, n)]))
        for j in range(b + 1, rest):
            l_ref[at(b, n), at(j, n)] = jnp.zeros((n, n), jnp.float32)
            k_ref[at(b, n), at(j + HALF, n)] = jnp.zeros((n, n), jnp.float32)


def factor_call(kernel, in_specs, out_shapes, n):
    return pl.pallas_call(
        kernel,
        out_shape=[jax.ShapeDtypeStruct(shape, jnp.float32) for shape in out_shapes],
        in_specs=in_specs,
        out_specs=[VMEM] * len(out_shapes),
        scratch_shapes=[
            pltpu.VMEM((n, 2 * n), jnp.float32),
            pltpu.VMEM((n, 2 * n), jnp.float32),
            pltpu.VMEM((LEAD, LEAD, n, n), jnp.float32),
        ],
        compiler_params=pltpu.CompilerParams(vmem_limit_bytes=32 * 2**20),
        cost_estimate=pl.CostEstimate(flops=8 * 10**9, bytes_accessed=2**20, transcendentals=0),
    )


def update_kernel(
    rows, cols, place_ref, mask_ref, a_ref, xr_ref, xc_ref, l1_ref, k1_ref, l2_ref, k2_ref, out_ref, x_ref, y_ref, zr_ref, zc_ref
):
    tile_rows, tile_cols, n, _ = a_ref.shape
    my_row, my_col = place_ref[0], place_ref[1]
    skip = 1 if cols == LEAD else 0
    half = HALF * n

    def mask(i, j):
        return mask_ref[i, j].astype(jnp.float32)

    def pair(ref, rows_at, cols_at):
        return ref[0, rows_at, cols_at], ref[1, rows_at, cols_at]

    def put(ref, rows_at, cols_at, value):
        ref[0, rows_at, cols_at], ref[1, rows_at, cols_at] = split(value)

    for k in range(LEAD):
        for i in range(tile_rows):
            put(x_ref, at(i, n), at(k, n), xr_ref[(my_col - k) & (LEAD - 1), i] * mask(i * rows + my_row, k))
        apart = (my_row ^ k) & (LEAD - 1)
        for j in range(skip, tile_cols):
            put(y_ref, at(k, n), at(j - skip, n), xc_ref[apart & 1, apart >> 1, j - skip] * mask(k, j * cols + my_col))
    every = slice(None)
    head, tail = slice(0, half), slice(half, LEAD * n)
    k1, k2 = split(k1_ref[...]), split(k2_ref[...])
    zr1 = dot_3(pair(x_ref, every, head), k1, ROW_BY_ROW)
    zr2 = dot_3(pair(x_ref, every, every), k2, ROW_BY_ROW)
    put(zr_ref, every, head, zr1)
    put(zr_ref, every, tail, zr2)
    put(zc_ref, head, every, dot_3(k1, pair(y_ref, head, every)))
    put(zc_ref, tail, every, dot_3(k2, pair(y_ref, every, every)))
    for i in range(tile_rows):
        in_lead = jnp.logical_and(i == 0, my_row < LEAD)
        product = dot_3(pair(zr_ref, at(i, n), every), pair(zc_ref, every, every))
        for j in range(skip, tile_cols):
            rest = a_ref[i, j] * mask(i * rows + my_row, j * cols + my_col) - product[:, at(j - skip, n)]
            out_ref[i, j] = jnp.where(in_lead, 0.0, rest).astype(jnp.bfloat16)
        for c in range(LEAD):
            z = (zr1 if c < HALF else zr2)[at(i, n), at(c % HALF, n)].astype(jnp.bfloat16)

            @pl.when(my_col == c)
            def _():
                out_ref[i, 0] = z
                if i == 0:
                    for r in range(LEAD):

                        @pl.when(my_row == r)
                        def _():
                            if c < HALF:
                                out_ref[0, 0] = l1_ref[at(r, n), at(c, n)].astype(jnp.bfloat16)
                            elif r < HALF:
                                out_ref[0, 0] = jnp.zeros((n, n), jnp.bfloat16)
                            else:
                                out_ref[0, 0] = l2_ref[at(r - HALF, n), at(c - HALF, n)].astype(jnp.bfloat16)


def update(rows, cols, place, tile_mask, mine, from_cols, from_rows, factors):
    tile_rows, tile_cols, n, _ = mine.shape
    width = LEAD * n
    used = tile_cols - 1 if cols == LEAD else tile_cols
    return pl.pallas_call(
        functools.partial(update_kernel, rows, cols),
        out_shape=jax.ShapeDtypeStruct(mine.shape, jnp.bfloat16),
        in_specs=[SMEM, SMEM] + [VMEM] * 7,
        out_specs=VMEM,
        scratch_shapes=[
            pltpu.VMEM((2, tile_rows * n, width), jnp.bfloat16),
            pltpu.VMEM((2, width, used * n), jnp.bfloat16),
            pltpu.VMEM((2, tile_rows * n, width), jnp.bfloat16),
            pltpu.VMEM((2, width, used * n), jnp.bfloat16),
        ],
        compiler_params=pltpu.CompilerParams(vmem_limit_bytes=40 * 2**20),
        cost_estimate=pl.CostEstimate(flops=4 * 10**9, bytes_accessed=2**22, transcendentals=0),
    )(place, tile_mask, mine, from_cols, from_rows, *factors)


def copy_down(value, axis):
    size, index = lax.axis_size(axis), lax.axis_index(axis)
    have = LEAD
    while have < size:
        pairs = [(i, i + have) for i in range(have) if i + have < size]
        value = jnp.where(index >= have, lax.ppermute(value, axis, pairs), value)
        have *= 2
    return value


def swap(value, axis, bit):
    size = lax.axis_size(axis)
    return [value, lax.ppermute(value, axis, [(i, i ^ bit) for i in range(size)])]


def rotate(value, wanted):
    rows, cols = lax.axis_size("row"), lax.axis_size("col")
    parts = [value]
    for shift in range(1, LEAD):
        pairs = [
            (r * cols + c, r * cols + c // LEAD * LEAD + (c + shift) % LEAD)
            for r in range(rows)
            for c in range(cols)
            if wanted(r, c)
        ]
        parts.append(lax.ppermute(value, ("row", "col"), pairs))
    return parts


def on_device(covariance, tile_mask):
    tile_rows, _, tile_cols, _, n, _ = covariance.shape
    rows, cols = lax.axis_size("row"), lax.axis_size("col")
    my_row, my_col = lax.axis_index("row"), lax.axis_index("col")
    mine = covariance.reshape(tile_rows, tile_cols, n, n)
    place = jnp.stack([my_row, my_col]).astype(jnp.int32)
    skip = 1 if cols == LEAD else 0
    lead = copy_down(mine[0, 0], "row")
    lead, across = lax.optimization_barrier((lead, mine[0, skip:]))
    across = copy_down(across, "row")
    parts = rotate(copy_down(lead, "col"), lambda r, c: (r - c) % LEAD < SENT)
    start = (my_col - my_row) % LEAD
    lead = lax.dynamic_slice_in_dim(jnp.stack(parts + parts[: SENT - 1]), start, SENT, 0)
    lead, down = lax.optimization_barrier((lead, mine[:, 0]))
    lead = jnp.stack(swap(lead, "row", 2))
    down = rotate(copy_down(down, "col"), lambda r, c: True)
    lead, across = lax.optimization_barrier((lead, across))
    lead = jnp.stack(swap(lead, "row", 1))
    across = swap(across, "row", 2)
    whole, half = LEAD * n, HALF * n
    l1, k1, s = factor_call(
        factor_first, [SMEM, VMEM], [(whole, half), (half, half), (LEAD - HALF, LEAD - HALF, n, n)], n
    )(place, lead)
    s, *across = lax.optimization_barrier((s, *across))
    across = jnp.stack(swap(jnp.stack(across), "row", 1))
    l2, k2 = factor_call(factor_second, [VMEM] * 3, [(whole - half, whole - half), (whole - half, whole)], n)(s, l1, k1)
    l2, *down = lax.optimization_barrier((l2, *down))
    down = jnp.stack(down)
    out = update(rows, cols, place, tile_mask, mine, down, across, (l1, k1, l2, k2))
    return out.reshape(tile_rows, 1, tile_cols, 1, n, n)


def solution(mesh):
    in_specs = (P(None, "row", None, "col", None, None), P())
    out_specs = P(None, "row", None, "col", None, None)
    return jax.shard_map(on_device, mesh=mesh, in_specs=in_specs, out_specs=out_specs, check_vma=False)
```

time: 71.6 us -> 55.9 us (0.78)
  the two profiles are of different devices: /device:TPU:19 before, /device:TPU:13 now
where the time goes in v2:
time: 55.9 us; the launch traced here: 55.6 us
  starting transfers between devices  23.2 us (42%)
  Pallas kernels  20.4 us (36%)
  waiting for transfers between devices  7.72 us (14%)
  local copies, waits for them, and re-layouts  3.56 us (6%)
    ppermute x6, starting transfers between devices, rotate(): parts.append(lax.ppermute(value, ('row', 'col'), pairs))  13.9 us
    pallas_call x1, Pallas kernels, on_device(): factor_call(factor_first, [SMEM, VMEM], [(whole, half), (half, half), (LE...  8.56 us
    pallas_call x1, Pallas kernels, on_device(): factor_call(factor_second, [VMEM] * 3, [(whole - half, whole - half), (wh...  7.19 us
    ppermute x4, starting transfers between devices, swap(): lax.ppermute(value, axis, [(i, i ^ bit) for i in range(size)])  6.7 us
    pallas_call x1, Pallas kernels, update(): pl.pallas_call(functools.partial(update_kernel, rows, cols), out_shape=ja...  4.6 us
    ppermute x2, waiting for transfers between devices, copy_down(): value = jnp.where(index >= have, lax.ppermute(value, axis, pairs), value)  3.44 us
    ppermute x4, waiting for transfers between devices, swap(): lax.ppermute(value, axis, [(i, i ^ bit) for i in range(size)])  3.36 us
    ppermute x2, starting transfers between devices, copy_down(): value = jnp.where(index >= have, lax.ppermute(value, axis, pairs), value)  2.57 us
  transfers between devices with their start and end apart: 12, of which 4 were waited for; matrix products, arithmetic and copies ran while one was open for 4% of the time, Pallas kernels for 28%

profile of v2, /device:TPU:13, one launch (start us, length us, event | category | flops | bytes accessed | tf_op | source)
XLA Modules:
  0.0 55.6 jit_solution(1326832044386983784)
XLA Ops:
  0.0 0.9 %slice_bitcast_fusion.2 = f32[128,128]{1,0:T(8,128)S(1)} fusion(f32[3,6,128,128]{3,2,1,0:T(8,128)} %bitcast.37), kind=kLoop, calls=%fused_computation.8 | loop fusion | bytes 131072 | tf_op jit(solution)/shard_map/squeeze | solution.py:282
  0.9 1.3 %collective-permute-start = (f32[128,128]{1,0:T(8,128)S(1)}, f32[128,128]{1,0:T(8,128)S(1)}, u32[]{:S(2)}, u32[]{:S(2)}) collective-permute-start(f32[128,128]{1,0:T(8,128)S(1)} %slice_bitcast_fusion.2), channel_id=1, source_target_pairs={{0,16},{4,20},{8,24},{12,28},{1,17},{5,21},{9,25},{13,29},{2,18},{... | collective-permute-start | bytes 196616 | tf_op jit(solution)/shard_map/ppermute | solution.py:251
  2.2 1.0 %slice_bitcast_fusion = f32[5,128,128]{2,1,0:T(8,128)S(1)} fusion(f32[3,6,128,128]{3,2,1,0:T(8,128)} %bitcast.38), kind=kLoop, calls=%fused_computation.5 | loop fusion | bytes 655360 | tf_op jit(solution)/shard_map/squeeze | solution.py:283
  3.2 0.9 %slice_bitcast_fusion.1 = f32[3,128,128]{2,1,0:T(8,128)S(1)} fusion(f32[3,6,128,128]{3,2,1,0:T(8,128)} %bitcast.39), kind=kLoop, calls=%fused_computation.6 | loop fusion | bytes 393216 | tf_op jit(solution)/shard_map/squeeze | solution.py:288
  4.2 1.7 %collective-permute-done = f32[128,128]{1,0:T(8,128)S(1)} collective-permute-done((f32[128,128]{1,0:T(8,128)S(1)}, f32[128,128]{1,0:T(8,128)S(1)}, u32[]{:S(2)}, u32[]{:S(2)}) %collective-permute-start) | collective-permute-done | bytes 65568 | tf_op jit(solution)/shard_map/ppermute | solution.py:251
  6.0 3.2 %collective-permute-start.1 = (f32[128,128]{1,0:T(8,128)S(1)}, f32[128,128]{1,0:T(8,128)S(1)}, u32[]{:S(2)}, u32[]{:S(2)}) collective-permute-start(f32[128,128]{1,0:T(8,128)S(1)} %broadcast_select_fusion.1), channel_id=1, source_target_pairs={{0,1},{2,3},{3,0},{4,5},{5,6},{7,4},{8,9},{9,10},{10,11},{13,14},{... | collective-permute-start | bytes 196616 | tf_op jit(solution)/shard_map/ppermute | solution.py:271
  9.2 2.9 %collective-permute-start.2 = (f32[128,128]{1,0:T(8,128)S(1)}, f32[128,128]{1,0:T(8,128)S(1)}, u32[]{:S(2)}, u32[]{:S(2)}) collective-permute-start(f32[128,128]{1,0:T(8,128)S(1)} %broadcast_select_fusion.1), channel_id=1, source_target_pairs={{0,2},{2,0},{3,1},{4,6},{5,7},{7,5},{8,10},{9,11},{10,8},{13,15},{... | collective-permute-start | bytes 196616 | tf_op jit(solution)/shard_map/ppermute | solution.py:271
  12.1 1.5 %collective-permute-start.3 = (f32[128,128]{1,0:T(8,128)S(1)}, f32[128,128]{1,0:T(8,128)S(1)}, u32[]{:S(2)}, u32[]{:S(2)}) collective-permute-start(f32[128,128]{1,0:T(8,128)S(1)} %broadcast_select_fusion.1), channel_id=1, source_target_pairs={{0,3},{2,1},{3,2},{4,7},{5,4},{7,6},{8,11},{9,8},{10,9},{13,12},{1... | collective-permute-start | bytes 196616 | tf_op jit(solution)/shard_map/ppermute | solution.py:271
  13.6 1.3 %collective-permute-start.5 = (f32[5,128,128]{2,1,0:T(8,128)S(1)}, f32[5,128,128]{2,1,0:T(8,128)S(1)}, u32[]{:S(2)}, u32[]{:S(2)}) collective-permute-start(f32[5,128,128]{2,1,0:T(8,128)S(1)} %slice_bitcast_fusion), channel_id=1, source_target_pairs={{0,16},{4,20},{8,24},{12,28},{1,17},{5,21},{9,25},{13,29},{2,18},{... | collective-permute-start | bytes 983048 | tf_op jit(solution)/shard_map/ppermute | solution.py:251
  14.9 0.9 %collective-permute-done.2 = f32[128,128]{1,0:T(8,128)S(1)} collective-permute-done((f32[128,128]{1,0:T(8,128)S(1)}, f32[128,128]{1,0:T(8,128)S(1)}, u32[]{:S(2)}, u32[]{:S(2)}) %collective-permute-start.2) | collective-permute-done | bytes 65568 | tf_op jit(solution)/shard_map/ppermute | solution.py:271
  15.9 2.8 %collective-permute-start.4 = (f32[3,128,128]{2,1,0:T(8,128)S(1)}, f32[3,128,128]{2,1,0:T(8,128)S(1)}, u32[]{:S(2)}, u32[]{:S(2)}) collective-permute-start(f32[3,128,128]{2,1,0:T(8,128)S(1)} %constant_dynamic-slice_fusion), channel_id=1, source_target_pairs={{0,8},{4,12},{8,0},{12,4},{16,24},{20,28},{24,16},{28,20},{1,9},{5... | collective-permute-start | bytes 589832 | tf_op jit(solution)/shard_map/ppermute | solution.py:258
  18.7 3.4 %collective-permute-done.4 = f32[3,128,128]{2,1,0:T(8,128)S(1)} collective-permute-done((f32[3,128,128]{2,1,0:T(8,128)S(1)}, f32[3,128,128]{2,1,0:T(8,128)S(1)}, u32[]{:S(2)}, u32[]{:S(2)}) %collective-permute-start.4) | collective-permute-done | bytes 196640 | tf_op jit(solution)/shard_map/ppermute | solution.py:258
  22.1 1.7 %collective-permute-done.5 = f32[5,128,128]{2,1,0:T(8,128)S(1)} collective-permute-done((f32[5,128,128]{2,1,0:T(8,128)S(1)}, f32[5,128,128]{2,1,0:T(8,128)S(1)}, u32[]{:S(2)}, u32[]{:S(2)}) %collective-permute-start.5) | collective-permute-done | bytes 327712 | tf_op jit(solution)/shard_map/ppermute | solution.py:251
  23.8 1.6 %collective-permute-start.6 = (f32[2,3,128,128]{3,2,1,0:T(8,128)S(1)}, f32[2,3,128,128]{3,2,1,0:T(8,128)S(1)}, u32[]{:S(2)}, u32[]{:S(2)}) collective-permute-start(f32[2,3,128,128]{3,2,1,0:T(8,128)S(1)} %pad_maximum_fusion.4), channel_id=1, source_target_pairs={{0,4},{4,0},{8,12},{12,8},{16,20},{20,16},{24,28},{28,24},{1,5},{5... | collective-permute-start | bytes 1179656 | tf_op jit(solution)/shard_map/ppermute | solution.py:258
  25.5 0.1 pad_add_fusion.place_ref
  25.5 3.2 %collective-permute-start.10 = (f32[3,128,128]{2,1,0:T(8,128)S(1)}, f32[3,128,128]{2,1,0:T(8,128)S(1)}, u32[]{:S(2)}, u32[]{:S(2)}) collective-permute-start(f32[3,128,128]{2,1,0:T(8,128)S(1)} %slice_bitcast_fusion.1), channel_id=1, source_target_pairs={{0,3},{1,0},{2,1},{3,2},{4,7},{5,4},{6,5},{7,6},{8,11},{9,8},{10,9... | collective-permute-start | bytes 589832 | tf_op jit(solution)/shard_map/ppermute | solution.py:271
  28.8 3.1 %collective-permute-start.9 = (f32[3,128,128]{2,1,0:T(8,128)S(1)}, f32[3,128,128]{2,1,0:T(8,128)S(1)}, u32[]{:S(2)}, u32[]{:S(2)}) collective-permute-start(f32[3,128,128]{2,1,0:T(8,128)S(1)} %slice_bitcast_fusion.1), channel_id=1, source_target_pairs={{0,2},{1,3},{2,0},{3,1},{4,6},{5,7},{6,4},{7,5},{8,10},{9,11},{10,... | collective-permute-start | bytes 589832 | tf_op jit(solution)/shard_map/ppermute | solution.py:271
  31.9 1.1 %collective-permute-start.7 = (f32[5,128,128]{2,1,0:T(8,128)S(1)}, f32[5,128,128]{2,1,0:T(8,128)S(1)}, u32[]{:S(2)}, u32[]{:S(2)}) collective-permute-start(f32[5,128,128]{2,1,0:T(8,128)S(1)} %broadcast_select_fusion), channel_id=1, source_target_pairs={{0,8},{4,12},{8,0},{12,4},{16,24},{20,28},{24,16},{28,20},{1,9},{5... | collective-permute-start | bytes 983048 | tf_op jit(solution)/shard_map/ppermute | solution.py:258
  33.0 0.0 collective-permute-done.6
  33.0 0.1 pad_maximum_fusion.1.a_ref
  33.0 8.6 %shard_map.28 = (f32[512,256]{1,0:T(8,128)S(1)}, f32[256,256]{1,0:T(8,128)S(1)}, f32[2,2,128,128]{3,2,1,0:T(8,128)S(1)}) custom-call(s32[2]{0:T(128)S(1)} %pad_add_fusion.place_ref, f32[2,2,3,128,128]{4,3,2,1,0:T(8,128)S(1)} %pad_maximum_fusion.1.a_ref), custom_call_target="tpu_custom_call" | custom-call | flops 8000000000 | bytes 1048576 | tf_op jit(solution)/shard_map/pallas_call | solution.py:295
  41.6 0.0 collective-permute-done.7
  41.6 0.1 fusion
  41.8 1.2 %collective-permute-start.11 = (f32[2,5,128,128]{3,2,1,0:T(8,128)S(1)}, f32[2,5,128,128]{3,2,1,0:T(8,128)S(1)}, u32[]{:S(2)}, u32[]{:S(2)}) collective-permute-start(f32[2,5,128,128]{3,2,1,0:T(8,128)S(1)} %get-tuple-element.44), channel_id=1, source_target_pairs={{0,4},{4,0},{8,12},{12,8},{16,20},{20,16},{24,28},{28,24},{1,5},{5... | collective-permute-start | bytes 1966088 | tf_op jit(solution)/shard_map/ppermute | solution.py:258
  43.0 7.2 %shard_map.29 = (f32[256,256]{1,0:T(8,128)S(1)}, f32[256,512]{1,0:T(8,128)S(1)}) custom-call(f32[2,2,128,128]{3,2,1,0:T(8,128)S(1)} %get-tuple-element.30.s_in_ref, f32[512,256]{1,0:T(8,128)S(1)} %get-tuple-element.31.l_in_ref.l1_ref, f32[256,256]{1,0:T(8,128)S(1)} %get-tuple-element.32.k_in_ref.k1_ref), custom_call_target="tpu_custom_call" | custom-call | flops 8000000000 | bytes 1048576 | tf_op jit(solution)/shard_map/pallas_call | solution.py:300
  50.2 0.0 collective-permute-done.10
  50.2 0.0 collective-permute-done.8
  50.2 0.1 pad_maximum_fusion.2.xr_ref
  50.3 0.0 copy-start.1
  50.3 0.1 pad_maximum_fusion.xc_ref
  50.4 0.6 %copy-done.1 = s32[24,24]{1,0:T(8,128)S(1)} copy-done((s32[24,24]{1,0:T(8,128)S(1)}, s32[24,24]{1,0:T(8,128)}, u32[]{:S(2)}) %copy-start.1) | copy-done | bytes 2328
  51.0 4.6 %shard_map.30 = bf16[3,6,128,128]{3,2,1,0:T(8,128)(2,1)} custom-call(s32[2]{0:T(128)S(1)} %pad_add_fusion.place_ref, s32[24,24]{1,0:T(8,128)S(1)} %copy-done.1, f32[3,6,128,128]{3,2,1,0:T(8,128)S(1)} %bitcast.41, f32[4,3,128,128]{3,2,1,0:T(8,128)S(1)} %pad_maximum_fusion.2.xr_ref, f32[2,2,5,128,128]{4,3,2,1,0:T(8,128)S(1)} %pad_maximum_fusion.xc_ref, ...), custom_call_target="tpu_custom_call" | custom-call | flops 4000000000 | bytes 4194304 | tf_op jit(solution)/shard_map/pallas_call | solution.py:230
  (17 shorter events, 0.2 us)
Async XLA Ops:
  0.0 5.9 %copy-start = (f32[3,1,6,1,128,128]{5,4,3,2,1,0:T(8,128)S(1)}, f32[3,1,6,1,128,128]{5,4,3,2,1,0:T(8,128)}, u32[]{:S(2)}) copy-start(f32[3,1,6,1,128,128]{5,4,3,2,1,0:T(8,128)} %param.2) | copy-start | bytes 3538948
  0.9 5.0 %collective-permute-start = (f32[128,128]{1,0:T(8,128)S(1)}, f32[128,128]{1,0:T(8,128)S(1)}, u32[]{:S(2)}, u32[]{:S(2)}) collective-permute-start(f32[128,128]{1,0:T(8,128)S(1)} %slice_bitcast_fusion.2), channel_id=1, source_target_pairs={{0,16},{4,20},{8,24},{12,28},{1,17},{5,21},{9,25},{13,29},{2,18},{... | collective-permute-start | bytes 196616 | tf_op jit(solution)/shard_map/ppermute | solution.py:251
  6.0 8.9 %collective-permute-start.1 = (f32[128,128]{1,0:T(8,128)S(1)}, f32[128,128]{1,0:T(8,128)S(1)}, u32[]{:S(2)}, u32[]{:S(2)}) collective-permute-start(f32[128,128]{1,0:T(8,128)S(1)} %broadcast_select_fusion.1), channel_id=1, source_target_pairs={{0,1},{2,3},{3,0},{4,5},{5,6},{7,4},{8,9},{9,10},{10,11},{13,14},{... | collective-permute-start | bytes 196616 | tf_op jit(solution)/shard_map/ppermute | solution.py:271
  9.2 6.6 %collective-permute-start.2 = (f32[128,128]{1,0:T(8,128)S(1)}, f32[128,128]{1,0:T(8,128)S(1)}, u32[]{:S(2)}, u32[]{:S(2)}) collective-permute-start(f32[128,128]{1,0:T(8,128)S(1)} %broadcast_select_fusion.1), channel_id=1, source_target_pairs={{0,2},{2,0},{3,1},{4,6},{5,7},{7,5},{8,10},{9,11},{10,8},{13,15},{... | collective-permute-start | bytes 196616 | tf_op jit(solution)/shard_map/ppermute | solution.py:271
  12.1 3.8 %collective-permute-start.3 = (f32[128,128]{1,0:T(8,128)S(1)}, f32[128,128]{1,0:T(8,128)S(1)}, u32[]{:S(2)}, u32[]{:S(2)}) collective-permute-start(f32[128,128]{1,0:T(8,128)S(1)} %broadcast_select_fusion.1), channel_id=1, source_target_pairs={{0,3},{2,1},{3,2},{4,7},{5,4},{7,6},{8,11},{9,8},{10,9},{13,12},{1... | collective-permute-start | bytes 196616 | tf_op jit(solution)/shard_map/ppermute | solution.py:271
  13.6 10.2 %collective-permute-start.5 = (f32[5,128,128]{2,1,0:T(8,128)S(1)}, f32[5,128,128]{2,1,0:T(8,128)S(1)}, u32[]{:S(2)}, u32[]{:S(2)}) collective-permute-start(f32[5,128,128]{2,1,0:T(8,128)S(1)} %slice_bitcast_fusion), channel_id=1, source_target_pairs={{0,16},{4,20},{8,24},{12,28},{1,17},{5,21},{9,25},{13,29},{2,18},{... | collective-permute-start | bytes 983048 | tf_op jit(solution)/shard_map/ppermute | solution.py:251
  15.9 6.1 %collective-permute-start.4 = (f32[3,128,128]{2,1,0:T(8,128)S(1)}, f32[3,128,128]{2,1,0:T(8,128)S(1)}, u32[]{:S(2)}, u32[]{:S(2)}) collective-permute-start(f32[3,128,128]{2,1,0:T(8,128)S(1)} %constant_dynamic-slice_fusion), channel_id=1, source_target_pairs={{0,8},{4,12},{8,0},{12,4},{16,24},{20,28},{24,16},{28,20},{1,9},{5... | collective-permute-start | bytes 589832 | tf_op jit(solution)/shard_map/ppermute | solution.py:258
  23.8 9.1 %collective-permute-start.6 = (f32[2,3,128,128]{3,2,1,0:T(8,128)S(1)}, f32[2,3,128,128]{3,2,1,0:T(8,128)S(1)}, u32[]{:S(2)}, u32[]{:S(2)}) collective-permute-start(f32[2,3,128,128]{3,2,1,0:T(8,128)S(1)} %pad_maximum_fusion.4), channel_id=1, source_target_pairs={{0,4},{4,0},{8,12},{12,8},{16,20},{20,16},{24,28},{28,24},{1,5},{5... | collective-permute-start | bytes 1179656 | tf_op jit(solution)/shard_map/ppermute | solution.py:258
  25.5 24.6 %collective-permute-start.10 = (f32[3,128,128]{2,1,0:T(8,128)S(1)}, f32[3,128,128]{2,1,0:T(8,128)S(1)}, u32[]{:S(2)}, u32[]{:S(2)}) collective-permute-start(f32[3,128,128]{2,1,0:T(8,128)S(1)} %slice_bitcast_fusion.1), channel_id=1, source_target_pairs={{0,3},{1,0},{2,1},{3,2},{4,7},{5,4},{6,5},{7,6},{8,11},{9,8},{10,9... | collective-permute-start | bytes 589832 | tf_op jit(solution)/shard_map/ppermute | solution.py:271
  28.8 21.4 %collective-permute-start.8 = (f32[3,128,128]{2,1,0:T(8,128)S(1)}, f32[3,128,128]{2,1,0:T(8,128)S(1)}, u32[]{:S(2)}, u32[]{:S(2)}) collective-permute-start(f32[3,128,128]{2,1,0:T(8,128)S(1)} %slice_bitcast_fusion.1), channel_id=1, source_target_pairs={{0,1},{1,2},{2,3},{3,0},{4,5},{5,6},{6,7},{7,4},{8,9},{9,10},{10,1... | collective-permute-start | bytes 589832 | tf_op jit(solution)/shard_map/ppermute | solution.py:271
  28.8 21.4 %collective-permute-start.9 = (f32[3,128,128]{2,1,0:T(8,128)S(1)}, f32[3,128,128]{2,1,0:T(8,128)S(1)}, u32[]{:S(2)}, u32[]{:S(2)}) collective-permute-start(f32[3,128,128]{2,1,0:T(8,128)S(1)} %slice_bitcast_fusion.1), channel_id=1, source_target_pairs={{0,2},{1,3},{2,0},{3,1},{4,6},{5,7},{6,4},{7,5},{8,10},{9,11},{10,... | collective-permute-start | bytes 589832 | tf_op jit(solution)/shard_map/ppermute | solution.py:271
  31.9 9.7 %collective-permute-start.7 = (f32[5,128,128]{2,1,0:T(8,128)S(1)}, f32[5,128,128]{2,1,0:T(8,128)S(1)}, u32[]{:S(2)}, u32[]{:S(2)}) collective-permute-start(f32[5,128,128]{2,1,0:T(8,128)S(1)} %broadcast_select_fusion), channel_id=1, source_target_pairs={{0,8},{4,12},{8,0},{12,4},{16,24},{20,28},{24,16},{28,20},{1,9},{5... | collective-permute-start | bytes 983048 | tf_op jit(solution)/shard_map/ppermute | solution.py:258
  41.8 8.5 %collective-permute-start.11 = (f32[2,5,128,128]{3,2,1,0:T(8,128)S(1)}, f32[2,5,128,128]{3,2,1,0:T(8,128)S(1)}, u32[]{:S(2)}, u32[]{:S(2)}) collective-permute-start(f32[2,5,128,128]{3,2,1,0:T(8,128)S(1)} %get-tuple-element.44), channel_id=1, source_target_pairs={{0,4},{4,0},{8,12},{12,8},{16,20},{20,16},{24,28},{28,24},{1,5},{5... | collective-permute-start | bytes 1966088 | tf_op jit(solution)/shard_map/ppermute | solution.py:258
  50.3 0.7 %copy-start.1 = (s32[24,24]{1,0:T(8,128)S(1)}, s32[24,24]{1,0:T(8,128)}, u32[]{:S(2)}) copy-start(s32[24,24]{1,0:T(8,128)} %mask_ref.1) | copy-start | bytes 6916

commit v3 on v2

v3 whole, which is shorter than its diff:
```python
import functools

import jax
import jax.numpy as jnp
from jax import lax
from jax.experimental import pallas as pl
from jax.experimental.pallas import tpu as pltpu
from jax.sharding import PartitionSpec as P

LEAD = 4
HALF = 2
COST = (4, 4, 4, 8)
GROUP = 16
HIGHEST = lax.Precision.HIGHEST
VMEM = pl.BlockSpec(memory_space=pltpu.VMEM)
SMEM = pl.BlockSpec(memory_space=pltpu.SMEM)
ROW_BY_COL = (((1,), (0,)), ((), ()))
ROW_BY_ROW = (((1,), (1,)), ((), ()))


def dot(a, b, dims=ROW_BY_COL):
    return lax.dot_general(a, b, dims, precision=HIGHEST, preferred_element_type=jnp.float32)


def dot_t(a, b):
    return dot(a, b, ROW_BY_ROW)


def split(a):
    high = a.astype(jnp.bfloat16)
    return high, (a - high.astype(jnp.float32)).astype(jnp.bfloat16)


def dot_3(a, b, dims=ROW_BY_COL):
    def part(x, y):
        return lax.dot_general(x, y, dims, preferred_element_type=jnp.float32)

    return part(a[0], b[0]) + (part(a[0], b[1]) + part(a[1], b[0]))


def twice(a):
    return jnp.concatenate([a, a], axis=1)


def factor_tile(tile, u_ref, w_ref):
    n = tile.shape[0]
    row = lax.broadcasted_iota(jnp.int32, (n, n), 0)
    col = lax.broadcasted_iota(jnp.int32, (n, n), 1)
    w_ref[:, :n] = tile
    w_ref[:, n:] = jnp.where(row == col, 1.0, 0.0).astype(jnp.float32)
    group_row = lax.broadcasted_iota(jnp.int32, (GROUP, n), 0)
    group = w_ref[:GROUP, :]
    for first in range(0, n, GROUP):
        after = first + GROUP
        column = [jnp.broadcast_to(group[:, first + k : first + k + 1], (GROUP, n)) for k in range(GROUP)]
        if after < n:
            ahead = w_ref[after : after + GROUP, :]
            ahead_column = [jnp.broadcast_to(ahead[:, first + k : first + k + 1], (GROUP, n)) for k in range(GROUP)]
        pivots = inverses = jnp.ones((GROUP, n), jnp.float32)
        for k in range(GROUP):
            here = group_row == k
            pivot = jnp.broadcast_to(column[k][k : k + 1, :], (GROUP, n))
            inverse = 1.0 / pivot
            factors = jnp.where(here, 0.0, column[k] * inverse)
            pivots = jnp.where(here, pivot, pivots)
            inverses = jnp.where(here, inverse, inverses)
            u_ref[first + k : first + k + 1, :] = group[k : k + 1, :]
            for m in range(k + 1, GROUP):
                column[m] = column[m] - factors * jnp.broadcast_to(column[m][k : k + 1, :], (GROUP, n))
            group = group - twice(factors) * jnp.broadcast_to(group[k : k + 1, :], (GROUP, 2 * n))
        u_ref[first:after, :] = u_ref[first:after, :] * twice(lax.rsqrt(pivots))
        if after < n:
            reduced = group * twice(inverses)
            terms = [
                twice(ahead_column[k]) * jnp.broadcast_to(reduced[k : k + 1, :], (GROUP, 2 * n)) for k in range(GROUP)
            ]
            group = (ahead - sum(terms[2::2], terms[0])) - sum(terms[3::2], terms[1])
            if after + GROUP < n:
                rest = w_ref[after + GROUP :, :]
                w_ref[after + GROUP :, :] = rest - dot(rest[:, first:after], reduced)


def finish_tile(u):
    n = u.shape[0]
    row = lax.broadcasted_iota(jnp.int32, (n, n), 0)
    col = lax.broadcasted_iota(jnp.int32, (n, n), 1)
    return jnp.where(col >= row, u[:, :n], 0.0).T, u[:, n:]


def at(i, n):
    return slice(i * n, (i + 1) * n)


def gather_lead(place_ref, a_ref, s_ref):
    my_row, my_col = place_ref[0], place_ref[1]
    my_pair = (my_row >> 1) & 1

    def own(i, j):
        return 4 * ((i ^ my_row) & 1) + ((j ^ my_col) & (LEAD - 1))

    def far(i, j):
        return 8 + 2 * ((i ^ my_row) & 1) + ((j ^ my_col) & 1)

    for i in range(LEAD):
        for j in range(i + 1):
            if i // 2 == j // 2:
                s_ref[i, j] = a_ref[jnp.where(my_pair == i // 2, own(i, j), far(i, j))]
            else:
                tile = a_ref[jnp.where(my_pair == i // 2, own(i, j), own(j, i))]
                s_ref[i, j] = jnp.where(my_pair == i // 2, tile, tile.T)


def factor_kernel(b, *refs):
    refs = list(refs)
    left = LEAD - b
    if b == 0:
        place_ref, a_ref = refs[:2]
        del refs[:2]
        l_in, k_in = [], []
    else:
        s_in = refs.pop(0)
        l_in, k_in = refs[:b], refs[b : 2 * b]
        del refs[: 2 * b]
    if b < LEAD - 1:
        l_ref, k_ref, s_out, w_ref, u_ref, s_ref = refs
    else:
        l_ref, k_ref, w_ref, u_ref, s_ref = refs
    n = l_ref.shape[-1]
    if b == 0:
        gather_lead(place_ref, a_ref, s_ref)
    else:
        s_ref[0, 0] = s_in[0, 0]
        last = l_in[b - 1]
        for i in range(1, left):
            for j in range(i + 1):
                s_ref[i, j] = s_in[i, j] - dot_t(last[at(i + 1, n), :], last[at(j + 1, n), :])
        total = dot(last[at(1, n), :], k_in[b - 1][...])
        for j in range(b - 1):
            part = dot(l_in[j][at(b - j, n), :], k_in[j][...])
            pad = jnp.zeros((n, (b - 1 - j) * n), jnp.float32)
            total = total + jnp.concatenate([part, pad], axis=1)
    factor_tile(s_ref[0, 0], u_ref, w_ref)
    lower, inverse = finish_tile(u_ref[...])
    l_ref[at(0, n), :] = lower
    for i in range(1, left):
        l_ref[at(i, n), :] = dot_t(s_ref[i, 0], inverse)
    if b < LEAD - 1:
        for i in range(1, left):
            for j in range(1, i + 1):
                s_out[i - 1, j - 1] = s_ref[i, j]
        s_out[0, 0] = s_ref[1, 1] - dot_t(l_ref[at(1, n), :], l_ref[at(1, n), :])
    if b > 0:
        k_ref[:, : b * n] = -dot(inverse, total)
    k_ref[:, b * n :] = inverse


def factor_column(b, n, place, first, l_cols, k_rows):
    left = LEAD - b
    shapes = [(left * n, n), (n, (b + 1) * n)]
    if b < LEAD - 1:
        shapes.append((left - 1, left - 1, n, n))
    args = [place, first] if b == 0 else [first, *l_cols, *k_rows]
    return pl.pallas_call(
        functools.partial(factor_kernel, b),
        out_shape=[jax.ShapeDtypeStruct(shape, jnp.float32) for shape in shapes],
        in_specs=[SMEM, VMEM] if b == 0 else [VMEM] * len(args),
        out_specs=[VMEM] * len(shapes),
        scratch_shapes=[
            pltpu.VMEM((n, 2 * n), jnp.float32),
            pltpu.VMEM((n, 2 * n), jnp.float32),
            pltpu.VMEM((left, left, n, n), jnp.float32),
        ],
        compiler_params=pltpu.CompilerParams(vmem_limit_bytes=32 * 2**20),
        cost_estimate=pl.CostEstimate(flops=COST[b] * 10**9, bytes_accessed=2**20, transcendentals=0),
    )(*args)


def update_kernel(
    rows, cols, place_ref, mask_ref, a_ref, xr_ref, xc_ref, *refs
):
    l_cols, k_rows = refs[:LEAD], refs[LEAD : 2 * LEAD]
    out_ref, x_ref, y_ref, zr_ref, zc_ref, k_ref = refs[2 * LEAD :]
    tile_rows, tile_cols, n, _ = a_ref.shape
    my_row, my_col = place_ref[0], place_ref[1]
    skip = 1 if cols == LEAD else 0
    half = HALF * n
    every = slice(None)

    def mask(i, j):
        return mask_ref[i, j].astype(jnp.float32)

    def pair(ref, rows_at, cols_at):
        return ref[0, rows_at, cols_at], ref[1, rows_at, cols_at]

    def put(ref, rows_at, cols_at, value):
        ref[0, rows_at, cols_at], ref[1, rows_at, cols_at] = split(value)

    for k in range(LEAD):
        for i in range(tile_rows):
            put(x_ref, at(i, n), at(k, n), xr_ref[(my_col ^ k) & (LEAD - 1), i] * mask(i * rows + my_row, k))
        apart = (my_row ^ k) & (LEAD - 1)
        for j in range(skip, tile_cols):
            put(y_ref, at(k, n), at(j - skip, n), xc_ref[apart & 1, apart >> 1, j - skip] * mask(k, j * cols + my_col))
    for b in range(LEAD):
        put(k_ref, at(b, n), slice(0, (b + 1) * n), k_rows[b][...])
        if b % HALF + 1 < HALF:
            k_ref[:, at(b, n), (b + 1) * n : (b // HALF + 1) * half] = jnp.zeros((2, n, n), jnp.bfloat16)
    head, tail = slice(0, half), slice(half, LEAD * n)
    k1, k2 = pair(k_ref, head, head), pair(k_ref, tail, every)
    zr1 = dot_3(pair(x_ref, every, head), k1, ROW_BY_ROW)
    zr2 = dot_3(pair(x_ref, every, every), k2, ROW_BY_ROW)
    put(zr_ref, every, head, zr1)
    put(zr_ref, every, tail, zr2)
    put(zc_ref, head, every, dot_3(k1, pair(y_ref, head, every)))
    put(zc_ref, tail, every, dot_3(k2, pair(y_ref, every, every)))
    for i in range(tile_rows):
        in_lead = jnp.logical_and(i == 0, my_row < LEAD)
        product = dot_3(pair(zr_ref, at(i, n), every), pair(zc_ref, every, every))
        for j in range(skip, tile_cols):
            rest = a_ref[i, j] * mask(i * rows + my_row, j * cols + my_col) - product[:, at(j - skip, n)]
            out_ref[i, j] = jnp.where(in_lead, 0.0, rest).astype(jnp.bfloat16)
        for c in range(LEAD):
            z = (zr1 if c < HALF else zr2)[at(i, n), at(c % HALF, n)].astype(jnp.bfloat16)

            @pl.when(my_col == c)
            def _():
                out_ref[i, 0] = z
                if i == 0:
                    for r in range(LEAD):

                        @pl.when(my_row == r)
                        def _():
                            if r >= c:
                                out_ref[0, 0] = l_cols[c][at(r - c, n), :].astype(jnp.bfloat16)
                            else:
                                out_ref[0, 0] = jnp.zeros((n, n), jnp.bfloat16)


def update(rows, cols, place, tile_mask, mine, from_cols, from_rows, factors):
    tile_rows, tile_cols, n, _ = mine.shape
    width = LEAD * n
    used = tile_cols - 1 if cols == LEAD else tile_cols
    return pl.pallas_call(
        functools.partial(update_kernel, rows, cols),
        out_shape=jax.ShapeDtypeStruct(mine.shape, jnp.bfloat16),
        in_specs=[SMEM, SMEM] + [VMEM] * (3 + 2 * LEAD),
        out_specs=VMEM,
        scratch_shapes=[
            pltpu.VMEM((2, tile_rows * n, width), jnp.bfloat16),
            pltpu.VMEM((2, width, used * n), jnp.bfloat16),
            pltpu.VMEM((2, tile_rows * n, width), jnp.bfloat16),
            pltpu.VMEM((2, width, used * n), jnp.bfloat16),
            pltpu.VMEM((2, width, width), jnp.bfloat16),
        ],
        compiler_params=pltpu.CompilerParams(vmem_limit_bytes=40 * 2**20),
        cost_estimate=pl.CostEstimate(flops=4 * 10**9, bytes_accessed=2**22, transcendentals=0),
    )(place, tile_mask, mine, from_cols, from_rows, *factors)


def copy_down(value, axis):
    size, index = lax.axis_size(axis), lax.axis_index(axis)
    have = LEAD
    while have < size:
        if 2 * have == size:
            pairs = [(i, i ^ have) for i in range(size)]
        else:
            pairs = [(i, i + have) for i in range(have) if i + have < size]
        value = jnp.where(index >= have, lax.ppermute(value, axis, pairs), value)
        have *= 2
    return value


def swap(value, axis, bit):
    size = lax.axis_size(axis)
    return [value, lax.ppermute(value, axis, [(i, i ^ bit) for i in range(size)])]


def exchange(value, axis):
    size = lax.axis_size(axis)
    return [value] + [lax.ppermute(value, axis, [(i, i ^ s) for i in range(size)]) for s in range(1, LEAD)]


def on_device(covariance, tile_mask):
    tile_rows, _, tile_cols, _, n, _ = covariance.shape
    rows, cols = lax.axis_size("row"), lax.axis_size("col")
    my_row, my_col = lax.axis_index("row"), lax.axis_index("col")
    mine = covariance.reshape(tile_rows, tile_cols, n, n)
    place = jnp.stack([my_row, my_col]).astype(jnp.int32)
    skip = 1 if cols == LEAD else 0
    lead = copy_down(mine[0, 0], "row")
    _, across = lax.optimization_barrier((lead, mine[0, skip:]))
    across = copy_down(across, "row")
    lead = jnp.stack(exchange(copy_down(lead, "col"), "col"))
    _, down = lax.optimization_barrier((lead, mine[:, 0]))
    down = exchange(copy_down(down, "col"), "col")
    part = lax.dynamic_slice_in_dim(lead, (my_row ^ my_col) & 2, 2)
    lead = jnp.concatenate([lead, swap(lead, "row", 1)[1], swap(part, "row", 2)[1], swap(part, "row", 3)[1]])
    lead, across = lax.optimization_barrier((lead, across))
    across = swap(across, "row", 2)
    l_cols, k_rows = [], []
    state = lead
    for b in range(LEAD):
        column, row, *state = factor_column(b, n, place, state, l_cols, k_rows)
        l_cols.append(column)
        k_rows.append(row)
        if b == LEAD - 1:
            break
        (state,) = state
        if b == LEAD - 2:
            state, *across = lax.optimization_barrier((state, *across))
            across = swap(jnp.stack(across), "row", 1)
    row, *moved = lax.optimization_barrier((k_rows[-1], *across, *down))
    k_rows[-1] = row
    across, down = jnp.stack(moved[:2]), jnp.stack(moved[2:])
    out = update(rows, cols, place, tile_mask, mine, down, across, (*l_cols, *k_rows))
    return out.reshape(tile_rows, 1, tile_cols, 1, n, n)


def solution(mesh):
    in_specs = (P(None, "row", None, "col", None, None), P())
    out_specs = P(None, "row", None, "col", None, None)
    return jax.shard_map(on_device, mesh=mesh, in_specs=in_specs, out_specs=out_specs, check_vma=False)
```

time: 55.9 us -> 46 us (0.82)
  the two profiles are of different devices: /device:TPU:13 before, /device:TPU:0 now
where the time goes in v3:
time: 46 us; the launch traced here: 45.8 us
  Pallas kernels  19.7 us (43%)
  starting transfers between devices  15.1 us (33%)
  waiting for transfers between devices  6.8 us (15%)
  local copies, waits for them, and re-layouts  3.6 us (8%)
    pallas_call x4, Pallas kernels, factor_column(): pl.pallas_call(functools.partial(factor_kernel, b), out_shape=[jax.ShapeD...  15.1 us
    ppermute x6, starting transfers between devices, exchange(): lax.ppermute(value, axis, [(i, i ^ s) for i in range(size)])  8.33 us
    ppermute x2, starting transfers between devices, copy_down(): value = jnp.where(index >= have, lax.ppermute(value, axis, pairs), value)  4.63 us
    pallas_call x1, Pallas kernels, update(): pl.pallas_call(functools.partial(update_kernel, rows, cols), out_shape=ja...  4.61 us
    ppermute x5, waiting for transfers between devices, swap(): lax.ppermute(value, axis, [(i, i ^ bit) for i in range(size)])  3.59 us
    ppermute x6, waiting for transfers between devices, exchange(): lax.ppermute(value, axis, [(i, i ^ s) for i in range(size)])  2.92 us
    ppermute x5, starting transfers between devices, swap(): lax.ppermute(value, axis, [(i, i ^ bit) for i in range(size)])  2.17 us
    squeeze x1, local copies, waits for them, and re-layouts, on_device(): _, across = lax.optimization_barrier((lead, mine[0, skip:]))  0.99 us
  transfers between devices with their start and end apart: 13, of which 4 were waited for; matrix products, arithmetic and copies ran while one was open for 5% of the time, Pallas kernels for 33%

profile of v3, /device:TPU:0, one launch (start us, length us, event | category | flops | bytes accessed | tf_op | source)
XLA Modules:
  0.0 45.8 jit_solution(17220690680619157331)
XLA Ops:
  0.0 0.9 %slice_bitcast_fusion.2 = f32[128,128]{1,0:T(8,128)S(1)} fusion(f32[3,6,128,128]{3,2,1,0:T(8,128)} %bitcast.31), kind=kLoop, calls=%fused_computation.7 | loop fusion | bytes 131072 | tf_op jit(solution)/shard_map/squeeze | solution.py:290
  0.9 3.0 %collective-permute-start = (f32[128,128]{1,0:T(8,128)S(1)}, f32[128,128]{1,0:T(8,128)S(1)}, u32[]{:S(2)}, u32[]{:S(2)}) collective-permute-start(f32[128,128]{1,0:T(8,128)S(1)} %slice_bitcast_fusion.2), channel_id=1, source_target_pairs={{0,16},{4,20},{8,24},{12,28},{16,0},{20,4},{24,8},{28,12},{1,17},{... | collective-permute-start | bytes 196616 | tf_op jit(solution)/shard_map/ppermute | solution.py:268
  3.9 1.0 %slice_bitcast_fusion = f32[5,128,128]{2,1,0:T(8,128)S(1)} fusion(f32[3,6,128,128]{3,2,1,0:T(8,128)} %bitcast.32), kind=kLoop, calls=%fused_computation.3 | loop fusion | bytes 655360 | tf_op jit(solution)/shard_map/squeeze | solution.py:291
  4.9 0.9 %slice_bitcast_fusion.1 = f32[3,128,128]{2,1,0:T(8,128)S(1)} fusion(f32[3,6,128,128]{3,2,1,0:T(8,128)} %bitcast.33), kind=kLoop, calls=%fused_computation.5 | loop fusion | bytes 393216 | tf_op jit(solution)/shard_map/squeeze | solution.py:294
  5.9 0.3 collective-permute-done
  6.2 4.2 %collective-permute-start.3 = (f32[128,128]{1,0:T(8,128)S(1)}, f32[128,128]{1,0:T(8,128)S(1)}, u32[]{:S(2)}, u32[]{:S(2)}) collective-permute-start(f32[128,128]{1,0:T(8,128)S(1)} %get-tuple-element.56), channel_id=1, source_target_pairs={{0,3},{1,2},{2,1},{3,0},{4,7},{5,6},{6,5},{7,4},{8,11},{9,10},{10,... | collective-permute-start | bytes 196616 | tf_op jit(solution)/shard_map/ppermute | solution.py:280
  10.3 0.0 collective-permute-start.2
  10.3 0.6 %collective-permute-start.1 = (f32[128,128]{1,0:T(8,128)S(1)}, f32[128,128]{1,0:T(8,128)S(1)}, u32[]{:S(2)}, u32[]{:S(2)}) collective-permute-start(f32[128,128]{1,0:T(8,128)S(1)} %get-tuple-element.56), channel_id=1, source_target_pairs={{0,1},{1,0},{2,3},{3,2},{4,5},{5,4},{6,7},{7,6},{8,9},{9,8},{10,11... | collective-permute-start | bytes 196616 | tf_op jit(solution)/shard_map/ppermute | solution.py:280
  11.0 0.1 pad_add_fusion.refs_0_.place_ref
  11.1 1.7 %collective-permute-start.7 = (f32[5,128,128]{2,1,0:T(8,128)S(1)}, f32[5,128,128]{2,1,0:T(8,128)S(1)}, u32[]{:S(2)}, u32[]{:S(2)}) collective-permute-start(f32[5,128,128]{2,1,0:T(8,128)S(1)} %slice_bitcast_fusion), channel_id=1, source_target_pairs={{0,16},{4,20},{8,24},{12,28},{16,0},{20,4},{24,8},{28,12},{1,17},{... | collective-permute-start | bytes 983048 | tf_op jit(solution)/shard_map/ppermute | solution.py:268
  12.7 0.1 collective-permute-done.3
  12.9 2.8 %collective-permute-done.2 = f32[128,128]{1,0:T(8,128)S(1)} collective-permute-done((f32[128,128]{1,0:T(8,128)S(1)}, f32[128,128]{1,0:T(8,128)S(1)}, u32[]{:S(2)}, u32[]{:S(2)}) %collective-permute-start.2) | collective-permute-done | bytes 65568 | tf_op jit(solution)/shard_map/ppermute | solution.py:280
  15.6 0.0 collective-permute-done.1
  15.7 0.1 collective-permute-start.6
  15.8 1.6 %collective-permute-start.5 = (f32[2,128,128]{2,1,0:T(8,128)S(1)}, f32[2,128,128]{2,1,0:T(8,128)S(1)}, u32[]{:S(2)}, u32[]{:S(2)}) collective-permute-start(f32[2,128,128]{2,1,0:T(8,128)S(1)} %constant_dynamic-slice_fusion), channel_id=1, source_target_pairs={{0,8},{4,12},{8,0},{12,4},{16,24},{20,28},{24,16},{28,20},{1,9},{5... | collective-permute-start | bytes 393224 | tf_op jit(solution)/shard_map/ppermute | solution.py:275
  17.3 0.3 collective-permute-start.4
  17.6 2.1 %collective-permute-start.12 = (f32[3,128,128]{2,1,0:T(8,128)S(1)}, f32[3,128,128]{2,1,0:T(8,128)S(1)}, u32[]{:S(2)}, u32[]{:S(2)}) collective-permute-start(f32[3,128,128]{2,1,0:T(8,128)S(1)} %slice_bitcast_fusion.1), channel_id=1, source_target_pairs={{0,3},{1,2},{2,1},{3,0},{4,7},{5,6},{6,5},{7,4},{8,11},{9,10},{10,... | collective-permute-start | bytes 589832 | tf_op jit(solution)/shard_map/ppermute | solution.py:280
  19.8 1.0 %collective-permute-start.11 = (f32[3,128,128]{2,1,0:T(8,128)S(1)}, f32[3,128,128]{2,1,0:T(8,128)S(1)}, u32[]{:S(2)}, u32[]{:S(2)}) collective-permute-start(f32[3,128,128]{2,1,0:T(8,128)S(1)} %slice_bitcast_fusion.1), channel_id=1, source_target_pairs={{0,2},{1,3},{2,0},{3,1},{4,6},{5,7},{6,4},{7,5},{8,10},{9,11},{10,... | collective-permute-start | bytes 589832 | tf_op jit(solution)/shard_map/ppermute | solution.py:280
  20.8 3.6 %collective-permute-done.5 = f32[2,128,128]{2,1,0:T(8,128)S(1)} collective-permute-done((f32[2,128,128]{2,1,0:T(8,128)S(1)}, f32[2,128,128]{2,1,0:T(8,128)S(1)}, u32[]{:S(2)}, u32[]{:S(2)}) %collective-permute-start.5) | collective-permute-done | bytes 131104 | tf_op jit(solution)/shard_map/ppermute | solution.py:275
  24.4 0.4 collective-permute-start.10
  24.9 0.1 collective-permute-start.8
  25.0 4.1 %shard_map.28 = (f32[512,128]{1,0:T(8,128)S(1)}, f32[128,128]{1,0:T(8,128)S(1)}, f32[3,3,128,128]{3,2,1,0:T(8,128)S(1)}) custom-call(s32[2]{0:T(128)S(1)} %pad_add_fusion.refs_0_.place_ref, f32[12,128,128]{2,1,0:T(8,128)S(1)} %constant_dynamic-update-slice_fusion.refs_1_), custom_call_target="tpu_custom_call" | custom-call | flops 4000000000 | bytes 1048576 | tf_op jit(solution)/shard_map/pallas_call | solution.py:163
  29.0 3.9 %shard_map.29 = (f32[384,128]{1,0:T(8,128)S(1)}, f32[128,256]{1,0:T(8,128)S(1)}, f32[2,2,128,128]{3,2,1,0:T(8,128)S(1)}) custom-call(f32[3,3,128,128]{3,2,1,0:T(8,128)S(1)} %get-tuple-element.32.refs_0_, f32[512,128]{1,0:T(8,128)S(1)} %get-tuple-element.33.refs_1_.refs_0_, f32[128,128]{1,0:T(8,128)S(1)} %get-tuple-element.34.refs_2_.refs_3_.refs_4_), custom_call_target="tpu_custom_call" | custom-call | flops 4000000000 | bytes 1048576 | tf_op jit(solution)/shard_map/pallas_call | solution.py:163
  33.0 3.6 %shard_map.30 = (f32[256,128]{1,0:T(8,128)S(1)}, f32[128,384]{1,0:T(8,128)S(1)}, f32[1,1,128,128]{3,2,1,0:T(8,128)S(1)}) custom-call(f32[2,2,128,128]{3,2,1,0:T(8,128)S(1)} %get-tuple-element.35.refs_0_, f32[512,128]{1,0:T(8,128)S(1)} %get-tuple-element.33.refs_1_.refs_0_, f32[384,128]{1,0:T(8,128)S(1)} %get-tuple-element.36.refs_2_.refs_1_, ...), custom_call_target="tpu_custom_call" | custom-call | flops 4000000000 | bytes 1048576 | tf_op jit(solution)/shard_map/pallas_call | solution.py:163
  36.6 0.1 pad_maximum_fusion.2
  36.6 0.2 collective-permute-start.9
  36.8 3.5 %shard_map.31 = (f32[128,128]{1,0:T(8,128)S(1)}, f32[128,512]{1,0:T(8,128)S(1)}) custom-call(f32[1,1,128,128]{3,2,1,0:T(8,128)S(1)} %get-tuple-element.40.refs_0_, f32[512,128]{1,0:T(8,128)S(1)} %get-tuple-element.33.refs_1_.refs_0_, f32[384,128]{1,0:T(8,128)S(1)} %get-tuple-element.36.refs_2_.refs_1_, f32[256,128]{1,0:T(8,128)S(1)} %get-tuple-element.41.refs_3_.refs_2_, ...), custom_call_target="tpu_custom_call" | custom-call | flops 8000000000 | bytes 1048576 | tf_op jit(solution)/shard_map/pallas_call | solution.py:163
  40.3 0.1 pad_maximum_fusion.xc_ref
  40.5 0.0 copy-start.1
  40.5 0.1 pad_maximum_fusion.1.xr_ref
  40.5 0.6 %copy-done.1 = s32[24,24]{1,0:T(8,128)S(1)} copy-done((s32[24,24]{1,0:T(8,128)S(1)}, s32[24,24]{1,0:T(8,128)}, u32[]{:S(2)}) %copy-start.1) | copy-done | bytes 2328
  41.2 4.6 %shard_map.32 = bf16[3,6,128,128]{3,2,1,0:T(8,128)(2,1)} custom-call(s32[2]{0:T(128)S(1)} %pad_add_fusion.refs_0_.place_ref, s32[24,24]{1,0:T(8,128)S(1)} %copy-done.1, f32[3,6,128,128]{3,2,1,0:T(8,128)S(1)} %bitcast.35, f32[4,3,128,128]{3,2,1,0:T(8,128)S(1)} %pad_maximum_fusion.1.xr_ref, f32[2,2,5,128,128]{4,3,2,1,0:T(8,128)S(1)} %pad_maximum_fusion.xc_ref, ...), custom_call_target="tpu_custom_call" | custom-call | flops 4000000000 | bytes 4194304 | tf_op jit(solution)/shard_map/pallas_call | solution.py:243
  (20 shorter events, 0.2 us)
Async XLA Ops:
  0.0 6.2 %copy-start = (f32[3,1,6,1,128,128]{5,4,3,2,1,0:T(8,128)S(1)}, f32[3,1,6,1,128,128]{5,4,3,2,1,0:T(8,128)}, u32[]{:S(2)}) copy-start(f32[3,1,6,1,128,128]{5,4,3,2,1,0:T(8,128)} %param.2) | copy-start | bytes 3538948
  0.9 5.2 %collective-permute-start = (f32[128,128]{1,0:T(8,128)S(1)}, f32[128,128]{1,0:T(8,128)S(1)}, u32[]{:S(2)}, u32[]{:S(2)}) collective-permute-start(f32[128,128]{1,0:T(8,128)S(1)} %slice_bitcast_fusion.2), channel_id=1, source_target_pairs={{0,16},{4,20},{8,24},{12,28},{16,0},{20,4},{24,8},{28,12},{1,17},{... | collective-permute-start | bytes 196616 | tf_op jit(solution)/shard_map/ppermute | solution.py:268
  6.2 6.7 %collective-permute-start.3 = (f32[128,128]{1,0:T(8,128)S(1)}, f32[128,128]{1,0:T(8,128)S(1)}, u32[]{:S(2)}, u32[]{:S(2)}) collective-permute-start(f32[128,128]{1,0:T(8,128)S(1)} %get-tuple-element.56), channel_id=1, source_target_pairs={{0,3},{1,2},{2,1},{3,0},{4,7},{5,6},{6,5},{7,4},{8,11},{9,10},{10,... | collective-permute-start | bytes 196616 | tf_op jit(solution)/shard_map/ppermute | solution.py:280
  10.3 5.3 %collective-permute-start.2 = (f32[128,128]{1,0:T(8,128)S(1)}, f32[128,128]{1,0:T(8,128)S(1)}, u32[]{:S(2)}, u32[]{:S(2)}) collective-permute-start(f32[128,128]{1,0:T(8,128)S(1)} %get-tuple-element.56), channel_id=1, source_target_pairs={{0,2},{1,3},{2,0},{3,1},{4,6},{5,7},{6,4},{7,5},{8,10},{9,11},{10,... | collective-permute-start | bytes 196616 | tf_op jit(solution)/shard_map/ppermute | solution.py:280
  10.3 5.3 %collective-permute-start.1 = (f32[128,128]{1,0:T(8,128)S(1)}, f32[128,128]{1,0:T(8,128)S(1)}, u32[]{:S(2)}, u32[]{:S(2)}) collective-permute-start(f32[128,128]{1,0:T(8,128)S(1)} %get-tuple-element.56), channel_id=1, source_target_pairs={{0,1},{1,0},{2,3},{3,2},{4,5},{5,4},{6,7},{7,6},{8,9},{9,8},{10,11... | collective-permute-start | bytes 196616 | tf_op jit(solution)/shard_map/ppermute | solution.py:280
  11.1 13.8 %collective-permute-start.7 = (f32[5,128,128]{2,1,0:T(8,128)S(1)}, f32[5,128,128]{2,1,0:T(8,128)S(1)}, u32[]{:S(2)}, u32[]{:S(2)}) collective-permute-start(f32[5,128,128]{2,1,0:T(8,128)S(1)} %slice_bitcast_fusion), channel_id=1, source_target_pairs={{0,16},{4,20},{8,24},{12,28},{16,0},{20,4},{24,8},{28,12},{1,17},{... | collective-permute-start | bytes 983048 | tf_op jit(solution)/shard_map/ppermute | solution.py:268
  15.7 9.1 %collective-permute-start.6 = (f32[2,128,128]{2,1,0:T(8,128)S(1)}, f32[2,128,128]{2,1,0:T(8,128)S(1)}, u32[]{:S(2)}, u32[]{:S(2)}) collective-permute-start(f32[2,128,128]{2,1,0:T(8,128)S(1)} %constant_dynamic-slice_fusion), channel_id=1, source_target_pairs={{0,12},{4,8},{8,4},{12,0},{16,28},{20,24},{24,20},{28,16},{1,13},{... | collective-permute-start | bytes 393224 | tf_op jit(solution)/shard_map/ppermute | solution.py:275
  15.8 8.6 %collective-permute-start.5 = (f32[2,128,128]{2,1,0:T(8,128)S(1)}, f32[2,128,128]{2,1,0:T(8,128)S(1)}, u32[]{:S(2)}, u32[]{:S(2)}) collective-permute-start(f32[2,128,128]{2,1,0:T(8,128)S(1)} %constant_dynamic-slice_fusion), channel_id=1, source_target_pairs={{0,8},{4,12},{8,0},{12,4},{16,24},{20,28},{24,16},{28,20},{1,9},{5... | collective-permute-start | bytes 393224 | tf_op jit(solution)/shard_map/ppermute | solution.py:275
  17.3 2.4 %collective-permute-start.4 = (f32[4,128,128]{2,1,0:T(8,128)S(1)}, f32[4,128,128]{2,1,0:T(8,128)S(1)}, u32[]{:S(2)}, u32[]{:S(2)}) collective-permute-start(f32[4,128,128]{2,1,0:T(8,128)S(1)} %pad_maximum_fusion.3), channel_id=1, source_target_pairs={{0,4},{4,0},{8,12},{12,8},{16,20},{20,16},{24,28},{28,24},{1,5},{5... | collective-permute-start | bytes 786440 | tf_op jit(solution)/shard_map/ppermute | solution.py:275
  17.6 22.7 %collective-permute-start.12 = (f32[3,128,128]{2,1,0:T(8,128)S(1)}, f32[3,128,128]{2,1,0:T(8,128)S(1)}, u32[]{:S(2)}, u32[]{:S(2)}) collective-permute-start(f32[3,128,128]{2,1,0:T(8,128)S(1)} %slice_bitcast_fusion.1), channel_id=1, source_target_pairs={{0,3},{1,2},{2,1},{3,0},{4,7},{5,6},{6,5},{7,4},{8,11},{9,10},{10,... | collective-permute-start | bytes 589832 | tf_op jit(solution)/shard_map/ppermute | solution.py:280
  19.8 20.6 %collective-permute-start.11 = (f32[3,128,128]{2,1,0:T(8,128)S(1)}, f32[3,128,128]{2,1,0:T(8,128)S(1)}, u32[]{:S(2)}, u32[]{:S(2)}) collective-permute-start(f32[3,128,128]{2,1,0:T(8,128)S(1)} %slice_bitcast_fusion.1), channel_id=1, source_target_pairs={{0,2},{1,3},{2,0},{3,1},{4,6},{5,7},{6,4},{7,5},{8,10},{9,11},{10,... | collective-permute-start | bytes 589832 | tf_op jit(solution)/shard_map/ppermute | solution.py:280
  24.4 16.0 %collective-permute-start.10 = (f32[3,128,128]{2,1,0:T(8,128)S(1)}, f32[3,128,128]{2,1,0:T(8,128)S(1)}, u32[]{:S(2)}, u32[]{:S(2)}) collective-permute-start(f32[3,128,128]{2,1,0:T(8,128)S(1)} %slice_bitcast_fusion.1), channel_id=1, source_target_pairs={{0,1},{1,0},{2,3},{3,2},{4,5},{5,4},{6,7},{7,6},{8,9},{9,8},{10,11... | collective-permute-start | bytes 589832 | tf_op jit(solution)/shard_map/ppermute | solution.py:280
  24.9 11.7 %collective-permute-start.8 = (f32[5,128,128]{2,1,0:T(8,128)S(1)}, f32[5,128,128]{2,1,0:T(8,128)S(1)}, u32[]{:S(2)}, u32[]{:S(2)}) collective-permute-start(f32[5,128,128]{2,1,0:T(8,128)S(1)} %broadcast_select_fusion), channel_id=1, source_target_pairs={{0,8},{4,12},{8,0},{12,4},{16,24},{20,28},{24,16},{28,20},{1,9},{5... | collective-permute-start | bytes 983048 | tf_op jit(solution)/shard_map/ppermute | solution.py:275
  36.6 3.7 %collective-permute-start.9 = (f32[2,5,128,128]{3,2,1,0:T(8,128)S(1)}, f32[2,5,128,128]{3,2,1,0:T(8,128)S(1)}, u32[]{:S(2)}, u32[]{:S(2)}) collective-permute-start(f32[2,5,128,128]{3,2,1,0:T(8,128)S(1)} %pad_maximum_fusion.2), channel_id=1, source_target_pairs={{0,4},{4,0},{8,12},{12,8},{16,20},{20,16},{24,28},{28,24},{1,5},{5... | collective-permute-start | bytes 1966088 | tf_op jit(solution)/shard_map/ppermute | solution.py:275
  40.5 0.7 %copy-start.1 = (s32[24,24]{1,0:T(8,128)S(1)}, s32[24,24]{1,0:T(8,128)}, u32[]{:S(2)}) copy-start(s32[24,24]{1,0:T(8,128)} %mask_ref.1) | copy-start | bytes 6916

commit v4 on v3

v4 whole, which is shorter than its diff:
```python
import functools

import jax
import jax.numpy as jnp
from jax import lax
from jax.experimental import pallas as pl
from jax.experimental.pallas import tpu as pltpu
from jax.sharding import PartitionSpec as P

LEAD = 4
HALF = 2
PARTS = ((0, 3), (3, 4))
COST = 8
GROUP = 16
HIGHEST = lax.Precision.HIGHEST
VMEM = pl.BlockSpec(memory_space=pltpu.VMEM)
SMEM = pl.BlockSpec(memory_space=pltpu.SMEM)
ROW_BY_COL = (((1,), (0,)), ((), ()))
ROW_BY_ROW = (((1,), (1,)), ((), ()))


def dot(a, b, dims=ROW_BY_COL):
    return lax.dot_general(a, b, dims, precision=HIGHEST, preferred_element_type=jnp.float32)


def dot_t(a, b):
    return dot(a, b, ROW_BY_ROW)


def split(a):
    high = a.astype(jnp.bfloat16)
    return high, (a - high.astype(jnp.float32)).astype(jnp.bfloat16)


def dot_3(a, b, dims=ROW_BY_COL):
    left = jnp.concatenate([a[0], a[0], a[1]], axis=1)
    right = jnp.concatenate([b[0], b[1], b[0]], axis=dims[0][1][0])
    return lax.dot_general(left, right, dims, preferred_element_type=jnp.float32)


def factor_tile(tile, k_ref, w_ref, beside):
    n = tile.shape[0]
    w_ref[...] = tile
    row = lax.broadcasted_iota(jnp.int32, (GROUP, n), 0)
    lane = lax.broadcasted_iota(jnp.int32, (GROUP, n), 1)
    group = w_ref[:GROUP, :]
    for first in range(0, n, GROUP):
        after = first + GROUP
        column = [jnp.broadcast_to(group[:, first + k : first + k + 1], (GROUP, n)) for k in range(GROUP)]
        inside = jnp.logical_and(lane >= first, lane < after)
        group = jnp.where(inside, jnp.where(lane - first == row, 1.0, 0.0), group)
        if after < n:
            ahead = w_ref[after : after + GROUP, :]
            ahead_column = [jnp.broadcast_to(ahead[:, first + k : first + k + 1], (GROUP, n)) for k in range(GROUP)]
            ahead = jnp.where(inside, 0.0, ahead)
        pivot = jnp.broadcast_to(column[0][:1, :], (GROUP, n))
        pivots = inverses = jnp.ones((GROUP, n), jnp.float32)
        for k in range(GROUP):
            here = row == k
            inverse = 1.0 / pivot
            factors = jnp.where(here, 0.0, column[k] * inverse)
            pivots = jnp.where(here, pivot, pivots)
            inverses = jnp.where(here, inverse, inverses)
            if k + 1 < GROUP:
                both = jnp.broadcast_to(column[k][k + 1 : k + 2, :], (GROUP, n)) * jnp.broadcast_to(
                    column[k + 1][k : k + 1, :], (GROUP, n)
                )
                pivot = jnp.broadcast_to(column[k + 1][k + 1 : k + 2, :], (GROUP, n)) - both * inverse
            k_ref[first + k : first + k + 1, :] = group[k : k + 1, :]
            for m in range(k + 1, GROUP):
                column[m] = column[m] - factors * jnp.broadcast_to(column[m][k : k + 1, :], (GROUP, n))
            group = group - factors * jnp.broadcast_to(group[k : k + 1, :], (GROUP, n))
        k_ref[first:after, :] = jnp.where(lane < after, k_ref[first:after, :] * lax.rsqrt(pivots), 0.0)
        if after < n:
            reduced = group * inverses
            terms = [ahead_column[k] * jnp.broadcast_to(reduced[k : k + 1, :], (GROUP, n)) for k in range(GROUP)]
            group = (ahead - sum(terms[2::2], terms[0])) - sum(terms[3::2], terms[1])
            if after + GROUP < n:
                rest = w_ref[after + GROUP :, :]
                rest_lane = lax.broadcasted_iota(jnp.int32, rest.shape, 1)
                kept = jnp.where(jnp.logical_and(rest_lane >= first, rest_lane < after), 0.0, rest)
                w_ref[after + GROUP :, :] = kept - dot(rest[:, first:after], reduced)
        share = -(-len(beside) * GROUP // (n - first))
        for step in beside[:share]:
            step()
        beside = beside[share:]


def at(i, n):
    return slice(i * n, (i + 1) * n)


def gather_lead(place_ref, a_ref, s_ref):
    my_row, my_col = place_ref[0], place_ref[1]
    my_pair = (my_row >> 1) & 1

    def own(i, j):
        return 4 * ((i ^ my_row) & 1) + ((j ^ my_col) & (LEAD - 1))

    for i in range(LEAD):
        mine = my_pair == i // 2
        for j in range(i + 1):
            if i == j:
                s_ref[i, j] = a_ref[jnp.where(mine, own(i, j), 8 + ((i ^ my_row) & 1))]
            elif i // 2 == j // 2:
                tile = a_ref[jnp.where(mine, own(i, j), 10)]
                direct = jnp.logical_or(mine, my_row & 1 == 0)
                s_ref[i, j] = jnp.where(direct, tile, tile.T)
            else:
                tile = a_ref[jnp.where(mine, own(i, j), own(j, i))]
                s_ref[i, j] = jnp.where(mine, tile, tile.T)


def factor_kernel(low, high, *refs):
    refs = list(refs)
    if low == 0:
        place_ref, a_ref = refs[:2]
        del refs[:2]
    else:
        s_in, l_in, k_in = refs[:3]
        del refs[:3]
    l_out, k_out = refs[:2]
    s_out = refs[2] if high < LEAD else None
    w_ref, u_ref, t_ref, s_ref = refs[-4:]
    n = u_ref.shape[-1]
    if low == 0:
        gather_lead(place_ref, a_ref, s_ref)
    else:
        for i in range(low, LEAD):
            for j in range(low, i + 1):
                s_ref[i, j] = s_in[i - low, j - low]

    def l_tile(i, j):
        return l_in[at(i, n), at(j, n)] if j < low else l_out[at(i, n), at(j - low, n)]

    def k_row(i):
        width = (i + 1) * n
        return k_in[at(i, n), :width] if i < low else k_out[at(i - low, n), :width]

    def l_step(i, b):
        l_out[at(i, n), at(b - low, n)] = dot_t(s_ref[i, b], u_ref[b])

    def s_step(i, j, b):
        s_ref[i, j] = s_ref[i, j] - dot_t(l_tile(i, b), l_tile(j, b))

    def t_step(b):
        total = dot(l_tile(b, b - 1), k_row(b - 1))
        for j in range(b - 1):
            pad = jnp.zeros((n, (b - 1 - j) * n), jnp.float32)
            total = total + jnp.concatenate([dot(l_tile(b, j), k_row(j)), pad], axis=1)
        t_ref[:, : b * n] = total

    def k_step(b):
        k_out[at(b - low, n), : b * n] = -dot(u_ref[b], t_ref[:, : b * n])

    def corner_step(b):
        square = (n, n)
        row, col = lax.broadcasted_iota(jnp.int32, square, 0), lax.broadcasted_iota(jnp.int32, square, 1)
        l_out[at(b, n), at(b - low, n)] = jnp.where(row >= col, dot_t(s_ref[b, b], u_ref[b]), 0.0)

    later = []
    for b in range(low, high):
        if b > 0:
            later.append(functools.partial(t_step, b))
        factor_tile(s_ref[b, b], u_ref.at[b], w_ref, later)
        k_out[at(b - low, n), b * n : (b + 1) * n] = u_ref[b]
        if b + 1 < LEAD:
            l_step(b + 1, b)
            s_step(b + 1, b + 1, b)
        later = []
        if b > 0:
            later.append(functools.partial(k_step, b))
        for i in range(b + 2, LEAD):
            later.append(functools.partial(l_step, i, b))
            for j in range(b + 1, i + 1):
                later.append(functools.partial(s_step, i, j, b))
        later.append(functools.partial(corner_step, b))
    for step in later:
        step()
    if s_out is not None:
        for i in range(high, LEAD):
            for j in range(high, i + 1):
                s_out[i - high, j - high] = s_ref[i, j]


def factor_columns(low, high, n, args):
    shapes = [(LEAD * n, (high - low) * n), ((high - low) * n, high * n)]
    if high < LEAD:
        shapes.append((LEAD - high, LEAD - high, n, n))
    return pl.pallas_call(
        functools.partial(factor_kernel, low, high),
        out_shape=[jax.ShapeDtypeStruct(shape, jnp.float32) for shape in shapes],
        in_specs=[SMEM, VMEM] if low == 0 else [VMEM] * len(args),
        out_specs=[VMEM] * len(shapes),
        scratch_shapes=[
            pltpu.VMEM((n, n), jnp.float32),
            pltpu.VMEM((LEAD, n, n), jnp.float32),
            pltpu.VMEM((n, LEAD * n), jnp.float32),
            pltpu.VMEM((LEAD, LEAD, n, n), jnp.float32),
        ],
        compiler_params=pltpu.CompilerParams(vmem_limit_bytes=32 * 2**20),
        cost_estimate=pl.CostEstimate(flops=COST * (high - low) * 10**9, bytes_accessed=2**20, transcendentals=0),
    )(*args)


def marks_at(tile_rows, tile_cols):
    return 2, 2 + tile_rows * tile_cols, 2 + tile_rows * (tile_cols + LEAD)


def update_kernel(cols, marks_ref, a_ref, xr_ref, xc_ref, *refs):
    l_cols, k_rows = refs[: len(PARTS)], refs[len(PARTS) : 2 * len(PARTS)]
    out_ref, x_ref, y_ref, z_ref, k_ref = refs[2 * len(PARTS) :]
    part = [p for p, (low, high) in enumerate(PARTS) for _ in range(low, high)]
    tile_rows, tile_cols, n, _ = a_ref.shape
    my_row, my_col = marks_ref[0], marks_ref[1]
    of_tiles, of_rows, of_cols = marks_at(tile_rows, tile_cols)
    skip = 1 if cols == LEAD else 0
    half = HALF * n
    every = slice(None)

    def mark(at_entry):
        return marks_ref[at_entry].astype(jnp.float32)

    def pair(ref, rows_at, cols_at):
        return ref[0, rows_at, cols_at], ref[1, rows_at, cols_at]

    def put(ref, rows_at, cols_at, value):
        ref[0, rows_at, cols_at], ref[1, rows_at, cols_at] = split(value)

    for k in range(LEAD):
        for i in range(tile_rows):
            put(x_ref, at(i, n), at(k, n), xr_ref[(my_col ^ k) & (LEAD - 1), i] * mark(of_rows + i * LEAD + k))
        apart = (my_row ^ k) & (LEAD - 1)
        for j in range(skip, tile_cols):
            tile = xc_ref[apart & 1, apart >> 1, j - skip] * mark(of_cols + k * tile_cols + j)
            put(y_ref, at(k, n), at(j - skip, n), tile)
    for b in range(LEAD):
        rows_of = k_rows[part[b]]
        put(k_ref, at(b, n), slice(0, (b + 1) * n), rows_of[at(b - PARTS[part[b]][0], n), : (b + 1) * n])
        if b % HALF + 1 < HALF:
            k_ref[:, at(b, n), (b + 1) * n : (b // HALF + 1) * half] = jnp.zeros((2, n, n), jnp.bfloat16)
    head, tail = slice(0, half), slice(half, LEAD * n)
    k1, k2 = pair(k_ref, head, head), pair(k_ref, tail, every)
    put(z_ref, every, head, dot_3(pair(x_ref, every, head), k1, ROW_BY_ROW))
    put(z_ref, every, tail, dot_3(pair(x_ref, every, every), k2, ROW_BY_ROW))
    z_rows = pair(z_ref, every, every)
    for first in range(skip, tile_cols, 2):
        some = range(first, min(first + 2, tile_cols))
        here = slice((first - skip) * n, (some[-1] + 1 - skip) * n)
        z_head = split(dot_3(k1, pair(y_ref, head, here)))
        z_tail = split(dot_3(k2, pair(y_ref, every, here)))
        product = dot_3(z_rows, [jnp.concatenate(parts, axis=0) for parts in zip(z_head, z_tail)])
        for i in range(tile_rows):
            in_lead = jnp.logical_and(i == 0, my_row < LEAD)
            for j in some:
                rest = a_ref[i, j] * mark(of_tiles + i * tile_cols + j) - product[at(i, n), at(j - first, n)]
                out_ref[i, j] = jnp.where(in_lead, 0.0, rest).astype(jnp.bfloat16)
    for i in range(tile_rows):
        for c in range(LEAD):

            @pl.when(my_col == c)
            def _():
                out_ref[i, 0] = z_ref[0, at(i, n), at(c, n)]
                if i == 0:
                    for r in range(LEAD):

                        @pl.when(my_row == r)
                        def _():
                            if r >= c:
                                tile = l_cols[part[c]][at(r, n), at(c - PARTS[part[c]][0], n)]
                                out_ref[0, 0] = tile.astype(jnp.bfloat16)
                            else:
                                out_ref[0, 0] = jnp.zeros((n, n), jnp.bfloat16)


def update(cols, marks, mine, from_cols, from_rows, factors):
    tile_rows, tile_cols, n, _ = mine.shape
    width = LEAD * n
    used = tile_cols - 1 if cols == LEAD else tile_cols
    return pl.pallas_call(
        functools.partial(update_kernel, cols),
        out_shape=jax.ShapeDtypeStruct(mine.shape, jnp.bfloat16),
        in_specs=[SMEM] + [VMEM] * (3 + 2 * len(PARTS)),
        out_specs=VMEM,
        scratch_shapes=[
            pltpu.VMEM((2, tile_rows * n, width), jnp.bfloat16),
            pltpu.VMEM((2, width, used * n), jnp.bfloat16),
            pltpu.VMEM((2, tile_rows * n, width), jnp.bfloat16),
            pltpu.VMEM((2, width, width), jnp.bfloat16),
        ],
        compiler_params=pltpu.CompilerParams(vmem_limit_bytes=40 * 2**20),
        cost_estimate=pl.CostEstimate(flops=4 * 10**9, bytes_accessed=2**22, transcendentals=0),
    )(marks, mine, from_cols, from_rows, *factors)


def copy_down(value, axis):
    size, index = lax.axis_size(axis), lax.axis_index(axis)
    have = LEAD
    while have < size:
        if 2 * have == size:
            pairs = [(i, i ^ have) for i in range(size)]
        else:
            pairs = [(i, i + have) for i in range(have) if i + have < size]
        value = jnp.where(index >= have, lax.ppermute(value, axis, pairs), value)
        have *= 2
    return value


def swap(value, axis, bit):
    size = lax.axis_size(axis)
    return [value, lax.ppermute(value, axis, [(i, i ^ bit) for i in range(size)])]


def exchange(value, axis):
    size = lax.axis_size(axis)
    return [value] + [lax.ppermute(value, axis, [(i, i ^ s) for i in range(size)]) for s in range(1, LEAD)]


def on_device(covariance, tile_mask):
    tile_rows, _, tile_cols, _, n, _ = covariance.shape
    rows, cols = lax.axis_size("row"), lax.axis_size("col")
    my_row, my_col = lax.axis_index("row"), lax.axis_index("col")
    mine = covariance.reshape(tile_rows, tile_cols, n, n)
    of_rows = lax.dynamic_index_in_dim(tile_mask.reshape(tile_rows, rows, -1), my_row, 1, keepdims=False)
    of_tiles = lax.dynamic_index_in_dim(of_rows.reshape(tile_rows, tile_cols, cols), my_col, 2, keepdims=False)
    of_cols = lax.dynamic_index_in_dim(tile_mask[:LEAD].reshape(LEAD, tile_cols, cols), my_col, 2, keepdims=False)
    place = jnp.stack([my_row, my_col]).astype(jnp.int32)
    marks = jnp.concatenate([place, of_tiles.reshape(-1), of_rows[:, :LEAD].reshape(-1), of_cols.reshape(-1)])
    skip = 1 if cols == LEAD else 0
    lead = copy_down(mine[0, 0], "row")
    _, across = lax.optimization_barrier((lead, mine[0, skip:]))
    across = copy_down(across, "row")
    lead = jnp.stack(exchange(copy_down(lead, "col"), "col"))
    corner = lax.dynamic_index_in_dim(lead, (my_row ^ my_col) & (LEAD - 1), 0)
    beside = lax.dynamic_index_in_dim(lead, (my_row ^ my_col ^ 1) & (LEAD - 1), 0)
    far = swap(jnp.concatenate([corner, beside]), "row", 3)[1]
    partner = swap(lead, "row", 1)[1]
    lead = jnp.concatenate([lead, partner, swap(corner, "row", 2)[1], far])
    _, down = lax.optimization_barrier((partner, mine[:, 0]))
    down = exchange(copy_down(down, "col"), "col")
    lead, across = lax.optimization_barrier((lead, across))
    across = swap(across, "row", 2)
    l_cols, k_rows = [], []
    args = [marks, lead]
    for p, (low, high) in enumerate(PARTS):
        column, row, *state = factor_columns(low, high, n, args)
        l_cols.append(column)
        k_rows.append(row)
        if high == LEAD:
            break
        if p == len(PARTS) - 2:
            state[0], *across = lax.optimization_barrier((state[0], *across))
            across = swap(jnp.stack(across), "row", 1)
        args = [state[0], jnp.concatenate(l_cols, axis=1), k_rows[0]]
    row, *moved = lax.optimization_barrier((k_rows[-1], *across, *down))
    k_rows[-1] = row
    across, down = jnp.stack(moved[:2]), jnp.stack(moved[2:])
    out = update(cols, marks, mine, down, across, (*l_cols, *k_rows))
    return out.reshape(tile_rows, 1, tile_cols, 1, n, n)


def solution(mesh):
    in_specs = (P(None, "row", None, "col", None, None), P())
    out_specs = P(None, "row", None, "col", None, None)
    return jax.shard_map(on_device, mesh=mesh, in_specs=in_specs, out_specs=out_specs, check_vma=False)
```

time: 46 us -> 43.8 us (0.952)
  waiting for transfers between devices: 6.8 us -> 1.95 us
  starting transfers between devices: 15.1 us -> 17 us
  local copies, waits for them, and re-layouts: 3.6 us -> 5.29 us
  Pallas kernels: 19.7 us -> 18.5 us
    ppermute x5, waiting for transfers between devices: 3.59 us -> 0.57 us  [swap(): lax.ppermute(value, axis, [(i, i ^ bit) for i in range(size)])]
    ppermute x6, waiting for transfers between devices: 2.92 us -> 1.37 us  [exchange(): lax.ppermute(value, axis, [(i, i ^ s) for i in range(size)])]
    ppermute x5, starting transfers between devices: 2.17 us -> 3.47 us  [swap(): lax.ppermute(value, axis, [(i, i ^ bit) for i in range(size)])]
    pallas_call x5 -> x3, Pallas kernels: 19.7 us -> 18.5 us  [the longest x2 13.7 us: factor_columns(): pl.pallas_call(functools.partial(factor_kernel, low, high), out_shape=[ja...]
    dynamic_slice x1 -> x4, local copies, waits for them, and re-layouts: 0.02 us -> 1.18 us  [the longest x1 0.71 us: on_device(): lax.dynamic_index_in_dim(tile_mask.reshape(tile_rows, rows, -1), my_row,...]
    slice x0 -> x1, local copies, waits for them, and re-layouts: none -> 0.69 us  [on_device(): tile_mask[:LEAD].reshape(LEAD, tile_cols, cols)]
    unnamed x9 -> x7, local copies, waits for them, and re-layouts: 0.69 us -> 0.05 us
    ppermute x6, starting transfers between devices: 8.33 us -> 8.97 us  [exchange(): lax.ppermute(value, axis, [(i, i ^ s) for i in range(size)])]
  transfers between devices with their start and end apart: 13 -> 13, of which waited for: 4 -> 3; matrix products, arithmetic and copies ran while one was open for 5% -> 10% of each run, Pallas kernels for 33% -> 32%
where the time goes in v4:
time: 43.8 us; the launch traced here: 43.5 us
  Pallas kernels  18.5 us (42%)
  starting transfers between devices  17 us (39%)
  local copies, waits for them, and re-layouts  5.29 us (12%)
  waiting for transfers between devices  1.95 us (4%)
  other arithmetic  0.52 us (1%)
    pallas_call x2, Pallas kernels, factor_columns(): pl.pallas_call(functools.partial(factor_kernel, low, high), out_shape=[ja...  13.7 us
    ppermute x6, starting transfers between devices, exchange(): lax.ppermute(value, axis, [(i, i ^ s) for i in range(size)])  8.97 us
    pallas_call x1, Pallas kernels, update(): pl.pallas_call(functools.partial(update_kernel, cols), out_shape=jax.Shap...  4.77 us
    ppermute x2, starting transfers between devices, copy_down(): value = jnp.where(index >= have, lax.ppermute(value, axis, pairs), value)  4.6 us
    ppermute x5, starting transfers between devices, swap(): lax.ppermute(value, axis, [(i, i ^ bit) for i in range(size)])  3.47 us
    ppermute x6, waiting for transfers between devices, exchange(): lax.ppermute(value, axis, [(i, i ^ s) for i in range(size)])  1.37 us
    squeeze x1, local copies, waits for them, and re-layouts, on_device(): _, across = lax.optimization_barrier((lead, mine[0, skip:]))  0.99 us
    squeeze x1, local copies, waits for them, and re-layouts, on_device(): _, down = lax.optimization_barrier((partner, mine[:, 0]))  0.95 us
  transfers between devices with their start and end apart: 13, of which 3 were waited for; matrix products, arithmetic and copies ran while one was open for 10% of the time, Pallas kernels for 32%

profile of v4, /device:TPU:0, one launch (start us, length us, event | category | flops | bytes accessed | tf_op | source)
XLA Modules:
  0.0 43.5 jit_solution(3555243541540840753)
XLA Ops:
  0.0 0.9 %slice_bitcast_fusion.2 = f32[128,128]{1,0:T(8,128)S(1)} fusion(f32[3,6,128,128]{3,2,1,0:T(8,128)} %bitcast.38), kind=kLoop, calls=%fused_computation.8 | loop fusion | bytes 131072 | tf_op jit(solution)/shard_map/squeeze | solution.py:330
  0.9 3.0 %collective-permute-start = (f32[128,128]{1,0:T(8,128)S(1)}, f32[128,128]{1,0:T(8,128)S(1)}, u32[]{:S(2)}, u32[]{:S(2)}) collective-permute-start(f32[128,128]{1,0:T(8,128)S(1)} %slice_bitcast_fusion.2), channel_id=1, source_target_pairs={{0,16},{4,20},{8,24},{12,28},{16,0},{20,4},{24,8},{28,12},{1,17},{... | collective-permute-start | bytes 196616 | tf_op jit(solution)/shard_map/ppermute | solution.py:304
  3.9 1.0 %slice_bitcast_fusion = f32[5,128,128]{2,1,0:T(8,128)S(1)} fusion(f32[3,6,128,128]{3,2,1,0:T(8,128)} %bitcast.39), kind=kLoop, calls=%fused_computation.3 | loop fusion | bytes 655360 | tf_op jit(solution)/shard_map/squeeze | solution.py:331
  4.9 0.9 %slice_bitcast_fusion.1 = f32[3,128,128]{2,1,0:T(8,128)S(1)} fusion(f32[3,6,128,128]{3,2,1,0:T(8,128)} %bitcast.40), kind=kLoop, calls=%fused_computation.5 | loop fusion | bytes 393216 | tf_op jit(solution)/shard_map/squeeze | solution.py:339
  5.9 0.7 %slice.16 = s32[4,24]{1,0:T(4,128)S(1)} slice(s32[24,24]{1,0:T(8,128)} %param.3), slice={[0:4], [0:24]} | slice | bytes 768 | tf_op jit(solution)/shard_map/slice | solution.py:326
  6.6 3.8 %collective-permute-start.3 = (f32[128,128]{1,0:T(8,128)S(1)}, f32[128,128]{1,0:T(8,128)S(1)}, u32[]{:S(2)}, u32[]{:S(2)}) collective-permute-start(f32[128,128]{1,0:T(8,128)S(1)} %get-tuple-element.44), channel_id=1, source_target_pairs={{0,3},{1,2},{2,1},{3,0},{4,7},{5,6},{6,5},{7,4},{8,11},{9,10},{10,... | collective-permute-start | bytes 196616 | tf_op jit(solution)/shard_map/ppermute | solution.py:316
  10.3 0.7 %collective-permute-start.1 = (f32[128,128]{1,0:T(8,128)S(1)}, f32[128,128]{1,0:T(8,128)S(1)}, u32[]{:S(2)}, u32[]{:S(2)}) collective-permute-start(f32[128,128]{1,0:T(8,128)S(1)} %get-tuple-element.44), channel_id=1, source_target_pairs={{0,1},{1,0},{2,3},{3,2},{4,5},{5,4},{6,7},{7,6},{8,9},{9,8},{10,11... | collective-permute-start | bytes 196616 | tf_op jit(solution)/shard_map/ppermute | solution.py:316
  11.0 0.7 %constant_dynamic-slice_fusion.2 = s32[3,1,24]{2,1,0:T(1,128)S(1)} fusion(s32[3,8,24]{2,1,0:T(8,128)} %bitcast.56, s32[]{:T(128)S(6)} %select_n.33), kind=kLoop, calls=%fused_computation.21 | loop fusion | bytes 580 | tf_op jit(solution)/shard_map/jit(dynamic_index_in_dim)/dynamic_slice | solution.py:324
  11.8 0.1 reshape.28
  11.8 0.1 reshape.30
  11.9 0.2 dynamic-slice_reduce_fusion.1
  12.1 0.1 reshape.29
  12.2 0.1 reshape.31
  12.3 0.2 dynamic-slice_reduce_fusion
  12.5 0.1 reshape.32
  12.6 0.1 concatenate.10.refs_0_.marks_ref
  12.7 1.6 %collective-permute-start.7 = (f32[5,128,128]{2,1,0:T(8,128)S(1)}, f32[5,128,128]{2,1,0:T(8,128)S(1)}, u32[]{:S(2)}, u32[]{:S(2)}) collective-permute-start(f32[5,128,128]{2,1,0:T(8,128)S(1)} %slice_bitcast_fusion), channel_id=1, source_target_pairs={{0,16},{4,20},{8,24},{12,28},{16,0},{20,4},{24,8},{28,12},{1,17},{... | collective-permute-start | bytes 983048 | tf_op jit(solution)/shard_map/ppermute | solution.py:304
  14.3 1.3 %collective-permute-done.2 = f32[128,128]{1,0:T(8,128)S(1)} collective-permute-done((f32[128,128]{1,0:T(8,128)S(1)}, f32[128,128]{1,0:T(8,128)S(1)}, u32[]{:S(2)}, u32[]{:S(2)}) %collective-permute-start.2) | collective-permute-done | bytes 65568 | tf_op jit(solution)/shard_map/ppermute | solution.py:316
  15.7 0.1 collective-permute-start.4
  15.8 1.6 %collective-permute-start.5 = (f32[1,128,128]{2,1,0:T(8,128)S(1)}, f32[1,128,128]{2,1,0:T(8,128)S(1)}, u32[]{:S(2)}, u32[]{:S(2)}) collective-permute-start(f32[1,128,128]{2,1,0:T(8,128)S(1)} %get-tuple-element.46), channel_id=1, source_target_pairs={{0,8},{4,12},{8,0},{12,4},{16,24},{20,28},{24,16},{28,20},{1,9},{5... | collective-permute-start | bytes 196616 | tf_op jit(solution)/shard_map/ppermute | solution.py:311
  17.4 0.4 collective-permute-start.6
  17.8 2.7 %collective-permute-start.12 = (f32[3,128,128]{2,1,0:T(8,128)S(1)}, f32[3,128,128]{2,1,0:T(8,128)S(1)}, u32[]{:S(2)}, u32[]{:S(2)}) collective-permute-start(f32[3,128,128]{2,1,0:T(8,128)S(1)} %slice_bitcast_fusion.1), channel_id=1, source_target_pairs={{0,3},{1,2},{2,1},{3,0},{4,7},{5,6},{6,5},{7,4},{8,11},{9,10},{10,... | collective-permute-start | bytes 589832 | tf_op jit(solution)/shard_map/ppermute | solution.py:316
  20.5 1.8 %collective-permute-start.10 = (f32[3,128,128]{2,1,0:T(8,128)S(1)}, f32[3,128,128]{2,1,0:T(8,128)S(1)}, u32[]{:S(2)}, u32[]{:S(2)}) collective-permute-start(f32[3,128,128]{2,1,0:T(8,128)S(1)} %slice_bitcast_fusion.1), channel_id=1, source_target_pairs={{0,1},{1,0},{2,3},{3,2},{4,5},{5,4},{6,7},{7,6},{8,9},{9,8},{10,11... | collective-permute-start | bytes 589832 | tf_op jit(solution)/shard_map/ppermute | solution.py:316
  22.4 0.6 %collective-permute-done.6 = f32[2,128,128]{2,1,0:T(8,128)S(1)} collective-permute-done((f32[2,128,128]{2,1,0:T(8,128)S(1)}, f32[2,128,128]{2,1,0:T(8,128)S(1)}, u32[]{:S(2)}, u32[]{:S(2)}) %collective-permute-start.6) | collective-permute-done | bytes 131104 | tf_op jit(solution)/shard_map/ppermute | solution.py:311
  23.0 1.4 %collective-permute-start.8 = (f32[5,128,128]{2,1,0:T(8,128)S(1)}, f32[5,128,128]{2,1,0:T(8,128)S(1)}, u32[]{:S(2)}, u32[]{:S(2)}) collective-permute-start(f32[5,128,128]{2,1,0:T(8,128)S(1)} %broadcast_select_fusion), channel_id=1, source_target_pairs={{0,8},{4,12},{8,0},{12,4},{16,24},{20,28},{24,16},{28,20},{1,9},{5... | collective-permute-start | bytes 983048 | tf_op jit(solution)/shard_map/ppermute | solution.py:311
  24.4 10.5 %shard_map.28 = (f32[512,384]{1,0:T(8,128)S(1)}, f32[384,384]{1,0:T(8,128)S(1)}, f32[1,1,128,128]{3,2,1,0:T(8,128)S(1)}) custom-call(s32[56]{0:T(128)S(1)} %concatenate.10.refs_0_.marks_ref, f32[11,128,128]{2,1,0:T(8,128)S(1)} %constant_dynamic-update-slice_fusion.refs_1_), custom_call_target="tpu_custom_call" | custom-call | flops 24000000000 | bytes 1048576 | tf_op jit(solution)/shard_map/pallas_call | solution.py:190
  34.9 0.1 pad_maximum_fusion.2
  35.0 0.1 collective-permute-start.9
  35.1 3.2 %shard_map.29 = (f32[512,128]{1,0:T(8,128)S(1)}, f32[128,512]{1,0:T(8,128)S(1)}) custom-call(f32[1,1,128,128]{3,2,1,0:T(8,128)S(1)} %get-tuple-element.28.refs_0_, f32[512,384]{1,0:T(8,128)S(1)} %get-tuple-element.29.refs_1_.refs_0_, f32[384,384]{1,0:T(8,128)S(1)} %get-tuple-element.30.refs_2_), custom_call_target="tpu_custom_call" | custom-call | flops 8000000000 | bytes 1048576 | tf_op jit(solution)/shard_map/pallas_call | solution.py:190
  38.3 0.3 pad_maximum_fusion.xc_ref
  38.6 0.1 pad_maximum_fusion.1.xr_ref
  38.7 4.8 %shard_map.30 = bf16[3,6,128,128]{3,2,1,0:T(8,128)(2,1)} custom-call(s32[56]{0:T(128)S(1)} %concatenate.10.refs_0_.marks_ref, f32[3,6,128,128]{3,2,1,0:T(8,128)S(1)} %bitcast.42, f32[4,3,128,128]{3,2,1,0:T(8,128)S(1)} %pad_maximum_fusion.1.xr_ref, f32[2,2,5,128,128]{4,3,2,1,0:T(8,128)S(1)} %pad_maximum_fusion.xc_ref, ...), custom_call_target="tpu_custom_call" | custom-call | flops 4000000000 | bytes 4194304 | tf_op jit(solution)/shard_map/pallas_call | solution.py:280
  (27 shorter events, 0.3 us)
Async XLA Ops:
  0.0 6.6 %copy-start = (f32[3,1,6,1,128,128]{5,4,3,2,1,0:T(8,128)S(1)}, f32[3,1,6,1,128,128]{5,4,3,2,1,0:T(8,128)}, u32[]{:S(2)}) copy-start(f32[3,1,6,1,128,128]{5,4,3,2,1,0:T(8,128)} %param.2) | copy-start | bytes 3538948
  0.9 5.6 %collective-permute-start = (f32[128,128]{1,0:T(8,128)S(1)}, f32[128,128]{1,0:T(8,128)S(1)}, u32[]{:S(2)}, u32[]{:S(2)}) collective-permute-start(f32[128,128]{1,0:T(8,128)S(1)} %slice_bitcast_fusion.2), channel_id=1, source_target_pairs={{0,16},{4,20},{8,24},{12,28},{16,0},{20,4},{24,8},{28,12},{1,17},{... | collective-permute-start | bytes 196616 | tf_op jit(solution)/shard_map/ppermute | solution.py:304
  6.6 7.7 %collective-permute-start.3 = (f32[128,128]{1,0:T(8,128)S(1)}, f32[128,128]{1,0:T(8,128)S(1)}, u32[]{:S(2)}, u32[]{:S(2)}) collective-permute-start(f32[128,128]{1,0:T(8,128)S(1)} %get-tuple-element.44), channel_id=1, source_target_pairs={{0,3},{1,2},{2,1},{3,0},{4,7},{5,6},{6,5},{7,4},{8,11},{9,10},{10,... | collective-permute-start | bytes 196616 | tf_op jit(solution)/shard_map/ppermute | solution.py:316
  10.3 5.3 %collective-permute-start.2 = (f32[128,128]{1,0:T(8,128)S(1)}, f32[128,128]{1,0:T(8,128)S(1)}, u32[]{:S(2)}, u32[]{:S(2)}) collective-permute-start(f32[128,128]{1,0:T(8,128)S(1)} %get-tuple-element.44), channel_id=1, source_target_pairs={{0,2},{1,3},{2,0},{3,1},{4,6},{5,7},{6,4},{7,5},{8,10},{9,11},{10,... | collective-permute-start | bytes 196616 | tf_op jit(solution)/shard_map/ppermute | solution.py:316
  10.3 5.3 %collective-permute-start.1 = (f32[128,128]{1,0:T(8,128)S(1)}, f32[128,128]{1,0:T(8,128)S(1)}, u32[]{:S(2)}, u32[]{:S(2)}) collective-permute-start(f32[128,128]{1,0:T(8,128)S(1)} %get-tuple-element.44), channel_id=1, source_target_pairs={{0,1},{1,0},{2,3},{3,2},{4,5},{5,4},{6,7},{7,6},{8,9},{9,8},{10,11... | collective-permute-start | bytes 196616 | tf_op jit(solution)/shard_map/ppermute | solution.py:316
  12.7 10.3 %collective-permute-start.7 = (f32[5,128,128]{2,1,0:T(8,128)S(1)}, f32[5,128,128]{2,1,0:T(8,128)S(1)}, u32[]{:S(2)}, u32[]{:S(2)}) collective-permute-start(f32[5,128,128]{2,1,0:T(8,128)S(1)} %slice_bitcast_fusion), channel_id=1, source_target_pairs={{0,16},{4,20},{8,24},{12,28},{16,0},{20,4},{24,8},{28,12},{1,17},{... | collective-permute-start | bytes 983048 | tf_op jit(solution)/shard_map/ppermute | solution.py:304
  15.7 2.1 %collective-permute-start.4 = (f32[4,128,128]{2,1,0:T(8,128)S(1)}, f32[4,128,128]{2,1,0:T(8,128)S(1)}, u32[]{:S(2)}, u32[]{:S(2)}) collective-permute-start(f32[4,128,128]{2,1,0:T(8,128)S(1)} %pad_maximum_fusion.3), channel_id=1, source_target_pairs={{0,4},{4,0},{8,12},{12,8},{16,20},{20,16},{24,28},{28,24},{1,5},{5... | collective-permute-start | bytes 786440 | tf_op jit(solution)/shard_map/ppermute | solution.py:311
  15.8 4.7 %collective-permute-start.5 = (f32[1,128,128]{2,1,0:T(8,128)S(1)}, f32[1,128,128]{2,1,0:T(8,128)S(1)}, u32[]{:S(2)}, u32[]{:S(2)}) collective-permute-start(f32[1,128,128]{2,1,0:T(8,128)S(1)} %get-tuple-element.46), channel_id=1, source_target_pairs={{0,8},{4,12},{8,0},{12,4},{16,24},{20,28},{24,16},{28,20},{1,9},{5... | collective-permute-start | bytes 196616 | tf_op jit(solution)/shard_map/ppermute | solution.py:311
  17.4 5.6 %collective-permute-start.6 = (f32[2,128,128]{2,1,0:T(8,128)S(1)}, f32[2,128,128]{2,1,0:T(8,128)S(1)}, u32[]{:S(2)}, u32[]{:S(2)}) collective-permute-start(f32[2,128,128]{2,1,0:T(8,128)S(1)} %pad_maximum_fusion.4), channel_id=1, source_target_pairs={{0,12},{4,8},{8,4},{12,0},{16,28},{20,24},{24,20},{28,16},{1,13},{... | collective-permute-start | bytes 393224 | tf_op jit(solution)/shard_map/ppermute | solution.py:311
  17.8 20.4 %collective-permute-start.12 = (f32[3,128,128]{2,1,0:T(8,128)S(1)}, f32[3,128,128]{2,1,0:T(8,128)S(1)}, u32[]{:S(2)}, u32[]{:S(2)}) collective-permute-start(f32[3,128,128]{2,1,0:T(8,128)S(1)} %slice_bitcast_fusion.1), channel_id=1, source_target_pairs={{0,3},{1,2},{2,1},{3,0},{4,7},{5,6},{6,5},{7,4},{8,11},{9,10},{10,... | collective-permute-start | bytes 589832 | tf_op jit(solution)/shard_map/ppermute | solution.py:316
  20.5 17.8 %collective-permute-start.11 = (f32[3,128,128]{2,1,0:T(8,128)S(1)}, f32[3,128,128]{2,1,0:T(8,128)S(1)}, u32[]{:S(2)}, u32[]{:S(2)}) collective-permute-start(f32[3,128,128]{2,1,0:T(8,128)S(1)} %slice_bitcast_fusion.1), channel_id=1, source_target_pairs={{0,2},{1,3},{2,0},{3,1},{4,6},{5,7},{6,4},{7,5},{8,10},{9,11},{10,... | collective-permute-start | bytes 589832 | tf_op jit(solution)/shard_map/ppermute | solution.py:316
  20.5 17.8 %collective-permute-start.10 = (f32[3,128,128]{2,1,0:T(8,128)S(1)}, f32[3,128,128]{2,1,0:T(8,128)S(1)}, u32[]{:S(2)}, u32[]{:S(2)}) collective-permute-start(f32[3,128,128]{2,1,0:T(8,128)S(1)} %slice_bitcast_fusion.1), channel_id=1, source_target_pairs={{0,1},{1,0},{2,3},{3,2},{4,5},{5,4},{6,7},{7,6},{8,9},{9,8},{10,11... | collective-permute-start | bytes 589832 | tf_op jit(solution)/shard_map/ppermute | solution.py:316
  23.0 11.9 %collective-permute-start.8 = (f32[5,128,128]{2,1,0:T(8,128)S(1)}, f32[5,128,128]{2,1,0:T(8,128)S(1)}, u32[]{:S(2)}, u32[]{:S(2)}) collective-permute-start(f32[5,128,128]{2,1,0:T(8,128)S(1)} %broadcast_select_fusion), channel_id=1, source_target_pairs={{0,8},{4,12},{8,0},{12,4},{16,24},{20,28},{24,16},{28,20},{1,9},{5... | collective-permute-start | bytes 983048 | tf_op jit(solution)/shard_map/ppermute | solution.py:311
  35.0 3.3 %collective-permute-start.9 = (f32[2,5,128,128]{3,2,1,0:T(8,128)S(1)}, f32[2,5,128,128]{3,2,1,0:T(8,128)S(1)}, u32[]{:S(2)}, u32[]{:S(2)}) collective-permute-start(f32[2,5,128,128]{3,2,1,0:T(8,128)S(1)} %pad_maximum_fusion.2), channel_id=1, source_target_pairs={{0,4},{4,0},{8,12},{12,8},{16,20},{20,16},{24,28},{28,24},{1,5},{5... | collective-permute-start | bytes 1966088 | tf_op jit(solution)/shard_map/ppermute | solution.py:311

commit v5 on v4

--- a/solution.py
+++ b/solution.py
@@ -58,7 +58,7 @@
         for k in range(GROUP):
             here = row == k
             inverse = 1.0 / pivot
-            factors = jnp.where(here, 0.0, column[k] * inverse)
+            factors = jnp.where(here, 0.0, column[k]) * inverse
             pivots = jnp.where(here, pivot, pivots)
             inverses = jnp.where(here, inverse, inverses)
             if k + 1 < GROUP:
@@ -97,18 +97,19 @@
     def own(i, j):
         return 4 * ((i ^ my_row) & 1) + ((j ^ my_col) & (LEAD - 1))
 
-    for i in range(LEAD):
+    def step(i, j):
         mine = my_pair == i // 2
-        for j in range(i + 1):
-            if i == j:
-                s_ref[i, j] = a_ref[jnp.where(mine, own(i, j), 8 + ((i ^ my_row) & 1))]
-            elif i // 2 == j // 2:
-                tile = a_ref[jnp.where(mine, own(i, j), 10)]
-                direct = jnp.logical_or(mine, my_row & 1 == 0)
-                s_ref[i, j] = jnp.where(direct, tile, tile.T)
-            else:
-                tile = a_ref[jnp.where(mine, own(i, j), own(j, i))]
-                s_ref[i, j] = jnp.where(mine, tile, tile.T)
+        if i == j:
+            s_ref[i, j] = a_ref[jnp.where(mine, own(i, j), 8 + ((i ^ my_row) & 1))]
+        elif i // 2 == j // 2:
+            tile = a_ref[jnp.where(mine, own(i, j), 10)]
+            direct = jnp.logical_or(mine, my_row & 1 == 0)
+            s_ref[i, j] = jnp.where(direct, tile, tile.T)
+        else:
+            tile = a_ref[jnp.where(mine, own(i, j), own(j, i))]
+            s_ref[i, j] = jnp.where(mine, tile, tile.T)
+
+    return {(i, j): functools.partial(step, i, j) for i in range(LEAD) for j in range(i + 1)}
 
 
 def factor_kernel(low, high, *refs):
@@ -124,7 +125,8 @@
     w_ref, u_ref, t_ref, s_ref = refs[-4:]
     n = u_ref.shape[-1]
     if low == 0:
-        gather_lead(place_ref, a_ref, s_ref)
+        take = gather_lead(place_ref, a_ref, s_ref)
+        take.pop((0, 0))()
     else:
         for i in range(low, LEAD):
             for j in range(low, i + 1):
@@ -158,7 +160,7 @@
         row, col = lax.broadcasted_iota(jnp.int32, square, 0), lax.broadcasted_iota(jnp.int32, square, 1)
         l_out[at(b, n), at(b - low, n)] = jnp.where(row >= col, dot_t(s_ref[b, b], u_ref[b]), 0.0)
 
-    later = []
+    later = list(take.values()) if low == 0 else []
     for b in range(low, high):
         if b > 0:
             later.append(functools.partial(t_step, b))
@@ -244,17 +246,14 @@
     put(z_ref, every, head, dot_3(pair(x_ref, every, head), k1, ROW_BY_ROW))
     put(z_ref, every, tail, dot_3(pair(x_ref, every, every), k2, ROW_BY_ROW))
     z_rows = pair(z_ref, every, every)
-    for first in range(skip, tile_cols, 2):
-        some = range(first, min(first + 2, tile_cols))
-        here = slice((first - skip) * n, (some[-1] + 1 - skip) * n)
-        z_head = split(dot_3(k1, pair(y_ref, head, here)))
-        z_tail = split(dot_3(k2, pair(y_ref, every, here)))
-        product = dot_3(z_rows, [jnp.concatenate(parts, axis=0) for parts in zip(z_head, z_tail)])
-        for i in range(tile_rows):
-            in_lead = jnp.logical_and(i == 0, my_row < LEAD)
-            for j in some:
-                rest = a_ref[i, j] * mark(of_tiles + i * tile_cols + j) - product[at(i, n), at(j - first, n)]
-                out_ref[i, j] = jnp.where(in_lead, 0.0, rest).astype(jnp.bfloat16)
+    z_head = split(dot_3(k1, pair(y_ref, head, every)))
+    z_tail = split(dot_3(k2, pair(y_ref, every, every)))
+    product = dot_3(z_rows, [jnp.concatenate(parts, axis=0) for parts in zip(z_head, z_tail)])
+    for i in range(tile_rows):
+        in_lead = jnp.logical_and(i == 0, my_row < LEAD)
+        for j in range(skip, tile_cols):
+            rest = a_ref[i, j] * mark(of_tiles + i * tile_cols + j) - product[at(i, n), at(j - skip, n)]
+            out_ref[i, j] = jnp.where(in_lead, 0.0, rest).astype(jnp.bfloat16)
     for i in range(tile_rows):
         for c in range(LEAD):
 
@@ -338,7 +337,7 @@
     lead = jnp.concatenate([lead, partner, swap(corner, "row", 2)[1], far])
     _, down = lax.optimization_barrier((partner, mine[:, 0]))
     down = exchange(copy_down(down, "col"), "col")
-    lead, across = lax.optimization_barrier((lead, across))
+    _, across = lax.optimization_barrier((partner, across))
     across = swap(across, "row", 2)
     l_cols, k_rows = [], []
     args = [marks, lead]

time: 43.8 us -> 43.1 us (0.984)
  Pallas kernels: 18.5 us -> 17.8 us
    pallas_call x1, Pallas kernels: 4.77 us -> 4.04 us  [update(): pl.pallas_call(functools.partial(update_kernel, cols), out_shape=jax.Shap...]
where the time goes in v5:
time: 43.1 us; the launch traced here: 42.8 us
  Pallas kernels  17.8 us (41%)
  starting transfers between devices  17 us (39%)
  local copies, waits for them, and re-layouts  5.29 us (12%)
  waiting for transfers between devices  1.95 us (5%)
  other arithmetic  0.52 us (1%)
    pallas_call x2, Pallas kernels, factor_columns(): pl.pallas_call(functools.partial(factor_kernel, low, high), out_shape=[ja...  13.8 us
    ppermute x6, starting transfers between devices, exchange(): lax.ppermute(value, axis, [(i, i ^ s) for i in range(size)])  8.97 us
    ppermute x2, starting transfers between devices, copy_down(): value = jnp.where(index >= have, lax.ppermute(value, axis, pairs), value)  4.6 us
    pallas_call x1, Pallas kernels, update(): pl.pallas_call(functools.partial(update_kernel, cols), out_shape=jax.Shap...  4.04 us
    ppermute x5, starting transfers between devices, swap(): lax.ppermute(value, axis, [(i, i ^ bit) for i in range(size)])  3.47 us
    ppermute x6, waiting for transfers between devices, exchange(): lax.ppermute(value, axis, [(i, i ^ s) for i in range(size)])  1.37 us
    squeeze x1, local copies, waits for them, and re-layouts, on_device(): _, across = lax.optimization_barrier((lead, mine[0, skip:]))  0.99 us
    squeeze x1, local copies, waits for them, and re-layouts, on_device(): _, down = lax.optimization_barrier((partner, mine[:, 0]))  0.95 us
  transfers between devices with their start and end apart: 13, of which 3 were waited for; matrix products, arithmetic and copies ran while one was open for 10% of the time, Pallas kernels for 32%

profile of v5, /device:TPU:0, one launch (start us, length us, event | category | flops | bytes accessed | tf_op | source)
XLA Modules:
  0.0 42.8 jit_solution(6818539930337113795)
XLA Ops:
  0.0 0.9 %slice_bitcast_fusion.2 = f32[128,128]{1,0:T(8,128)S(1)} fusion(f32[3,6,128,128]{3,2,1,0:T(8,128)} %bitcast.38), kind=kLoop, calls=%fused_computation.8 | loop fusion | bytes 131072 | tf_op jit(solution)/shard_map/squeeze | solution.py:329
  0.9 3.0 %collective-permute-start = (f32[128,128]{1,0:T(8,128)S(1)}, f32[128,128]{1,0:T(8,128)S(1)}, u32[]{:S(2)}, u32[]{:S(2)}) collective-permute-start(f32[128,128]{1,0:T(8,128)S(1)} %slice_bitcast_fusion.2), channel_id=1, source_target_pairs={{0,16},{4,20},{8,24},{12,28},{16,0},{20,4},{24,8},{28,12},{1,17},{... | collective-permute-start | bytes 196616 | tf_op jit(solution)/shard_map/ppermute | solution.py:303
  3.9 1.0 %slice_bitcast_fusion = f32[5,128,128]{2,1,0:T(8,128)S(1)} fusion(f32[3,6,128,128]{3,2,1,0:T(8,128)} %bitcast.39), kind=kLoop, calls=%fused_computation.3 | loop fusion | bytes 655360 | tf_op jit(solution)/shard_map/squeeze | solution.py:330
  4.9 0.9 %slice_bitcast_fusion.1 = f32[3,128,128]{2,1,0:T(8,128)S(1)} fusion(f32[3,6,128,128]{3,2,1,0:T(8,128)} %bitcast.40), kind=kLoop, calls=%fused_computation.5 | loop fusion | bytes 393216 | tf_op jit(solution)/shard_map/squeeze | solution.py:338
  5.9 0.7 %slice.16 = s32[4,24]{1,0:T(4,128)S(1)} slice(s32[24,24]{1,0:T(8,128)} %param.3), slice={[0:4], [0:24]} | slice | bytes 768 | tf_op jit(solution)/shard_map/slice | solution.py:325
  6.6 3.8 %collective-permute-start.3 = (f32[128,128]{1,0:T(8,128)S(1)}, f32[128,128]{1,0:T(8,128)S(1)}, u32[]{:S(2)}, u32[]{:S(2)}) collective-permute-start(f32[128,128]{1,0:T(8,128)S(1)} %get-tuple-element.42), channel_id=1, source_target_pairs={{0,3},{1,2},{2,1},{3,0},{4,7},{5,6},{6,5},{7,4},{8,11},{9,10},{10,... | collective-permute-start | bytes 196616 | tf_op jit(solution)/shard_map/ppermute | solution.py:315
  10.3 0.7 %collective-permute-start.1 = (f32[128,128]{1,0:T(8,128)S(1)}, f32[128,128]{1,0:T(8,128)S(1)}, u32[]{:S(2)}, u32[]{:S(2)}) collective-permute-start(f32[128,128]{1,0:T(8,128)S(1)} %get-tuple-element.42), channel_id=1, source_target_pairs={{0,1},{1,0},{2,3},{3,2},{4,5},{5,4},{6,7},{7,6},{8,9},{9,8},{10,11... | collective-permute-start | bytes 196616 | tf_op jit(solution)/shard_map/ppermute | solution.py:315
  11.0 0.7 %constant_dynamic-slice_fusion.2 = s32[3,1,24]{2,1,0:T(1,128)S(1)} fusion(s32[3,8,24]{2,1,0:T(8,128)} %bitcast.56, s32[]{:T(128)S(6)} %select_n.33), kind=kLoop, calls=%fused_computation.21 | loop fusion | bytes 580 | tf_op jit(solution)/shard_map/jit(dynamic_index_in_dim)/dynamic_slice | solution.py:323
  11.8 0.1 reshape.28
  11.8 0.1 reshape.30
  11.9 0.2 dynamic-slice_reduce_fusion.1
  12.1 0.1 reshape.29
  12.2 0.1 reshape.31
  12.3 0.2 dynamic-slice_reduce_fusion
  12.5 0.1 reshape.32
  12.6 0.1 concatenate.10.refs_0_.marks_ref
  12.7 1.6 %collective-permute-start.7 = (f32[5,128,128]{2,1,0:T(8,128)S(1)}, f32[5,128,128]{2,1,0:T(8,128)S(1)}, u32[]{:S(2)}, u32[]{:S(2)}) collective-permute-start(f32[5,128,128]{2,1,0:T(8,128)S(1)} %slice_bitcast_fusion), channel_id=1, source_target_pairs={{0,16},{4,20},{8,24},{12,28},{16,0},{20,4},{24,8},{28,12},{1,17},{... | collective-permute-start | bytes 983048 | tf_op jit(solution)/shard_map/ppermute | solution.py:303
  14.3 1.3 %collective-permute-done.2 = f32[128,128]{1,0:T(8,128)S(1)} collective-permute-done((f32[128,128]{1,0:T(8,128)S(1)}, f32[128,128]{1,0:T(8,128)S(1)}, u32[]{:S(2)}, u32[]{:S(2)}) %collective-permute-start.2) | collective-permute-done | bytes 65568 | tf_op jit(solution)/shard_map/ppermute | solution.py:315
  15.7 0.1 collective-permute-start.4
  15.8 1.6 %collective-permute-start.5 = (f32[1,128,128]{2,1,0:T(8,128)S(1)}, f32[1,128,128]{2,1,0:T(8,128)S(1)}, u32[]{:S(2)}, u32[]{:S(2)}) collective-permute-start(f32[1,128,128]{2,1,0:T(8,128)S(1)} %get-tuple-element.44), channel_id=1, source_target_pairs={{0,8},{4,12},{8,0},{12,4},{16,24},{20,28},{24,16},{28,20},{1,9},{5... | collective-permute-start | bytes 196616 | tf_op jit(solution)/shard_map/ppermute | solution.py:310
  17.4 0.4 collective-permute-start.6
  17.8 2.7 %collective-permute-start.12 = (f32[3,128,128]{2,1,0:T(8,128)S(1)}, f32[3,128,128]{2,1,0:T(8,128)S(1)}, u32[]{:S(2)}, u32[]{:S(2)}) collective-permute-start(f32[3,128,128]{2,1,0:T(8,128)S(1)} %slice_bitcast_fusion.1), channel_id=1, source_target_pairs={{0,3},{1,2},{2,1},{3,0},{4,7},{5,6},{6,5},{7,4},{8,11},{9,10},{10,... | collective-permute-start | bytes 589832 | tf_op jit(solution)/shard_map/ppermute | solution.py:315
  20.5 1.8 %collective-permute-start.10 = (f32[3,128,128]{2,1,0:T(8,128)S(1)}, f32[3,128,128]{2,1,0:T(8,128)S(1)}, u32[]{:S(2)}, u32[]{:S(2)}) collective-permute-start(f32[3,128,128]{2,1,0:T(8,128)S(1)} %slice_bitcast_fusion.1), channel_id=1, source_target_pairs={{0,1},{1,0},{2,3},{3,2},{4,5},{5,4},{6,7},{7,6},{8,9},{9,8},{10,11... | collective-permute-start | bytes 589832 | tf_op jit(solution)/shard_map/ppermute | solution.py:315
  22.4 0.6 %collective-permute-done.6 = f32[2,128,128]{2,1,0:T(8,128)S(1)} collective-permute-done((f32[2,128,128]{2,1,0:T(8,128)S(1)}, f32[2,128,128]{2,1,0:T(8,128)S(1)}, u32[]{:S(2)}, u32[]{:S(2)}) %collective-permute-start.6) | collective-permute-done | bytes 131104 | tf_op jit(solution)/shard_map/ppermute | solution.py:310
  23.0 1.4 %collective-permute-start.8 = (f32[5,128,128]{2,1,0:T(8,128)S(1)}, f32[5,128,128]{2,1,0:T(8,128)S(1)}, u32[]{:S(2)}, u32[]{:S(2)}) collective-permute-start(f32[5,128,128]{2,1,0:T(8,128)S(1)} %broadcast_select_fusion), channel_id=1, source_target_pairs={{0,8},{4,12},{8,0},{12,4},{16,24},{20,28},{24,16},{28,20},{1,9},{5... | collective-permute-start | bytes 983048 | tf_op jit(solution)/shard_map/ppermute | solution.py:310
  24.4 10.6 %shard_map.28 = (f32[512,384]{1,0:T(8,128)S(1)}, f32[384,384]{1,0:T(8,128)S(1)}, f32[1,1,128,128]{3,2,1,0:T(8,128)S(1)}) custom-call(s32[56]{0:T(128)S(1)} %concatenate.10.refs_0_.marks_ref, f32[11,128,128]{2,1,0:T(8,128)S(1)} %constant_dynamic-update-slice_fusion.refs_1_), custom_call_target="tpu_custom_call" | custom-call | flops 24000000000 | bytes 1048576 | tf_op jit(solution)/shard_map/pallas_call | solution.py:192
  35.0 0.1 pad_maximum_fusion.2
  35.1 0.1 collective-permute-start.9
  35.2 3.2 %shard_map.29 = (f32[512,128]{1,0:T(8,128)S(1)}, f32[128,512]{1,0:T(8,128)S(1)}) custom-call(f32[1,1,128,128]{3,2,1,0:T(8,128)S(1)} %get-tuple-element.26.refs_0_, f32[512,384]{1,0:T(8,128)S(1)} %get-tuple-element.27.refs_1_.refs_0_, f32[384,384]{1,0:T(8,128)S(1)} %get-tuple-element.28.refs_2_), custom_call_target="tpu_custom_call" | custom-call | flops 8000000000 | bytes 1048576 | tf_op jit(solution)/shard_map/pallas_call | solution.py:192
  38.4 0.3 pad_maximum_fusion.xc_ref
  38.7 0.1 pad_maximum_fusion.1.xr_ref
  38.7 4.0 %shard_map.30 = bf16[3,6,128,128]{3,2,1,0:T(8,128)(2,1)} custom-call(s32[56]{0:T(128)S(1)} %concatenate.10.refs_0_.marks_ref, f32[3,6,128,128]{3,2,1,0:T(8,128)S(1)} %bitcast.42, f32[4,3,128,128]{3,2,1,0:T(8,128)S(1)} %pad_maximum_fusion.1.xr_ref, f32[2,2,5,128,128]{4,3,2,1,0:T(8,128)S(1)} %pad_maximum_fusion.xc_ref, ...), custom_call_target="tpu_custom_call" | custom-call | flops 4000000000 | bytes 4194304 | tf_op jit(solution)/shard_map/pallas_call | solution.py:279
  (27 shorter events, 0.3 us)
Async XLA Ops:
  0.0 6.6 %copy-start = (f32[3,1,6,1,128,128]{5,4,3,2,1,0:T(8,128)S(1)}, f32[3,1,6,1,128,128]{5,4,3,2,1,0:T(8,128)}, u32[]{:S(2)}) copy-start(f32[3,1,6,1,128,128]{5,4,3,2,1,0:T(8,128)} %param.2) | copy-start | bytes 3538948
  0.9 5.6 %collective-permute-start = (f32[128,128]{1,0:T(8,128)S(1)}, f32[128,128]{1,0:T(8,128)S(1)}, u32[]{:S(2)}, u32[]{:S(2)}) collective-permute-start(f32[128,128]{1,0:T(8,128)S(1)} %slice_bitcast_fusion.2), channel_id=1, source_target_pairs={{0,16},{4,20},{8,24},{12,28},{16,0},{20,4},{24,8},{28,12},{1,17},{... | collective-permute-start | bytes 196616 | tf_op jit(solution)/shard_map/ppermute | solution.py:303
  6.6 7.7 %collective-permute-start.3 = (f32[128,128]{1,0:T(8,128)S(1)}, f32[128,128]{1,0:T(8,128)S(1)}, u32[]{:S(2)}, u32[]{:S(2)}) collective-permute-start(f32[128,128]{1,0:T(8,128)S(1)} %get-tuple-element.42), channel_id=1, source_target_pairs={{0,3},{1,2},{2,1},{3,0},{4,7},{5,6},{6,5},{7,4},{8,11},{9,10},{10,... | collective-permute-start | bytes 196616 | tf_op jit(solution)/shard_map/ppermute | solution.py:315
  10.3 5.3 %collective-permute-start.2 = (f32[128,128]{1,0:T(8,128)S(1)}, f32[128,128]{1,0:T(8,128)S(1)}, u32[]{:S(2)}, u32[]{:S(2)}) collective-permute-start(f32[128,128]{1,0:T(8,128)S(1)} %get-tuple-element.42), channel_id=1, source_target_pairs={{0,2},{1,3},{2,0},{3,1},{4,6},{5,7},{6,4},{7,5},{8,10},{9,11},{10,... | collective-permute-start | bytes 196616 | tf_op jit(solution)/shard_map/ppermute | solution.py:315
  10.3 5.3 %collective-permute-start.1 = (f32[128,128]{1,0:T(8,128)S(1)}, f32[128,128]{1,0:T(8,128)S(1)}, u32[]{:S(2)}, u32[]{:S(2)}) collective-permute-start(f32[128,128]{1,0:T(8,128)S(1)} %get-tuple-element.42), channel_id=1, source_target_pairs={{0,1},{1,0},{2,3},{3,2},{4,5},{5,4},{6,7},{7,6},{8,9},{9,8},{10,11... | collective-permute-start | bytes 196616 | tf_op jit(solution)/shard_map/ppermute | solution.py:315
  12.7 10.3 %collective-permute-start.7 = (f32[5,128,128]{2,1,0:T(8,128)S(1)}, f32[5,128,128]{2,1,0:T(8,128)S(1)}, u32[]{:S(2)}, u32[]{:S(2)}) collective-permute-start(f32[5,128,128]{2,1,0:T(8,128)S(1)} %slice_bitcast_fusion), channel_id=1, source_target_pairs={{0,16},{4,20},{8,24},{12,28},{16,0},{20,4},{24,8},{28,12},{1,17},{... | collective-permute-start | bytes 983048 | tf_op jit(solution)/shard_map/ppermute | solution.py:303
  15.7 2.1 %collective-permute-start.4 = (f32[4,128,128]{2,1,0:T(8,128)S(1)}, f32[4,128,128]{2,1,0:T(8,128)S(1)}, u32[]{:S(2)}, u32[]{:S(2)}) collective-permute-start(f32[4,128,128]{2,1,0:T(8,128)S(1)} %pad_maximum_fusion.3), channel_id=1, source_target_pairs={{0,4},{4,0},{8,12},{12,8},{16,20},{20,16},{24,28},{28,24},{1,5},{5... | collective-permute-start | bytes 786440 | tf_op jit(solution)/shard_map/ppermute | solution.py:310
  15.8 4.7 %collective-permute-start.5 = (f32[1,128,128]{2,1,0:T(8,128)S(1)}, f32[1,128,128]{2,1,0:T(8,128)S(1)}, u32[]{:S(2)}, u32[]{:S(2)}) collective-permute-start(f32[1,128,128]{2,1,0:T(8,128)S(1)} %get-tuple-element.44), channel_id=1, source_target_pairs={{0,8},{4,12},{8,0},{12,4},{16,24},{20,28},{24,16},{28,20},{1,9},{5... | collective-permute-start | bytes 196616 | tf_op jit(solution)/shard_map/ppermute | solution.py:310
  17.4 5.6 %collective-permute-start.6 = (f32[2,128,128]{2,1,0:T(8,128)S(1)}, f32[2,128,128]{2,1,0:T(8,128)S(1)}, u32[]{:S(2)}, u32[]{:S(2)}) collective-permute-start(f32[2,128,128]{2,1,0:T(8,128)S(1)} %pad_maximum_fusion.4), channel_id=1, source_target_pairs={{0,12},{4,8},{8,4},{12,0},{16,28},{20,24},{24,20},{28,16},{1,13},{... | collective-permute-start | bytes 393224 | tf_op jit(solution)/shard_map/ppermute | solution.py:310
  17.8 20.5 %collective-permute-start.12 = (f32[3,128,128]{2,1,0:T(8,128)S(1)}, f32[3,128,128]{2,1,0:T(8,128)S(1)}, u32[]{:S(2)}, u32[]{:S(2)}) collective-permute-start(f32[3,128,128]{2,1,0:T(8,128)S(1)} %slice_bitcast_fusion.1), channel_id=1, source_target_pairs={{0,3},{1,2},{2,1},{3,0},{4,7},{5,6},{6,5},{7,4},{8,11},{9,10},{10,... | collective-permute-start | bytes 589832 | tf_op jit(solution)/shard_map/ppermute | solution.py:315
  20.5 17.8 %collective-permute-start.11 = (f32[3,128,128]{2,1,0:T(8,128)S(1)}, f32[3,128,128]{2,1,0:T(8,128)S(1)}, u32[]{:S(2)}, u32[]{:S(2)}) collective-permute-start(f32[3,128,128]{2,1,0:T(8,128)S(1)} %slice_bitcast_fusion.1), channel_id=1, source_target_pairs={{0,2},{1,3},{2,0},{3,1},{4,6},{5,7},{6,4},{7,5},{8,10},{9,11},{10,... | collective-permute-start | bytes 589832 | tf_op jit(solution)/shard_map/ppermute | solution.py:315
  20.5 17.8 %collective-permute-start.10 = (f32[3,128,128]{2,1,0:T(8,128)S(1)}, f32[3,128,128]{2,1,0:T(8,128)S(1)}, u32[]{:S(2)}, u32[]{:S(2)}) collective-permute-start(f32[3,128,128]{2,1,0:T(8,128)S(1)} %slice_bitcast_fusion.1), channel_id=1, source_target_pairs={{0,1},{1,0},{2,3},{3,2},{4,5},{5,4},{6,7},{7,6},{8,9},{9,8},{10,11... | collective-permute-start | bytes 589832 | tf_op jit(solution)/shard_map/ppermute | solution.py:315
  23.0 12.0 %collective-permute-start.8 = (f32[5,128,128]{2,1,0:T(8,128)S(1)}, f32[5,128,128]{2,1,0:T(8,128)S(1)}, u32[]{:S(2)}, u32[]{:S(2)}) collective-permute-start(f32[5,128,128]{2,1,0:T(8,128)S(1)} %broadcast_select_fusion), channel_id=1, source_target_pairs={{0,8},{4,12},{8,0},{12,4},{16,24},{20,28},{24,16},{28,20},{1,9},{5... | collective-permute-start | bytes 983048 | tf_op jit(solution)/shard_map/ppermute | solution.py:310
  35.1 3.3 %collective-permute-start.9 = (f32[2,5,128,128]{3,2,1,0:T(8,128)S(1)}, f32[2,5,128,128]{3,2,1,0:T(8,128)S(1)}, u32[]{:S(2)}, u32[]{:S(2)}) collective-permute-start(f32[2,5,128,128]{3,2,1,0:T(8,128)S(1)} %pad_maximum_fusion.2), channel_id=1, source_target_pairs={{0,4},{4,0},{8,12},{12,8},{16,20},{20,16},{24,28},{28,24},{1,5},{5... | collective-permute-start | bytes 1966088 | tf_op jit(solution)/shard_map/ppermute | solution.py:310

commit v6 on v5

--- a/solution.py
+++ b/solution.py
@@ -11,6 +11,7 @@
 HALF = 2
 PARTS = ((0, 3), (3, 4))
 COST = 8
+LANES = 128
 GROUP = 16
 HIGHEST = lax.Precision.HIGHEST
 VMEM = pl.BlockSpec(memory_space=pltpu.VMEM)
@@ -20,7 +21,14 @@
 
 
 def dot(a, b, dims=ROW_BY_COL):
-    return lax.dot_general(a, b, dims, precision=HIGHEST, preferred_element_type=jnp.float32)
+    if a.shape[1] < LANES:
+        return lax.dot_general(a, b, dims, precision=HIGHEST, preferred_element_type=jnp.float32)
+    (x, rest), (y, other) = split(a), split(b)
+    x_last = (a - x.astype(jnp.float32) - rest.astype(jnp.float32)).astype(jnp.bfloat16)
+    y_last = (b - y.astype(jnp.float32) - other.astype(jnp.float32)).astype(jnp.bfloat16)
+    left = jnp.concatenate([x, x, rest, rest, x, x_last], axis=1)
+    right = jnp.concatenate([y, other, y, other, y_last, y], axis=dims[0][1][0])
+    return lax.dot_general(left, right, dims, preferred_element_type=jnp.float32)
 
 
 def dot_t(a, b):

time: 43.1 us -> 42.6 us (0.988)
  Pallas kernels: 17.8 us -> 16.9 us
  waiting for transfers between devices: 1.95 us -> 2.64 us
    pallas_call x2, Pallas kernels: 13.8 us -> 12.8 us  [factor_columns(): pl.pallas_call(functools.partial(factor_kernel, low, high), out_shape=[ja...]
    ppermute x6, waiting for transfers between devices: 1.37 us -> 2.06 us  [exchange(): lax.ppermute(value, axis, [(i, i ^ s) for i in range(size)])]
  transfers between devices with their start and end apart: 13 -> 13, of which waited for: 3 -> 4; matrix products, arithmetic and copies ran while one was open for 10% -> 11% of each run, Pallas kernels for 32% -> 30%
where the time goes in v6:
time: 42.6 us; the launch traced here: 42.3 us
  starting transfers between devices  17 us (40%)
  Pallas kernels  16.9 us (40%)
  local copies, waits for them, and re-layouts  5.29 us (12%)
  waiting for transfers between devices  2.64 us (6%)
    pallas_call x2, Pallas kernels, factor_columns(): pl.pallas_call(functools.partial(factor_kernel, low, high), out_shape=[ja...  12.8 us
    ppermute x6, starting transfers between devices, exchange(): lax.ppermute(value, axis, [(i, i ^ s) for i in range(size)])  8.97 us
    ppermute x2, starting transfers between devices, copy_down(): value = jnp.where(index >= have, lax.ppermute(value, axis, pairs), value)  4.6 us
    pallas_call x1, Pallas kernels, update(): pl.pallas_call(functools.partial(update_kernel, cols), out_shape=jax.Shap...  4.04 us
    ppermute x5, starting transfers between devices, swap(): lax.ppermute(value, axis, [(i, i ^ bit) for i in range(size)])  3.47 us
    ppermute x6, waiting for transfers between devices, exchange(): lax.ppermute(value, axis, [(i, i ^ s) for i in range(size)])  2.06 us
    squeeze x1, local copies, waits for them, and re-layouts, on_device(): _, across = lax.optimization_barrier((lead, mine[0, skip:]))  0.99 us
    squeeze x1, local copies, waits for them, and re-layouts, on_device(): _, down = lax.optimization_barrier((partner, mine[:, 0]))  0.95 us
  transfers between devices with their start and end apart: 13, of which 4 were waited for; matrix products, arithmetic and copies ran while one was open for 11% of the time, Pallas kernels for 30%

profile of v6, /device:TPU:0, one launch (start us, length us, event | category | flops | bytes accessed | tf_op | source)
XLA Modules:
  0.0 42.3 jit_solution(7938942261740025709)
XLA Ops:
  0.0 0.9 %slice_bitcast_fusion.2 = f32[128,128]{1,0:T(8,128)S(1)} fusion(f32[3,6,128,128]{3,2,1,0:T(8,128)} %bitcast.38), kind=kLoop, calls=%fused_computation.8 | loop fusion | bytes 131072 | tf_op jit(solution)/shard_map/squeeze | solution.py:337
  0.9 3.0 %collective-permute-start = (f32[128,128]{1,0:T(8,128)S(1)}, f32[128,128]{1,0:T(8,128)S(1)}, u32[]{:S(2)}, u32[]{:S(2)}) collective-permute-start(f32[128,128]{1,0:T(8,128)S(1)} %slice_bitcast_fusion.2), channel_id=1, source_target_pairs={{0,16},{4,20},{8,24},{12,28},{16,0},{20,4},{24,8},{28,12},{1,17},{... | collective-permute-start | bytes 196616 | tf_op jit(solution)/shard_map/ppermute | solution.py:311
  3.9 1.0 %slice_bitcast_fusion = f32[5,128,128]{2,1,0:T(8,128)S(1)} fusion(f32[3,6,128,128]{3,2,1,0:T(8,128)} %bitcast.39), kind=kLoop, calls=%fused_computation.3 | loop fusion | bytes 655360 | tf_op jit(solution)/shard_map/squeeze | solution.py:338
  4.9 0.9 %slice_bitcast_fusion.1 = f32[3,128,128]{2,1,0:T(8,128)S(1)} fusion(f32[3,6,128,128]{3,2,1,0:T(8,128)} %bitcast.40), kind=kLoop, calls=%fused_computation.5 | loop fusion | bytes 393216 | tf_op jit(solution)/shard_map/squeeze | solution.py:346
  5.9 0.7 %slice.16 = s32[4,24]{1,0:T(4,128)S(1)} slice(s32[24,24]{1,0:T(8,128)} %param.3), slice={[0:4], [0:24]} | slice | bytes 768 | tf_op jit(solution)/shard_map/slice | solution.py:333
  6.6 3.8 %collective-permute-start.3 = (f32[128,128]{1,0:T(8,128)S(1)}, f32[128,128]{1,0:T(8,128)S(1)}, u32[]{:S(2)}, u32[]{:S(2)}) collective-permute-start(f32[128,128]{1,0:T(8,128)S(1)} %get-tuple-element.42), channel_id=1, source_target_pairs={{0,3},{1,2},{2,1},{3,0},{4,7},{5,6},{6,5},{7,4},{8,11},{9,10},{10,... | collective-permute-start | bytes 196616 | tf_op jit(solution)/shard_map/ppermute | solution.py:323
  10.3 0.7 %collective-permute-start.1 = (f32[128,128]{1,0:T(8,128)S(1)}, f32[128,128]{1,0:T(8,128)S(1)}, u32[]{:S(2)}, u32[]{:S(2)}) collective-permute-start(f32[128,128]{1,0:T(8,128)S(1)} %get-tuple-element.42), channel_id=1, source_target_pairs={{0,1},{1,0},{2,3},{3,2},{4,5},{5,4},{6,7},{7,6},{8,9},{9,8},{10,11... | collective-permute-start | bytes 196616 | tf_op jit(solution)/shard_map/ppermute | solution.py:323
  11.0 0.7 %constant_dynamic-slice_fusion.2 = s32[3,1,24]{2,1,0:T(1,128)S(1)} fusion(s32[3,8,24]{2,1,0:T(8,128)} %bitcast.56, s32[]{:T(128)S(6)} %select_n.33), kind=kLoop, calls=%fused_computation.21 | loop fusion | bytes 580 | tf_op jit(solution)/shard_map/jit(dynamic_index_in_dim)/dynamic_slice | solution.py:331
  11.8 0.1 reshape.28
  11.8 0.1 reshape.30
  11.9 0.2 dynamic-slice_reduce_fusion.1
  12.1 0.1 reshape.29
  12.2 0.1 reshape.31
  12.3 0.2 dynamic-slice_reduce_fusion
  12.5 0.1 reshape.32
  12.6 0.1 concatenate.10.refs_0_.marks_ref
  12.7 1.6 %collective-permute-start.7 = (f32[5,128,128]{2,1,0:T(8,128)S(1)}, f32[5,128,128]{2,1,0:T(8,128)S(1)}, u32[]{:S(2)}, u32[]{:S(2)}) collective-permute-start(f32[5,128,128]{2,1,0:T(8,128)S(1)} %slice_bitcast_fusion), channel_id=1, source_target_pairs={{0,16},{4,20},{8,24},{12,28},{16,0},{20,4},{24,8},{28,12},{1,17},{... | collective-permute-start | bytes 983048 | tf_op jit(solution)/shard_map/ppermute | solution.py:311
  14.3 1.3 %collective-permute-done.2 = f32[128,128]{1,0:T(8,128)S(1)} collective-permute-done((f32[128,128]{1,0:T(8,128)S(1)}, f32[128,128]{1,0:T(8,128)S(1)}, u32[]{:S(2)}, u32[]{:S(2)}) %collective-permute-start.2) | collective-permute-done | bytes 65568 | tf_op jit(solution)/shard_map/ppermute | solution.py:323
  15.7 0.1 collective-permute-start.4
  15.8 1.6 %collective-permute-start.5 = (f32[1,128,128]{2,1,0:T(8,128)S(1)}, f32[1,128,128]{2,1,0:T(8,128)S(1)}, u32[]{:S(2)}, u32[]{:S(2)}) collective-permute-start(f32[1,128,128]{2,1,0:T(8,128)S(1)} %get-tuple-element.44), channel_id=1, source_target_pairs={{0,8},{4,12},{8,0},{12,4},{16,24},{20,28},{24,16},{28,20},{1,9},{5... | collective-permute-start | bytes 196616 | tf_op jit(solution)/shard_map/ppermute | solution.py:318
  17.4 0.4 collective-permute-start.6
  17.8 2.7 %collective-permute-start.12 = (f32[3,128,128]{2,1,0:T(8,128)S(1)}, f32[3,128,128]{2,1,0:T(8,128)S(1)}, u32[]{:S(2)}, u32[]{:S(2)}) collective-permute-start(f32[3,128,128]{2,1,0:T(8,128)S(1)} %slice_bitcast_fusion.1), channel_id=1, source_target_pairs={{0,3},{1,2},{2,1},{3,0},{4,7},{5,6},{6,5},{7,4},{8,11},{9,10},{10,... | collective-permute-start | bytes 589832 | tf_op jit(solution)/shard_map/ppermute | solution.py:323
  20.5 1.8 %collective-permute-start.10 = (f32[3,128,128]{2,1,0:T(8,128)S(1)}, f32[3,128,128]{2,1,0:T(8,128)S(1)}, u32[]{:S(2)}, u32[]{:S(2)}) collective-permute-start(f32[3,128,128]{2,1,0:T(8,128)S(1)} %slice_bitcast_fusion.1), channel_id=1, source_target_pairs={{0,1},{1,0},{2,3},{3,2},{4,5},{5,4},{6,7},{7,6},{8,9},{9,8},{10,11... | collective-permute-start | bytes 589832 | tf_op jit(solution)/shard_map/ppermute | solution.py:323
  22.4 0.6 %collective-permute-done.6 = f32[2,128,128]{2,1,0:T(8,128)S(1)} collective-permute-done((f32[2,128,128]{2,1,0:T(8,128)S(1)}, f32[2,128,128]{2,1,0:T(8,128)S(1)}, u32[]{:S(2)}, u32[]{:S(2)}) %collective-permute-start.6) | collective-permute-done | bytes 131104 | tf_op jit(solution)/shard_map/ppermute | solution.py:318
  23.0 1.4 %collective-permute-start.8 = (f32[5,128,128]{2,1,0:T(8,128)S(1)}, f32[5,128,128]{2,1,0:T(8,128)S(1)}, u32[]{:S(2)}, u32[]{:S(2)}) collective-permute-start(f32[5,128,128]{2,1,0:T(8,128)S(1)} %broadcast_select_fusion), channel_id=1, source_target_pairs={{0,8},{4,12},{8,0},{12,4},{16,24},{20,28},{24,16},{28,20},{1,9},{5... | collective-permute-start | bytes 983048 | tf_op jit(solution)/shard_map/ppermute | solution.py:318
  24.4 9.8 %shard_map.28 = (f32[512,384]{1,0:T(8,128)S(1)}, f32[384,384]{1,0:T(8,128)S(1)}, f32[1,1,128,128]{3,2,1,0:T(8,128)S(1)}) custom-call(s32[56]{0:T(128)S(1)} %concatenate.10.refs_0_.marks_ref, f32[11,128,128]{2,1,0:T(8,128)S(1)} %constant_dynamic-update-slice_fusion.refs_1_), custom_call_target="tpu_custom_call" | custom-call | flops 24000000000 | bytes 1048576 | tf_op jit(solution)/shard_map/pallas_call | solution.py:200
  34.2 0.1 pad_maximum_fusion.2
  34.3 0.1 collective-permute-start.9
  34.4 3.0 %shard_map.29 = (f32[512,128]{1,0:T(8,128)S(1)}, f32[128,512]{1,0:T(8,128)S(1)}) custom-call(f32[1,1,128,128]{3,2,1,0:T(8,128)S(1)} %get-tuple-element.26.refs_0_, f32[512,384]{1,0:T(8,128)S(1)} %get-tuple-element.27.refs_1_.refs_0_, f32[384,384]{1,0:T(8,128)S(1)} %get-tuple-element.28.refs_2_), custom_call_target="tpu_custom_call" | custom-call | flops 8000000000 | bytes 1048576 | tf_op jit(solution)/shard_map/pallas_call | solution.py:200
  37.4 0.7 %collective-permute-done.11 = f32[3,128,128]{2,1,0:T(8,128)S(1)} collective-permute-done((f32[3,128,128]{2,1,0:T(8,128)S(1)}, f32[3,128,128]{2,1,0:T(8,128)S(1)}, u32[]{:S(2)}, u32[]{:S(2)}) %collective-permute-start.11) | collective-permute-done | bytes 196640 | tf_op jit(solution)/shard_map/ppermute | solution.py:323
  38.1 0.1 pad_maximum_fusion.xc_ref
  38.3 4.0 %shard_map.30 = bf16[3,6,128,128]{3,2,1,0:T(8,128)(2,1)} custom-call(s32[56]{0:T(128)S(1)} %concatenate.10.refs_0_.marks_ref, f32[3,6,128,128]{3,2,1,0:T(8,128)S(1)} %bitcast.42, f32[4,3,128,128]{3,2,1,0:T(8,128)S(1)} %pad_maximum_fusion.1.xr_ref, f32[2,2,5,128,128]{4,3,2,1,0:T(8,128)S(1)} %pad_maximum_fusion.xc_ref, ...), custom_call_target="tpu_custom_call" | custom-call | flops 4000000000 | bytes 4194304 | tf_op jit(solution)/shard_map/pallas_call | solution.py:287
  (27 shorter events, 0.3 us)
Async XLA Ops:
  0.0 6.6 %copy-start = (f32[3,1,6,1,128,128]{5,4,3,2,1,0:T(8,128)S(1)}, f32[3,1,6,1,128,128]{5,4,3,2,1,0:T(8,128)}, u32[]{:S(2)}) copy-start(f32[3,1,6,1,128,128]{5,4,3,2,1,0:T(8,128)} %param.2) | copy-start | bytes 3538948
  0.9 5.6 %collective-permute-start = (f32[128,128]{1,0:T(8,128)S(1)}, f32[128,128]{1,0:T(8,128)S(1)}, u32[]{:S(2)}, u32[]{:S(2)}) collective-permute-start(f32[128,128]{1,0:T(8,128)S(1)} %slice_bitcast_fusion.2), channel_id=1, source_target_pairs={{0,16},{4,20},{8,24},{12,28},{16,0},{20,4},{24,8},{28,12},{1,17},{... | collective-permute-start | bytes 196616 | tf_op jit(solution)/shard_map/ppermute | solution.py:311
  6.6 7.7 %collective-permute-start.3 = (f32[128,128]{1,0:T(8,128)S(1)}, f32[128,128]{1,0:T(8,128)S(1)}, u32[]{:S(2)}, u32[]{:S(2)}) collective-permute-start(f32[128,128]{1,0:T(8,128)S(1)} %get-tuple-element.42), channel_id=1, source_target_pairs={{0,3},{1,2},{2,1},{3,0},{4,7},{5,6},{6,5},{7,4},{8,11},{9,10},{10,... | collective-permute-start | bytes 196616 | tf_op jit(solution)/shard_map/ppermute | solution.py:323
  10.3 5.3 %collective-permute-start.2 = (f32[128,128]{1,0:T(8,128)S(1)}, f32[128,128]{1,0:T(8,128)S(1)}, u32[]{:S(2)}, u32[]{:S(2)}) collective-permute-start(f32[128,128]{1,0:T(8,128)S(1)} %get-tuple-element.42), channel_id=1, source_target_pairs={{0,2},{1,3},{2,0},{3,1},{4,6},{5,7},{6,4},{7,5},{8,10},{9,11},{10,... | collective-permute-start | bytes 196616 | tf_op jit(solution)/shard_map/ppermute | solution.py:323
  10.3 5.3 %collective-permute-start.1 = (f32[128,128]{1,0:T(8,128)S(1)}, f32[128,128]{1,0:T(8,128)S(1)}, u32[]{:S(2)}, u32[]{:S(2)}) collective-permute-start(f32[128,128]{1,0:T(8,128)S(1)} %get-tuple-element.42), channel_id=1, source_target_pairs={{0,1},{1,0},{2,3},{3,2},{4,5},{5,4},{6,7},{7,6},{8,9},{9,8},{10,11... | collective-permute-start | bytes 196616 | tf_op jit(solution)/shard_map/ppermute | solution.py:323
  12.7 10.3 %collective-permute-start.7 = (f32[5,128,128]{2,1,0:T(8,128)S(1)}, f32[5,128,128]{2,1,0:T(8,128)S(1)}, u32[]{:S(2)}, u32[]{:S(2)}) collective-permute-start(f32[5,128,128]{2,1,0:T(8,128)S(1)} %slice_bitcast_fusion), channel_id=1, source_target_pairs={{0,16},{4,20},{8,24},{12,28},{16,0},{20,4},{24,8},{28,12},{1,17},{... | collective-permute-start | bytes 983048 | tf_op jit(solution)/shard_map/ppermute | solution.py:311
  15.7 2.1 %collective-permute-start.4 = (f32[4,128,128]{2,1,0:T(8,128)S(1)}, f32[4,128,128]{2,1,0:T(8,128)S(1)}, u32[]{:S(2)}, u32[]{:S(2)}) collective-permute-start(f32[4,128,128]{2,1,0:T(8,128)S(1)} %pad_maximum_fusion.3), channel_id=1, source_target_pairs={{0,4},{4,0},{8,12},{12,8},{16,20},{20,16},{24,28},{28,24},{1,5},{5... | collective-permute-start | bytes 786440 | tf_op jit(solution)/shard_map/ppermute | solution.py:318
  15.8 4.7 %collective-permute-start.5 = (f32[1,128,128]{2,1,0:T(8,128)S(1)}, f32[1,128,128]{2,1,0:T(8,128)S(1)}, u32[]{:S(2)}, u32[]{:S(2)}) collective-permute-start(f32[1,128,128]{2,1,0:T(8,128)S(1)} %get-tuple-element.44), channel_id=1, source_target_pairs={{0,8},{4,12},{8,0},{12,4},{16,24},{20,28},{24,16},{28,20},{1,9},{5... | collective-permute-start | bytes 196616 | tf_op jit(solution)/shard_map/ppermute | solution.py:318
  17.4 5.6 %collective-permute-start.6 = (f32[2,128,128]{2,1,0:T(8,128)S(1)}, f32[2,128,128]{2,1,0:T(8,128)S(1)}, u32[]{:S(2)}, u32[]{:S(2)}) collective-permute-start(f32[2,128,128]{2,1,0:T(8,128)S(1)} %pad_maximum_fusion.4), channel_id=1, source_target_pairs={{0,12},{4,8},{8,4},{12,0},{16,28},{20,24},{24,20},{28,16},{1,13},{... | collective-permute-start | bytes 393224 | tf_op jit(solution)/shard_map/ppermute | solution.py:318
  17.8 19.5 %collective-permute-start.12 = (f32[3,128,128]{2,1,0:T(8,128)S(1)}, f32[3,128,128]{2,1,0:T(8,128)S(1)}, u32[]{:S(2)}, u32[]{:S(2)}) collective-permute-start(f32[3,128,128]{2,1,0:T(8,128)S(1)} %slice_bitcast_fusion.1), channel_id=1, source_target_pairs={{0,3},{1,2},{2,1},{3,0},{4,7},{5,6},{6,5},{7,4},{8,11},{9,10},{10,... | collective-permute-start | bytes 589832 | tf_op jit(solution)/shard_map/ppermute | solution.py:323
  20.5 17.6 %collective-permute-start.11 = (f32[3,128,128]{2,1,0:T(8,128)S(1)}, f32[3,128,128]{2,1,0:T(8,128)S(1)}, u32[]{:S(2)}, u32[]{:S(2)}) collective-permute-start(f32[3,128,128]{2,1,0:T(8,128)S(1)} %slice_bitcast_fusion.1), channel_id=1, source_target_pairs={{0,2},{1,3},{2,0},{3,1},{4,6},{5,7},{6,4},{7,5},{8,10},{9,11},{10,... | collective-permute-start | bytes 589832 | tf_op jit(solution)/shard_map/ppermute | solution.py:323
  20.5 17.5 %collective-permute-start.10 = (f32[3,128,128]{2,1,0:T(8,128)S(1)}, f32[3,128,128]{2,1,0:T(8,128)S(1)}, u32[]{:S(2)}, u32[]{:S(2)}) collective-permute-start(f32[3,128,128]{2,1,0:T(8,128)S(1)} %slice_bitcast_fusion.1), channel_id=1, source_target_pairs={{0,1},{1,0},{2,3},{3,2},{4,5},{5,4},{6,7},{7,6},{8,9},{9,8},{10,11... | collective-permute-start | bytes 589832 | tf_op jit(solution)/shard_map/ppermute | solution.py:323
  23.0 11.2 %collective-permute-start.8 = (f32[5,128,128]{2,1,0:T(8,128)S(1)}, f32[5,128,128]{2,1,0:T(8,128)S(1)}, u32[]{:S(2)}, u32[]{:S(2)}) collective-permute-start(f32[5,128,128]{2,1,0:T(8,128)S(1)} %broadcast_select_fusion), channel_id=1, source_target_pairs={{0,8},{4,12},{8,0},{12,4},{16,24},{20,28},{24,16},{28,20},{1,9},{5... | collective-permute-start | bytes 983048 | tf_op jit(solution)/shard_map/ppermute | solution.py:318
  34.3 3.8 %collective-permute-start.9 = (f32[2,5,128,128]{3,2,1,0:T(8,128)S(1)}, f32[2,5,128,128]{3,2,1,0:T(8,128)S(1)}, u32[]{:S(2)}, u32[]{:S(2)}) collective-permute-start(f32[2,5,128,128]{3,2,1,0:T(8,128)S(1)} %pad_maximum_fusion.2), channel_id=1, source_target_pairs={{0,4},{4,0},{8,12},{12,8},{16,20},{20,16},{24,28},{28,24},{1,5},{5... | collective-permute-start | bytes 1966088 | tf_op jit(solution)/shard_map/ppermute | solution.py:318

commit v7 on v6

--- a/solution.py
+++ b/solution.py
@@ -217,9 +217,9 @@
     return 2, 2 + tile_rows * tile_cols, 2 + tile_rows * (tile_cols + LEAD)
 
 
-def update_kernel(cols, marks_ref, a_ref, xr_ref, xc_ref, *refs):
+def update_kernel(cols, marks_ref, a_ref, xr_ref, xc_ref, xc_far_ref, *refs):
     l_cols, k_rows = refs[: len(PARTS)], refs[len(PARTS) : 2 * len(PARTS)]
-    out_ref, x_ref, y_ref, z_ref, k_ref = refs[2 * len(PARTS) :]
+    out_ref, x_ref, y_ref, z_ref, k_ref, done_ref, sems = refs[2 * len(PARTS) :]
     part = [p for p, (low, high) in enumerate(PARTS) for _ in range(low, high)]
     tile_rows, tile_cols, n, _ = a_ref.shape
     my_row, my_col = marks_ref[0], marks_ref[1]
@@ -242,7 +242,8 @@
             put(x_ref, at(i, n), at(k, n), xr_ref[(my_col ^ k) & (LEAD - 1), i] * mark(of_rows + i * LEAD + k))
         apart = (my_row ^ k) & (LEAD - 1)
         for j in range(skip, tile_cols):
-            tile = xc_ref[apart & 1, apart >> 1, j - skip] * mark(of_cols + k * tile_cols + j)
+            near, far = xc_ref[apart >> 1, j - skip], xc_far_ref[apart >> 1, j - skip]
+            tile = jnp.where(apart & 1 == 0, near, far) * mark(of_cols + k * tile_cols + j)
             put(y_ref, at(k, n), at(j - skip, n), tile)
     for b in range(LEAD):
         rows_of = k_rows[part[b]]
@@ -254,30 +255,43 @@
     put(z_ref, every, head, dot_3(pair(x_ref, every, head), k1, ROW_BY_ROW))
     put(z_ref, every, tail, dot_3(pair(x_ref, every, every), k2, ROW_BY_ROW))
     z_rows = pair(z_ref, every, every)
+
+    def panel(i):
+        for c in range(LEAD):
+
+            @pl.when(my_col == c)
+            def _():
+                done_ref[i, 0] = z_ref[0, at(i, n), at(c, n)]
+                if i == 0:
+                    for r in range(LEAD):
+
+                        @pl.when(my_row == r)
+                        def _():
+                            if r >= c:
+                                tile = l_cols[part[c]][at(r, n), at(c - PARTS[part[c]][0], n)]
+                                done_ref[0, 0] = tile.astype(jnp.bfloat16)
+                            else:
+                                done_ref[0, 0] = jnp.zeros((n, n), jnp.bfloat16)
+
     z_head = split(dot_3(k1, pair(y_ref, head, every)))
     z_tail = split(dot_3(k2, pair(y_ref, every, every)))
     product = dot_3(z_rows, [jnp.concatenate(parts, axis=0) for parts in zip(z_head, z_tail)])
+    copies = []
     for i in range(tile_rows):
         in_lead = jnp.logical_and(i == 0, my_row < LEAD)
         for j in range(skip, tile_cols):
             rest = a_ref[i, j] * mark(of_tiles + i * tile_cols + j) - product[at(i, n), at(j - skip, n)]
-            out_ref[i, j] = jnp.where(in_lead, 0.0, rest).astype(jnp.bfloat16)
+            done_ref[i, j] = jnp.where(in_lead, 0.0, rest).astype(jnp.bfloat16)
+        if skip:
+            copies.append(pltpu.make_async_copy(done_ref.at[i, 1:], out_ref.at[i, 1:], sems.at[i]))
+            copies[-1].start()
     for i in range(tile_rows):
-        for c in range(LEAD):
-
-            @pl.when(my_col == c)
-            def _():
-                out_ref[i, 0] = z_ref[0, at(i, n), at(c, n)]
-                if i == 0:
-                    for r in range(LEAD):
-
-                        @pl.when(my_row == r)
-                        def _():
-                            if r >= c:
-                                tile = l_cols[part[c]][at(r, n), at(c - PARTS[part[c]][0], n)]
-                                out_ref[0, 0] = tile.astype(jnp.bfloat16)
-                            else:
-                                out_ref[0, 0] = jnp.zeros((n, n), jnp.bfloat16)
+        panel(i)
+    panels = slice(0, 1) if skip else slice(0, tile_cols)
+    copies.append(pltpu.make_async_copy(done_ref.at[:, panels], out_ref.at[:, panels], sems.at[tile_rows]))
+    copies[-1].start()
+    for copy in copies:
+        copy.wait()
 
 
 def update(cols, marks, mine, from_cols, from_rows, factors):
@@ -287,17 +301,19 @@
     return pl.pallas_call(
         functools.partial(update_kernel, cols),
         out_shape=jax.ShapeDtypeStruct(mine.shape, jnp.bfloat16),
-        in_specs=[SMEM] + [VMEM] * (3 + 2 * len(PARTS)),
-        out_specs=VMEM,
+        in_specs=[SMEM] + [VMEM] * (4 + 2 * len(PARTS)),
+        out_specs=pl.BlockSpec(memory_space=pl.ANY),
         scratch_shapes=[
             pltpu.VMEM((2, tile_rows * n, width), jnp.bfloat16),
             pltpu.VMEM((2, width, used * n), jnp.bfloat16),
             pltpu.VMEM((2, tile_rows * n, width), jnp.bfloat16),
             pltpu.VMEM((2, width, width), jnp.bfloat16),
+            pltpu.VMEM(mine.shape, jnp.bfloat16),
+            pltpu.SemaphoreType.DMA((tile_rows + 1,)),
         ],
         compiler_params=pltpu.CompilerParams(vmem_limit_bytes=40 * 2**20),
         cost_estimate=pl.CostEstimate(flops=4 * 10**9, bytes_accessed=2**22, transcendentals=0),
-    )(marks, mine, from_cols, from_rows, *factors)
+    )(marks, mine, from_cols, *from_rows, *factors)
 
 
 def copy_down(value, axis):
@@ -320,7 +336,8 @@
 
 def exchange(value, axis):
     size = lax.axis_size(axis)
-    return [value] + [lax.ppermute(value, axis, [(i, i ^ s) for i in range(size)]) for s in range(1, LEAD)]
+    parts = [lax.ppermute(value, axis, [(i, i ^ s) for i in range(size)]) for s in range(LEAD - 1, 0, -1)]
+    return [value] + parts[::-1]
 
 
 def on_device(covariance, tile_mask):
@@ -361,7 +378,7 @@
         args = [state[0], jnp.concatenate(l_cols, axis=1), k_rows[0]]
     row, *moved = lax.optimization_barrier((k_rows[-1], *across, *down))
     k_rows[-1] = row
-    across, down = jnp.stack(moved[:2]), jnp.stack(moved[2:])
+    across, down = moved[:2], jnp.stack(moved[2:])
     out = update(cols, marks, mine, down, across, (*l_cols, *k_rows))
     return out.reshape(tile_rows, 1, tile_cols, 1, n, n)
 

time: 42.6 us -> 42.4 us (level)
  no operation moved by 1% of the time
where the time goes in v7:
time: 42.4 us; the launch traced here: 42.1 us
  starting transfers between devices  17 us (40%)
  Pallas kernels  16.8 us (40%)
  local copies, waits for them, and re-layouts  5.29 us (12%)
  waiting for transfers between devices  2.66 us (6%)
    pallas_call x2, Pallas kernels, factor_columns(): pl.pallas_call(functools.partial(factor_kernel, low, high), out_shape=[ja...  12.8 us
    ppermute x6, starting transfers between devices, exchange(): lax.ppermute(value, axis, [(i, i ^ s) for i in range(size)])  8.97 us
    ppermute x2, starting transfers between devices, copy_down(): value = jnp.where(index >= have, lax.ppermute(value, axis, pairs), value)  4.6 us
    pallas_call x1, Pallas kernels, update(): pl.pallas_call(functools.partial(update_kernel, cols), out_shape=jax.Shap...  3.99 us
    ppermute x5, starting transfers between devices, swap(): lax.ppermute(value, axis, [(i, i ^ bit) for i in range(size)])  3.47 us
    ppermute x6, waiting for transfers between devices, exchange(): lax.ppermute(value, axis, [(i, i ^ s) for i in range(size)])  2.08 us
    squeeze x1, local copies, waits for them, and re-layouts, on_device(): _, across = lax.optimization_barrier((lead, mine[0, skip:]))  0.99 us
    squeeze x1, local copies, waits for them, and re-layouts, on_device(): _, down = lax.optimization_barrier((partner, mine[:, 0]))  0.95 us
  transfers between devices with their start and end apart: 13, of which 4 were waited for; matrix products, arithmetic and copies ran while one was open for 11% of the time, Pallas kernels for 30%

profile of v7, /device:TPU:0, one launch (start us, length us, event | category | flops | bytes accessed | tf_op | source)
XLA Modules:
  0.0 42.1 jit_solution(9123253513546445595)
XLA Ops:
  0.0 0.9 %slice_bitcast_fusion.2 = f32[128,128]{1,0:T(8,128)S(1)} fusion(f32[3,6,128,128]{3,2,1,0:T(8,128)} %bitcast.36), kind=kLoop, calls=%fused_computation.7 | loop fusion | bytes 131072 | tf_op jit(solution)/shard_map/squeeze | solution.py:354
  0.9 3.0 %collective-permute-start = (f32[128,128]{1,0:T(8,128)S(1)}, f32[128,128]{1,0:T(8,128)S(1)}, u32[]{:S(2)}, u32[]{:S(2)}) collective-permute-start(f32[128,128]{1,0:T(8,128)S(1)} %slice_bitcast_fusion.2), channel_id=1, source_target_pairs={{0,16},{4,20},{8,24},{12,28},{16,0},{20,4},{24,8},{28,12},{1,17},{... | collective-permute-start | bytes 196616 | tf_op jit(solution)/shard_map/ppermute | solution.py:327
  3.9 1.0 %slice_bitcast_fusion = f32[5,128,128]{2,1,0:T(8,128)S(1)} fusion(f32[3,6,128,128]{3,2,1,0:T(8,128)} %bitcast.37), kind=kLoop, calls=%fused_computation.2 | loop fusion | bytes 655360 | tf_op jit(solution)/shard_map/squeeze | solution.py:355
  4.9 0.9 %slice_bitcast_fusion.1 = f32[3,128,128]{2,1,0:T(8,128)S(1)} fusion(f32[3,6,128,128]{3,2,1,0:T(8,128)} %bitcast.38), kind=kLoop, calls=%fused_computation.4 | loop fusion | bytes 393216 | tf_op jit(solution)/shard_map/squeeze | solution.py:363
  5.9 0.7 %slice.16 = s32[4,24]{1,0:T(4,128)S(1)} slice(s32[24,24]{1,0:T(8,128)} %param.3), slice={[0:4], [0:24]} | slice | bytes 768 | tf_op jit(solution)/shard_map/slice | solution.py:350
  6.6 3.8 %collective-permute-start.3 = (f32[128,128]{1,0:T(8,128)S(1)}, f32[128,128]{1,0:T(8,128)S(1)}, u32[]{:S(2)}, u32[]{:S(2)}) collective-permute-start(f32[128,128]{1,0:T(8,128)S(1)} %get-tuple-element.42), channel_id=1, source_target_pairs={{0,3},{1,2},{2,1},{3,0},{4,7},{5,6},{6,5},{7,4},{8,11},{9,10},{10,... | collective-permute-start | bytes 196616 | tf_op jit(solution)/shard_map/ppermute | solution.py:339
  10.3 0.7 %collective-permute-start.1 = (f32[128,128]{1,0:T(8,128)S(1)}, f32[128,128]{1,0:T(8,128)S(1)}, u32[]{:S(2)}, u32[]{:S(2)}) collective-permute-start(f32[128,128]{1,0:T(8,128)S(1)} %get-tuple-element.42), channel_id=1, source_target_pairs={{0,1},{1,0},{2,3},{3,2},{4,5},{5,4},{6,7},{7,6},{8,9},{9,8},{10,11... | collective-permute-start | bytes 196616 | tf_op jit(solution)/shard_map/ppermute | solution.py:339
  11.0 0.7 %constant_dynamic-slice_fusion.2 = s32[3,1,24]{2,1,0:T(1,128)S(1)} fusion(s32[3,8,24]{2,1,0:T(8,128)} %bitcast.52, s32[]{:T(128)S(6)} %select_n.33), kind=kLoop, calls=%fused_computation.20 | loop fusion | bytes 580 | tf_op jit(solution)/shard_map/jit(dynamic_index_in_dim)/dynamic_slice | solution.py:348
  11.8 0.1 reshape.28
  11.8 0.1 reshape.30
  11.9 0.2 dynamic-slice_reduce_fusion.1
  12.1 0.1 reshape.29
  12.2 0.1 reshape.31
  12.3 0.2 dynamic-slice_reduce_fusion
  12.5 0.1 reshape.32
  12.6 0.1 concatenate.10.refs_0_.marks_ref
  12.7 1.6 %collective-permute-start.7 = (f32[5,128,128]{2,1,0:T(8,128)S(1)}, f32[5,128,128]{2,1,0:T(8,128)S(1)}, u32[]{:S(2)}, u32[]{:S(2)}) collective-permute-start(f32[5,128,128]{2,1,0:T(8,128)S(1)} %slice_bitcast_fusion), channel_id=1, source_target_pairs={{0,16},{4,20},{8,24},{12,28},{16,0},{20,4},{24,8},{28,12},{1,17},{... | collective-permute-start | bytes 983048 | tf_op jit(solution)/shard_map/ppermute | solution.py:327
  14.3 1.3 %collective-permute-done.2 = f32[128,128]{1,0:T(8,128)S(1)} collective-permute-done((f32[128,128]{1,0:T(8,128)S(1)}, f32[128,128]{1,0:T(8,128)S(1)}, u32[]{:S(2)}, u32[]{:S(2)}) %collective-permute-start.2) | collective-permute-done | bytes 65568 | tf_op jit(solution)/shard_map/ppermute | solution.py:339
  15.6 0.1 collective-permute-done.1
  15.7 0.1 collective-permute-start.4
  15.8 1.6 %collective-permute-start.5 = (f32[1,128,128]{2,1,0:T(8,128)S(1)}, f32[1,128,128]{2,1,0:T(8,128)S(1)}, u32[]{:S(2)}, u32[]{:S(2)}) collective-permute-start(f32[1,128,128]{2,1,0:T(8,128)S(1)} %get-tuple-element.44), channel_id=1, source_target_pairs={{0,8},{4,12},{8,0},{12,4},{16,24},{20,28},{24,16},{28,20},{1,9},{5... | collective-permute-start | bytes 196616 | tf_op jit(solution)/shard_map/ppermute | solution.py:334
  17.4 0.4 collective-permute-start.6
  17.8 2.7 %collective-permute-start.12 = (f32[3,128,128]{2,1,0:T(8,128)S(1)}, f32[3,128,128]{2,1,0:T(8,128)S(1)}, u32[]{:S(2)}, u32[]{:S(2)}) collective-permute-start(f32[3,128,128]{2,1,0:T(8,128)S(1)} %slice_bitcast_fusion.1), channel_id=1, source_target_pairs={{0,3},{1,2},{2,1},{3,0},{4,7},{5,6},{6,5},{7,4},{8,11},{9,10},{10,... | collective-permute-start | bytes 589832 | tf_op jit(solution)/shard_map/ppermute | solution.py:339
  20.5 1.8 %collective-permute-start.10 = (f32[3,128,128]{2,1,0:T(8,128)S(1)}, f32[3,128,128]{2,1,0:T(8,128)S(1)}, u32[]{:S(2)}, u32[]{:S(2)}) collective-permute-start(f32[3,128,128]{2,1,0:T(8,128)S(1)} %slice_bitcast_fusion.1), channel_id=1, source_target_pairs={{0,1},{1,0},{2,3},{3,2},{4,5},{5,4},{6,7},{7,6},{8,9},{9,8},{10,11... | collective-permute-start | bytes 589832 | tf_op jit(solution)/shard_map/ppermute | solution.py:339
  22.4 0.6 %collective-permute-done.6 = f32[2,128,128]{2,1,0:T(8,128)S(1)} collective-permute-done((f32[2,128,128]{2,1,0:T(8,128)S(1)}, f32[2,128,128]{2,1,0:T(8,128)S(1)}, u32[]{:S(2)}, u32[]{:S(2)}) %collective-permute-start.6) | collective-permute-done | bytes 131104 | tf_op jit(solution)/shard_map/ppermute | solution.py:334
  23.0 1.4 %collective-permute-start.8 = (f32[5,128,128]{2,1,0:T(8,128)S(1)}, f32[5,128,128]{2,1,0:T(8,128)S(1)}, u32[]{:S(2)}, u32[]{:S(2)}) collective-permute-start(f32[5,128,128]{2,1,0:T(8,128)S(1)} %broadcast_select_fusion), channel_id=1, source_target_pairs={{0,8},{4,12},{8,0},{12,4},{16,24},{20,28},{24,16},{28,20},{1,9},{5... | collective-permute-start | bytes 983048 | tf_op jit(solution)/shard_map/ppermute | solution.py:334
  24.4 9.8 %shard_map.28 = (f32[512,384]{1,0:T(8,128)S(1)}, f32[384,384]{1,0:T(8,128)S(1)}, f32[1,1,128,128]{3,2,1,0:T(8,128)S(1)}) custom-call(s32[56]{0:T(128)S(1)} %concatenate.10.refs_0_.marks_ref, f32[11,128,128]{2,1,0:T(8,128)S(1)} %constant_dynamic-update-slice_fusion.refs_1_), custom_call_target="tpu_custom_call" | custom-call | flops 24000000000 | bytes 1048576 | tf_op jit(solution)/shard_map/pallas_call | solution.py:200
  34.3 0.1 collective-permute-start.9
  34.4 3.0 %shard_map.29 = (f32[512,128]{1,0:T(8,128)S(1)}, f32[128,512]{1,0:T(8,128)S(1)}) custom-call(f32[1,1,128,128]{3,2,1,0:T(8,128)S(1)} %get-tuple-element.26.refs_0_, f32[512,384]{1,0:T(8,128)S(1)} %get-tuple-element.27.refs_1_.refs_0_, f32[384,384]{1,0:T(8,128)S(1)} %get-tuple-element.28.refs_2_), custom_call_target="tpu_custom_call" | custom-call | flops 8000000000 | bytes 1048576 | tf_op jit(solution)/shard_map/pallas_call | solution.py:200
  37.3 0.7 %collective-permute-done.11 = f32[3,128,128]{2,1,0:T(8,128)S(1)} collective-permute-done((f32[3,128,128]{2,1,0:T(8,128)S(1)}, f32[3,128,128]{2,1,0:T(8,128)S(1)}, u32[]{:S(2)}, u32[]{:S(2)}) %collective-permute-start.11) | collective-permute-done | bytes 196640 | tf_op jit(solution)/shard_map/ppermute | solution.py:339
  38.1 0.1 pad_maximum_fusion.xr_ref
  38.1 4.0 %shard_map.30 = bf16[3,6,128,128]{3,2,1,0:T(8,128)(2,1)} custom-call(s32[56]{0:T(128)S(1)} %concatenate.10.refs_0_.marks_ref, f32[3,6,128,128]{3,2,1,0:T(8,128)S(1)} %bitcast.40, f32[4,3,128,128]{3,2,1,0:T(8,128)S(1)} %pad_maximum_fusion.xr_ref, f32[2,5,128,128]{3,2,1,0:T(8,128)S(1)} %pad_maximum_fusion.1.xc_ref, ...), custom_call_target="tpu_custom_call" | custom-call | flops 4000000000 | bytes 4194304 | tf_op jit(solution)/shard_map/pallas_call | solution.py:301
  (26 shorter events, 0.2 us)
Async XLA Ops:
  0.0 6.6 %copy-start = (f32[3,1,6,1,128,128]{5,4,3,2,1,0:T(8,128)S(1)}, f32[3,1,6,1,128,128]{5,4,3,2,1,0:T(8,128)}, u32[]{:S(2)}) copy-start(f32[3,1,6,1,128,128]{5,4,3,2,1,0:T(8,128)} %param.2) | copy-start | bytes 3538948
  0.9 5.6 %collective-permute-start = (f32[128,128]{1,0:T(8,128)S(1)}, f32[128,128]{1,0:T(8,128)S(1)}, u32[]{:S(2)}, u32[]{:S(2)}) collective-permute-start(f32[128,128]{1,0:T(8,128)S(1)} %slice_bitcast_fusion.2), channel_id=1, source_target_pairs={{0,16},{4,20},{8,24},{12,28},{16,0},{20,4},{24,8},{28,12},{1,17},{... | collective-permute-start | bytes 196616 | tf_op jit(solution)/shard_map/ppermute | solution.py:327
  6.6 7.7 %collective-permute-start.3 = (f32[128,128]{1,0:T(8,128)S(1)}, f32[128,128]{1,0:T(8,128)S(1)}, u32[]{:S(2)}, u32[]{:S(2)}) collective-permute-start(f32[128,128]{1,0:T(8,128)S(1)} %get-tuple-element.42), channel_id=1, source_target_pairs={{0,3},{1,2},{2,1},{3,0},{4,7},{5,6},{6,5},{7,4},{8,11},{9,10},{10,... | collective-permute-start | bytes 196616 | tf_op jit(solution)/shard_map/ppermute | solution.py:339
  10.3 5.3 %collective-permute-start.2 = (f32[128,128]{1,0:T(8,128)S(1)}, f32[128,128]{1,0:T(8,128)S(1)}, u32[]{:S(2)}, u32[]{:S(2)}) collective-permute-start(f32[128,128]{1,0:T(8,128)S(1)} %get-tuple-element.42), channel_id=1, source_target_pairs={{0,2},{1,3},{2,0},{3,1},{4,6},{5,7},{6,4},{7,5},{8,10},{9,11},{10,... | collective-permute-start | bytes 196616 | tf_op jit(solution)/shard_map/ppermute | solution.py:339
  10.3 5.3 %collective-permute-start.1 = (f32[128,128]{1,0:T(8,128)S(1)}, f32[128,128]{1,0:T(8,128)S(1)}, u32[]{:S(2)}, u32[]{:S(2)}) collective-permute-start(f32[128,128]{1,0:T(8,128)S(1)} %get-tuple-element.42), channel_id=1, source_target_pairs={{0,1},{1,0},{2,3},{3,2},{4,5},{5,4},{6,7},{7,6},{8,9},{9,8},{10,11... | collective-permute-start | bytes 196616 | tf_op jit(solution)/shard_map/ppermute | solution.py:339
  12.7 10.3 %collective-permute-start.7 = (f32[5,128,128]{2,1,0:T(8,128)S(1)}, f32[5,128,128]{2,1,0:T(8,128)S(1)}, u32[]{:S(2)}, u32[]{:S(2)}) collective-permute-start(f32[5,128,128]{2,1,0:T(8,128)S(1)} %slice_bitcast_fusion), channel_id=1, source_target_pairs={{0,16},{4,20},{8,24},{12,28},{16,0},{20,4},{24,8},{28,12},{1,17},{... | collective-permute-start | bytes 983048 | tf_op jit(solution)/shard_map/ppermute | solution.py:327
  15.7 2.1 %collective-permute-start.4 = (f32[4,128,128]{2,1,0:T(8,128)S(1)}, f32[4,128,128]{2,1,0:T(8,128)S(1)}, u32[]{:S(2)}, u32[]{:S(2)}) collective-permute-start(f32[4,128,128]{2,1,0:T(8,128)S(1)} %pad_maximum_fusion.2), channel_id=1, source_target_pairs={{0,4},{4,0},{8,12},{12,8},{16,20},{20,16},{24,28},{28,24},{1,5},{5... | collective-permute-start | bytes 786440 | tf_op jit(solution)/shard_map/ppermute | solution.py:334
  15.8 4.7 %collective-permute-start.5 = (f32[1,128,128]{2,1,0:T(8,128)S(1)}, f32[1,128,128]{2,1,0:T(8,128)S(1)}, u32[]{:S(2)}, u32[]{:S(2)}) collective-permute-start(f32[1,128,128]{2,1,0:T(8,128)S(1)} %get-tuple-element.44), channel_id=1, source_target_pairs={{0,8},{4,12},{8,0},{12,4},{16,24},{20,28},{24,16},{28,20},{1,9},{5... | collective-permute-start | bytes 196616 | tf_op jit(solution)/shard_map/ppermute | solution.py:334
  17.4 5.6 %collective-permute-start.6 = (f32[2,128,128]{2,1,0:T(8,128)S(1)}, f32[2,128,128]{2,1,0:T(8,128)S(1)}, u32[]{:S(2)}, u32[]{:S(2)}) collective-permute-start(f32[2,128,128]{2,1,0:T(8,128)S(1)} %pad_maximum_fusion.3), channel_id=1, source_target_pairs={{0,12},{4,8},{8,4},{12,0},{16,28},{20,24},{24,20},{28,16},{1,13},{... | collective-permute-start | bytes 393224 | tf_op jit(solution)/shard_map/ppermute | solution.py:334
  17.8 19.5 %collective-permute-start.12 = (f32[3,128,128]{2,1,0:T(8,128)S(1)}, f32[3,128,128]{2,1,0:T(8,128)S(1)}, u32[]{:S(2)}, u32[]{:S(2)}) collective-permute-start(f32[3,128,128]{2,1,0:T(8,128)S(1)} %slice_bitcast_fusion.1), channel_id=1, source_target_pairs={{0,3},{1,2},{2,1},{3,0},{4,7},{5,6},{6,5},{7,4},{8,11},{9,10},{10,... | collective-permute-start | bytes 589832 | tf_op jit(solution)/shard_map/ppermute | solution.py:339
  20.5 17.6 %collective-permute-start.11 = (f32[3,128,128]{2,1,0:T(8,128)S(1)}, f32[3,128,128]{2,1,0:T(8,128)S(1)}, u32[]{:S(2)}, u32[]{:S(2)}) collective-permute-start(f32[3,128,128]{2,1,0:T(8,128)S(1)} %slice_bitcast_fusion.1), channel_id=1, source_target_pairs={{0,2},{1,3},{2,0},{3,1},{4,6},{5,7},{6,4},{7,5},{8,10},{9,11},{10,... | collective-permute-start | bytes 589832 | tf_op jit(solution)/shard_map/ppermute | solution.py:339
  20.5 17.5 %collective-permute-start.10 = (f32[3,128,128]{2,1,0:T(8,128)S(1)}, f32[3,128,128]{2,1,0:T(8,128)S(1)}, u32[]{:S(2)}, u32[]{:S(2)}) collective-permute-start(f32[3,128,128]{2,1,0:T(8,128)S(1)} %slice_bitcast_fusion.1), channel_id=1, source_target_pairs={{0,1},{1,0},{2,3},{3,2},{4,5},{5,4},{6,7},{7,6},{8,9},{9,8},{10,11... | collective-permute-start | bytes 589832 | tf_op jit(solution)/shard_map/ppermute | solution.py:339
  23.0 11.2 %collective-permute-start.8 = (f32[5,128,128]{2,1,0:T(8,128)S(1)}, f32[5,128,128]{2,1,0:T(8,128)S(1)}, u32[]{:S(2)}, u32[]{:S(2)}) collective-permute-start(f32[5,128,128]{2,1,0:T(8,128)S(1)} %broadcast_select_fusion), channel_id=1, source_target_pairs={{0,8},{4,12},{8,0},{12,4},{16,24},{20,28},{24,16},{28,20},{1,9},{5... | collective-permute-start | bytes 983048 | tf_op jit(solution)/shard_map/ppermute | solution.py:334
  34.3 3.8 %collective-permute-start.9 = (f32[2,5,128,128]{3,2,1,0:T(8,128)S(1)}, f32[2,5,128,128]{3,2,1,0:T(8,128)S(1)}, u32[]{:S(2)}, u32[]{:S(2)}) collective-permute-start(f32[2,5,128,128]{3,2,1,0:T(8,128)S(1)} %pad_maximum_fusion.1.xc_ref), channel_id=1, source_target_pairs={{0,4},{4,0},{8,12},{12,8},{16,20},{20,16},{24,28},{28,24},{1,5},{5... | collective-permute-start | bytes 1966088 | tf_op jit(solution)/shard_map/ppermute | solution.py:334

commit v8 on v7

--- a/solution.py
+++ b/solution.py
@@ -352,8 +352,7 @@
     marks = jnp.concatenate([place, of_tiles.reshape(-1), of_rows[:, :LEAD].reshape(-1), of_cols.reshape(-1)])
     skip = 1 if cols == LEAD else 0
     lead = copy_down(mine[0, 0], "row")
-    _, across = lax.optimization_barrier((lead, mine[0, skip:]))
-    across = copy_down(across, "row")
+    across = copy_down(mine[0, skip:], "row")
     lead = jnp.stack(exchange(copy_down(lead, "col"), "col"))
     corner = lax.dynamic_index_in_dim(lead, (my_row ^ my_col) & (LEAD - 1), 0)
     beside = lax.dynamic_index_in_dim(lead, (my_row ^ my_col ^ 1) & (LEAD - 1), 0)

time: 42.4 us -> 42.7 us (level)
  waiting for transfers between devices: 2.66 us -> 4.07 us
  starting transfers between devices: 17 us -> 15.9 us
    ppermute x6, waiting for transfers between devices: 2.08 us -> 4.05 us  [exchange(): lax.ppermute(value, axis, [(i, i ^ s) for i in range(size)])]
    ppermute x2, starting transfers between devices: 4.6 us -> 3.04 us  [copy_down(): value = jnp.where(index >= have, lax.ppermute(value, axis, pairs), value)]
    ppermute x5, waiting for transfers between devices: 0.57 us -> 0.01 us  [swap(): lax.ppermute(value, axis, [(i, i ^ bit) for i in range(size)])]
  transfers between devices with their start and end apart: 13 -> 13, of which waited for: 4 -> 3; matrix products, arithmetic and copies ran while one was open for 11% -> 11% of each run, Pallas kernels for 30% -> 30%
where the time goes in v8:
time: 42.7 us; the launch traced here: 42.4 us
  Pallas kernels  16.8 us (39%)
  starting transfers between devices  15.9 us (37%)
  local copies, waits for them, and re-layouts  5.3 us (12%)
  waiting for transfers between devices  4.07 us (10%)
    pallas_call x2, Pallas kernels, factor_columns(): pl.pallas_call(functools.partial(factor_kernel, low, high), out_shape=[ja...  12.8 us
    ppermute x6, starting transfers between devices, exchange(): lax.ppermute(value, axis, [(i, i ^ s) for i in range(size)])  9.25 us
    ppermute x6, waiting for transfers between devices, exchange(): lax.ppermute(value, axis, [(i, i ^ s) for i in range(size)])  4.05 us
    pallas_call x1, Pallas kernels, update(): pl.pallas_call(functools.partial(update_kernel, cols), out_shape=jax.Shap...  3.97 us
    ppermute x5, starting transfers between devices, swap(): lax.ppermute(value, axis, [(i, i ^ bit) for i in range(size)])  3.66 us
    ppermute x2, starting transfers between devices, copy_down(): value = jnp.where(index >= have, lax.ppermute(value, axis, pairs), value)  3.04 us
    squeeze x1, local copies, waits for them, and re-layouts, on_device(): across = copy_down(mine[0, skip:], 'row')  0.99 us
    squeeze x1, local copies, waits for them, and re-layouts, on_device(): _, down = lax.optimization_barrier((partner, mine[:, 0]))  0.95 us
  transfers between devices with their start and end apart: 13, of which 3 were waited for; matrix products, arithmetic and copies ran while one was open for 11% of the time, Pallas kernels for 30%

profile of v8, /device:TPU:0, one launch (start us, length us, event | category | flops | bytes accessed | tf_op | source)
XLA Modules:
  0.0 42.4 jit_solution(5822940211215989762)
XLA Ops:
  0.0 0.9 %slice_bitcast_fusion.2 = f32[128,128]{1,0:T(8,128)S(1)} fusion(f32[3,6,128,128]{3,2,1,0:T(8,128)} %bitcast.38), kind=kLoop, calls=%fused_computation.7 | loop fusion | bytes 131072 | tf_op jit(solution)/shard_map/squeeze | solution.py:354
  0.9 3.0 %collective-permute-start = (f32[128,128]{1,0:T(8,128)S(1)}, f32[128,128]{1,0:T(8,128)S(1)}, u32[]{:S(2)}, u32[]{:S(2)}) collective-permute-start(f32[128,128]{1,0:T(8,128)S(1)} %slice_bitcast_fusion.2), channel_id=1, source_target_pairs={{0,16},{4,20},{8,24},{12,28},{16,0},{20,4},{24,8},{28,12},{1,17},{... | collective-permute-start | bytes 196616 | tf_op jit(solution)/shard_map/ppermute | solution.py:327
  3.9 1.0 %slice_bitcast_fusion = f32[5,128,128]{2,1,0:T(8,128)S(1)} fusion(f32[3,6,128,128]{3,2,1,0:T(8,128)} %bitcast.39), kind=kLoop, calls=%fused_computation.2 | loop fusion | bytes 655360 | tf_op jit(solution)/shard_map/squeeze | solution.py:355
  4.9 0.1 collective-permute-start.7
  5.0 0.9 %slice_bitcast_fusion.1 = f32[3,128,128]{2,1,0:T(8,128)S(1)} fusion(f32[3,6,128,128]{3,2,1,0:T(8,128)} %bitcast.40), kind=kLoop, calls=%fused_computation.4 | loop fusion | bytes 393216 | tf_op jit(solution)/shard_map/squeeze | solution.py:362
  5.9 0.7 %slice.16 = s32[4,24]{1,0:T(4,128)S(1)} slice(s32[24,24]{1,0:T(8,128)} %param.3), slice={[0:4], [0:24]} | slice | bytes 768 | tf_op jit(solution)/shard_map/slice | solution.py:350
  6.7 4.2 %collective-permute-start.3 = (f32[128,128]{1,0:T(8,128)S(1)}, f32[128,128]{1,0:T(8,128)S(1)}, u32[]{:S(2)}, u32[]{:S(2)}) collective-permute-start(f32[128,128]{1,0:T(8,128)S(1)} %get-tuple-element.40), channel_id=1, source_target_pairs={{0,3},{1,2},{2,1},{3,0},{4,7},{5,6},{6,5},{7,4},{8,11},{9,10},{10,... | collective-permute-start | bytes 196616 | tf_op jit(solution)/shard_map/ppermute | solution.py:339
  10.8 0.0 collective-permute-start.2
  10.8 0.6 %collective-permute-start.1 = (f32[128,128]{1,0:T(8,128)S(1)}, f32[128,128]{1,0:T(8,128)S(1)}, u32[]{:S(2)}, u32[]{:S(2)}) collective-permute-start(f32[128,128]{1,0:T(8,128)S(1)} %get-tuple-element.40), channel_id=1, source_target_pairs={{0,1},{1,0},{2,3},{3,2},{4,5},{5,4},{6,7},{7,6},{8,9},{9,8},{10,11... | collective-permute-start | bytes 196616 | tf_op jit(solution)/shard_map/ppermute | solution.py:339
  11.5 0.7 %constant_dynamic-slice_fusion.2 = s32[3,1,24]{2,1,0:T(1,128)S(1)} fusion(s32[3,8,24]{2,1,0:T(8,128)} %bitcast.55, s32[]{:T(128)S(6)} %select_n.33), kind=kLoop, calls=%fused_computation.20 | loop fusion | bytes 580 | tf_op jit(solution)/shard_map/jit(dynamic_index_in_dim)/dynamic_slice | solution.py:348
  12.2 0.1 reshape.28
  12.3 0.1 reshape.30
  12.3 0.2 dynamic-slice_reduce_fusion.1
  12.6 0.1 reshape.29
  12.6 0.1 reshape.31
  12.7 0.2 dynamic-slice_reduce_fusion
  13.0 0.1 reshape.32
  13.0 0.1 concatenate.10.refs_0_.marks_ref
  13.1 0.7 %collective-permute-done.3 = f32[128,128]{1,0:T(8,128)S(1)} collective-permute-done((f32[128,128]{1,0:T(8,128)S(1)}, f32[128,128]{1,0:T(8,128)S(1)}, u32[]{:S(2)}, u32[]{:S(2)}) %collective-permute-start.3) | collective-permute-done | bytes 65568 | tf_op jit(solution)/shard_map/ppermute | solution.py:339
  13.8 2.3 %collective-permute-done.2 = f32[128,128]{1,0:T(8,128)S(1)} collective-permute-done((f32[128,128]{1,0:T(8,128)S(1)}, f32[128,128]{1,0:T(8,128)S(1)}, u32[]{:S(2)}, u32[]{:S(2)}) %collective-permute-start.2) | collective-permute-done | bytes 65568 | tf_op jit(solution)/shard_map/ppermute | solution.py:339
  16.1 0.1 collective-permute-start.4
  16.2 1.6 %collective-permute-start.5 = (f32[1,128,128]{2,1,0:T(8,128)S(1)}, f32[1,128,128]{2,1,0:T(8,128)S(1)}, u32[]{:S(2)}, u32[]{:S(2)}) collective-permute-start(f32[1,128,128]{2,1,0:T(8,128)S(1)} %get-tuple-element.42), channel_id=1, source_target_pairs={{0,8},{4,12},{8,0},{12,4},{16,24},{20,28},{24,16},{28,20},{1,9},{5... | collective-permute-start | bytes 196616 | tf_op jit(solution)/shard_map/ppermute | solution.py:334
  17.8 0.4 collective-permute-start.6
  18.3 2.6 %collective-permute-start.12 = (f32[3,128,128]{2,1,0:T(8,128)S(1)}, f32[3,128,128]{2,1,0:T(8,128)S(1)}, u32[]{:S(2)}, u32[]{:S(2)}) collective-permute-start(f32[3,128,128]{2,1,0:T(8,128)S(1)} %slice_bitcast_fusion.1), channel_id=1, source_target_pairs={{0,3},{1,2},{2,1},{3,0},{4,7},{5,6},{6,5},{7,4},{8,11},{9,10},{10,... | collective-permute-start | bytes 589832 | tf_op jit(solution)/shard_map/ppermute | solution.py:339
  20.9 1.9 %collective-permute-start.10 = (f32[3,128,128]{2,1,0:T(8,128)S(1)}, f32[3,128,128]{2,1,0:T(8,128)S(1)}, u32[]{:S(2)}, u32[]{:S(2)}) collective-permute-start(f32[3,128,128]{2,1,0:T(8,128)S(1)} %slice_bitcast_fusion.1), channel_id=1, source_target_pairs={{0,1},{1,0},{2,3},{3,2},{4,5},{5,4},{6,7},{7,6},{8,9},{9,8},{10,11... | collective-permute-start | bytes 589832 | tf_op jit(solution)/shard_map/ppermute | solution.py:339
  22.8 1.6 %collective-permute-start.8 = (f32[5,128,128]{2,1,0:T(8,128)S(1)}, f32[5,128,128]{2,1,0:T(8,128)S(1)}, u32[]{:S(2)}, u32[]{:S(2)}) collective-permute-start(f32[5,128,128]{2,1,0:T(8,128)S(1)} %broadcast_select_fusion), channel_id=1, source_target_pairs={{0,8},{4,12},{8,0},{12,4},{16,24},{20,28},{24,16},{28,20},{1,9},{5... | collective-permute-start | bytes 983048 | tf_op jit(solution)/shard_map/ppermute | solution.py:334
  24.4 9.8 %shard_map.28 = (f32[512,384]{1,0:T(8,128)S(1)}, f32[384,384]{1,0:T(8,128)S(1)}, f32[1,1,128,128]{3,2,1,0:T(8,128)S(1)}) custom-call(s32[56]{0:T(128)S(1)} %concatenate.10.refs_0_.marks_ref, f32[11,128,128]{2,1,0:T(8,128)S(1)} %constant_dynamic-update-slice_fusion.refs_1_), custom_call_target="tpu_custom_call" | custom-call | flops 24000000000 | bytes 1048576 | tf_op jit(solution)/shard_map/pallas_call | solution.py:200
  34.3 0.1 collective-permute-start.9
  34.3 3.0 %shard_map.29 = (f32[512,128]{1,0:T(8,128)S(1)}, f32[128,512]{1,0:T(8,128)S(1)}) custom-call(f32[1,1,128,128]{3,2,1,0:T(8,128)S(1)} %get-tuple-element.24.refs_0_, f32[512,384]{1,0:T(8,128)S(1)} %get-tuple-element.25.refs_1_.refs_0_, f32[384,384]{1,0:T(8,128)S(1)} %get-tuple-element.26.refs_2_), custom_call_target="tpu_custom_call" | custom-call | flops 8000000000 | bytes 1048576 | tf_op jit(solution)/shard_map/pallas_call | solution.py:200
  37.3 1.1 %collective-permute-done.11 = f32[3,128,128]{2,1,0:T(8,128)S(1)} collective-permute-done((f32[3,128,128]{2,1,0:T(8,128)S(1)}, f32[3,128,128]{2,1,0:T(8,128)S(1)}, u32[]{:S(2)}, u32[]{:S(2)}) %collective-permute-start.11) | collective-permute-done | bytes 196640 | tf_op jit(solution)/shard_map/ppermute | solution.py:339
  38.4 0.1 pad_maximum_fusion.xr_ref
  38.5 4.0 %shard_map.30 = bf16[3,6,128,128]{3,2,1,0:T(8,128)(2,1)} custom-call(s32[56]{0:T(128)S(1)} %concatenate.10.refs_0_.marks_ref, f32[3,6,128,128]{3,2,1,0:T(8,128)S(1)} %bitcast.43, f32[4,3,128,128]{3,2,1,0:T(8,128)S(1)} %pad_maximum_fusion.xr_ref, f32[2,5,128,128]{3,2,1,0:T(8,128)S(1)} %pad_maximum_fusion.1.xc_ref, ...), custom_call_target="tpu_custom_call" | custom-call | flops 4000000000 | bytes 4194304 | tf_op jit(solution)/shard_map/pallas_call | solution.py:301
  (26 shorter events, 0.2 us)
Async XLA Ops:
  0.0 6.6 %copy-start = (f32[3,1,6,1,128,128]{5,4,3,2,1,0:T(8,128)S(1)}, f32[3,1,6,1,128,128]{5,4,3,2,1,0:T(8,128)}, u32[]{:S(2)}) copy-start(f32[3,1,6,1,128,128]{5,4,3,2,1,0:T(8,128)} %param.2) | copy-start | bytes 3538948
  0.9 5.7 %collective-permute-start = (f32[128,128]{1,0:T(8,128)S(1)}, f32[128,128]{1,0:T(8,128)S(1)}, u32[]{:S(2)}, u32[]{:S(2)}) collective-permute-start(f32[128,128]{1,0:T(8,128)S(1)} %slice_bitcast_fusion.2), channel_id=1, source_target_pairs={{0,16},{4,20},{8,24},{12,28},{16,0},{20,4},{24,8},{28,12},{1,17},{... | collective-permute-start | bytes 196616 | tf_op jit(solution)/shard_map/ppermute | solution.py:327
  4.9 13.3 %collective-permute-start.7 = (f32[5,128,128]{2,1,0:T(8,128)S(1)}, f32[5,128,128]{2,1,0:T(8,128)S(1)}, u32[]{:S(2)}, u32[]{:S(2)}) collective-permute-start(f32[5,128,128]{2,1,0:T(8,128)S(1)} %slice_bitcast_fusion), channel_id=1, source_target_pairs={{0,16},{4,20},{8,24},{12,28},{16,0},{20,4},{24,8},{28,12},{1,17},{... | collective-permute-start | bytes 983048 | tf_op jit(solution)/shard_map/ppermute | solution.py:327
  6.7 7.2 %collective-permute-start.3 = (f32[128,128]{1,0:T(8,128)S(1)}, f32[128,128]{1,0:T(8,128)S(1)}, u32[]{:S(2)}, u32[]{:S(2)}) collective-permute-start(f32[128,128]{1,0:T(8,128)S(1)} %get-tuple-element.40), channel_id=1, source_target_pairs={{0,3},{1,2},{2,1},{3,0},{4,7},{5,6},{6,5},{7,4},{8,11},{9,10},{10,... | collective-permute-start | bytes 196616 | tf_op jit(solution)/shard_map/ppermute | solution.py:339
  10.8 5.2 %collective-permute-start.2 = (f32[128,128]{1,0:T(8,128)S(1)}, f32[128,128]{1,0:T(8,128)S(1)}, u32[]{:S(2)}, u32[]{:S(2)}) collective-permute-start(f32[128,128]{1,0:T(8,128)S(1)} %get-tuple-element.40), channel_id=1, source_target_pairs={{0,2},{1,3},{2,0},{3,1},{4,6},{5,7},{6,4},{7,5},{8,10},{9,11},{10,... | collective-permute-start | bytes 196616 | tf_op jit(solution)/shard_map/ppermute | solution.py:339
  10.8 5.2 %collective-permute-start.1 = (f32[128,128]{1,0:T(8,128)S(1)}, f32[128,128]{1,0:T(8,128)S(1)}, u32[]{:S(2)}, u32[]{:S(2)}) collective-permute-start(f32[128,128]{1,0:T(8,128)S(1)} %get-tuple-element.40), channel_id=1, source_target_pairs={{0,1},{1,0},{2,3},{3,2},{4,5},{5,4},{6,7},{7,6},{8,9},{9,8},{10,11... | collective-permute-start | bytes 196616 | tf_op jit(solution)/shard_map/ppermute | solution.py:339
  16.1 2.2 %collective-permute-start.4 = (f32[4,128,128]{2,1,0:T(8,128)S(1)}, f32[4,128,128]{2,1,0:T(8,128)S(1)}, u32[]{:S(2)}, u32[]{:S(2)}) collective-permute-start(f32[4,128,128]{2,1,0:T(8,128)S(1)} %pad_maximum_fusion.2), channel_id=1, source_target_pairs={{0,4},{4,0},{8,12},{12,8},{16,20},{20,16},{24,28},{28,24},{1,5},{5... | collective-permute-start | bytes 786440 | tf_op jit(solution)/shard_map/ppermute | solution.py:334
  16.2 6.6 %collective-permute-start.5 = (f32[1,128,128]{2,1,0:T(8,128)S(1)}, f32[1,128,128]{2,1,0:T(8,128)S(1)}, u32[]{:S(2)}, u32[]{:S(2)}) collective-permute-start(f32[1,128,128]{2,1,0:T(8,128)S(1)} %get-tuple-element.42), channel_id=1, source_target_pairs={{0,8},{4,12},{8,0},{12,4},{16,24},{20,28},{24,16},{28,20},{1,9},{5... | collective-permute-start | bytes 196616 | tf_op jit(solution)/shard_map/ppermute | solution.py:334
  17.8 6.6 %collective-permute-start.6 = (f32[2,128,128]{2,1,0:T(8,128)S(1)}, f32[2,128,128]{2,1,0:T(8,128)S(1)}, u32[]{:S(2)}, u32[]{:S(2)}) collective-permute-start(f32[2,128,128]{2,1,0:T(8,128)S(1)} %pad_maximum_fusion.3), channel_id=1, source_target_pairs={{0,12},{4,8},{8,4},{12,0},{16,28},{20,24},{24,20},{28,16},{1,13},{... | collective-permute-start | bytes 393224 | tf_op jit(solution)/shard_map/ppermute | solution.py:334
  18.3 19.0 %collective-permute-start.12 = (f32[3,128,128]{2,1,0:T(8,128)S(1)}, f32[3,128,128]{2,1,0:T(8,128)S(1)}, u32[]{:S(2)}, u32[]{:S(2)}) collective-permute-start(f32[3,128,128]{2,1,0:T(8,128)S(1)} %slice_bitcast_fusion.1), channel_id=1, source_target_pairs={{0,3},{1,2},{2,1},{3,0},{4,7},{5,6},{6,5},{7,4},{8,11},{9,10},{10,... | collective-permute-start | bytes 589832 | tf_op jit(solution)/shard_map/ppermute | solution.py:339
  20.9 17.6 %collective-permute-start.11 = (f32[3,128,128]{2,1,0:T(8,128)S(1)}, f32[3,128,128]{2,1,0:T(8,128)S(1)}, u32[]{:S(2)}, u32[]{:S(2)}) collective-permute-start(f32[3,128,128]{2,1,0:T(8,128)S(1)} %slice_bitcast_fusion.1), channel_id=1, source_target_pairs={{0,2},{1,3},{2,0},{3,1},{4,6},{5,7},{6,4},{7,5},{8,10},{9,11},{10,... | collective-permute-start | bytes 589832 | tf_op jit(solution)/shard_map/ppermute | solution.py:339
  20.9 17.6 %collective-permute-start.10 = (f32[3,128,128]{2,1,0:T(8,128)S(1)}, f32[3,128,128]{2,1,0:T(8,128)S(1)}, u32[]{:S(2)}, u32[]{:S(2)}) collective-permute-start(f32[3,128,128]{2,1,0:T(8,128)S(1)} %slice_bitcast_fusion.1), channel_id=1, source_target_pairs={{0,1},{1,0},{2,3},{3,2},{4,5},{5,4},{6,7},{7,6},{8,9},{9,8},{10,11... | collective-permute-start | bytes 589832 | tf_op jit(solution)/shard_map/ppermute | solution.py:339
  22.8 11.4 %collective-permute-start.8 = (f32[5,128,128]{2,1,0:T(8,128)S(1)}, f32[5,128,128]{2,1,0:T(8,128)S(1)}, u32[]{:S(2)}, u32[]{:S(2)}) collective-permute-start(f32[5,128,128]{2,1,0:T(8,128)S(1)} %broadcast_select_fusion), channel_id=1, source_target_pairs={{0,8},{4,12},{8,0},{12,4},{16,24},{20,28},{24,16},{28,20},{1,9},{5... | collective-permute-start | bytes 983048 | tf_op jit(solution)/shard_map/ppermute | solution.py:334
  34.3 4.2 %collective-permute-start.9 = (f32[2,5,128,128]{3,2,1,0:T(8,128)S(1)}, f32[2,5,128,128]{3,2,1,0:T(8,128)S(1)}, u32[]{:S(2)}, u32[]{:S(2)}) collective-permute-start(f32[2,5,128,128]{3,2,1,0:T(8,128)S(1)} %pad_maximum_fusion.1.xc_ref), channel_id=1, source_target_pairs={{0,4},{4,0},{8,12},{12,8},{16,20},{20,16},{24,28},{28,24},{1,5},{5... | collective-permute-start | bytes 1966088 | tf_op jit(solution)/shard_map/ppermute | solution.py:334
